TPU v7x, 32 devices: a whole 2x2x4 slice. The times are simulated.
32 devices in a mesh: band: 2 (over core), dom: 16 (over z, y, x).
Axes of the slice: x: 2, y: 2, z: 4, core: 2. Of those that a mesh axis runs over, the one named last changes fastest.
Arguments:
- orbitals: float32 [24, 32, 128, 128], P('band', 'dom'), may hold values from -6 to 6
- occupations: float32 [24], replicated, may hold values from 0.25 to 2
Outputs:
- exchange_terms: float32 [24, 32, 128, 128], P('band', 'dom')
All inputs are finite; a program needn't handle non-finite values.
Results may differ from a plain program's by a relative error of at most 0.0001.
Values sent between devices are 32-bit elements; how exact they have to be, the bound alone decides.
No kernel may reach another device: no remote copies, remote signals or barrier semaphores. Data moves between devices by JAX's collectives and lax.ppermute only.
A program may use at most 128 MiB of HBM per device.

v0:
```python
import jax
import jax.numpy as jnp
from jax import lax
from jax.sharding import PartitionSpec as P

BLOCK = 2
STEPS = 2
SWEEPS = 2


def from_root(block, axis, source):
    block = jnp.where(lax.axis_index(axis) == source, block, jnp.zeros_like(block))
    return lax.psum(block, axis)


def extended(cells, sides, width):
    for axis, dim in sides:
        count = lax.axis_size(axis)
        ends = count - 1
        head = lax.slice_in_dim(cells, 0, width, axis=dim)
        tail = lax.slice_in_dim(cells, cells.shape[dim] - width, cells.shape[dim], axis=dim)
        cells = jnp.concatenate(
            [
                lax.ppermute(tail, axis, [(i, (i + 1) % count) for i in range(ends)]),
                cells,
                lax.ppermute(head, axis, [((i + 1) % count, i) for i in range(ends)]),
            ],
            axis=dim,
        )
    return cells


def lateral(field):
    padded = jnp.pad(field, ((0, 0), (0, 0), (1, 1), (1, 1)))
    total = padded[:, :, 2:, 1:-1] + padded[:, :, :-2, 1:-1]
    return total + padded[:, :, 1:-1, 2:] + padded[:, :, 1:-1, :-2]


def per_device(orbitals, occupations):
    orb_count, planes, cells_y, cells_z = orbitals.shape
    groups = lax.axis_size("band")
    exchange_terms = jnp.zeros(orbitals.shape, jnp.float32)
    for step_index in range(STEPS):
        owner = step_index * (groups // STEPS)
        first = owner * orb_count + step_index * BLOCK
        mine = orbitals[step_index * BLOCK : (step_index + 1) * BLOCK]
        owner_block = from_root(mine, "band", owner)
        weights = occupations[first : first + BLOCK]
        density = (owner_block[:, None] * orbitals[None]).reshape(
            BLOCK * orb_count, planes, cells_y, cells_z
        )
        potential = density / 6.0
        for sweep_index in range(SWEEPS):
            padded = extended(potential, (("dom", 1),), 1)
            along_x = padded[:, 2:] + padded[:, :-2]
            potential = (density + along_x + lateral(potential)) / 6.0
        potential = potential.reshape(BLOCK, orb_count, planes, cells_y, cells_z)
        step_sum = jnp.zeros(orbitals.shape, jnp.float32)
        for block_index in range(BLOCK):
            step_sum = (
                step_sum
                - weights[block_index] * potential[block_index] * owner_block[block_index][None]
            )
        exchange_terms = exchange_terms + step_sum
    return exchange_terms


def solution(mesh):
    in_specs = (P("band", "dom", None, None), P())
    out_specs = P("band", "dom", None, None)
    return jax.shard_map(
        per_device, mesh=mesh, in_specs=in_specs, out_specs=out_specs, check_vma=False
    )
```

profile of v0, /device:TPU:0, one launch (start us, length us, event | category | flops | bytes accessed | tf_op | source)
XLA Modules:
  0.0 324.2 jit_solution(4957920227807967499)
XLA Ops:
  6.5 0.0 all-reduce.7.cloned.1.call-start
  6.5 1.8 slice_select_fusion.1
  8.4 0.0 all-reduce.7.cloned.1.call-update
  8.4 22.8 %all-reduce.7.cloned.1.call-done = (f32[2,2,128,128]{3,2,1,0:T(8,128)}, f32[2,2,128,128]{3,2,1,0:T(8,128)}) async-done(((f32[2,2,128,128]{3,2,1,0:T(8,128)}, f32[2,2,128,128]{3,2,1,0:T(8,128)}), (f32[2,2,128,128]{3,2,1,0:T(8,128)}, f32[2,2,128,128]{3,2,1,0:T(8,128)})) %all-reduce.7.cloned.1.call-update) | async-done | bytes 524304 | tf_op jit(solution)/shard_map/psum | solution.py:13
  31.3 2.3 broadcast_multiply_fusion.1
  33.5 1.2 bitcast_multiply_fusion
  34.8 0.3 fusion.38
  35.1 1.3 collective-permute-start
  36.4 4.6 %collective-permute-start.1 = (f32[24,1,128,128]{3,2,1,0:T(8,128)S(1)}, f32[24,1,128,128]{3,2,1,0:T(8,128)S(1)}, u32[]{:S(2)}, u32[]{:S(2)}) collective-permute-start(f32[24,1,128,128]{3,2,1,0:T(8,128)S(1)} %get-tuple-element.10), channel_id=1, source_target_pairs={{0,1},{1,2},{2,3},{3,4},{4,5},{5,6},{6,7},{7,8},{8,9},{9,10},{10,1... | collective-permute-start | bytes 4718600 | tf_op jit(solution)/shard_map/ppermute | solution.py:24
  41.1 0.3 fusion.40
  41.4 1.3 collective-permute-start.4
  42.7 5.2 %collective-permute-start.5 = (f32[24,1,128,128]{3,2,1,0:T(8,128)S(1)}, f32[24,1,128,128]{3,2,1,0:T(8,128)S(1)}, u32[]{:S(2)}, u32[]{:S(2)}) collective-permute-start(f32[24,1,128,128]{3,2,1,0:T(8,128)S(1)} %get-tuple-element.14), channel_id=1, source_target_pairs={{0,1},{1,2},{2,3},{3,4},{4,5},{5,6},{6,7},{7,8},{8,9},{9,10},{10,1... | collective-permute-start | bytes 4718600 | tf_op jit(solution)/shard_map/ppermute | solution.py:24
  47.9 26.3 %collective-permute-done = f32[24,1,128,128]{3,2,1,0:T(8,128)S(1)} collective-permute-done((f32[24,1,128,128]{3,2,1,0:T(8,128)S(1)}, f32[24,1,128,128]{3,2,1,0:T(8,128)S(1)}, u32[]{:S(2)}, u32[]{:S(2)}) %collective-permute-start) | collective-permute-done | bytes 1572896 | tf_op jit(solution)/shard_map/ppermute | solution.py:26
  74.3 67.9 %collective-permute-done.1 = f32[24,1,128,128]{3,2,1,0:T(8,128)S(1)} collective-permute-done((f32[24,1,128,128]{3,2,1,0:T(8,128)S(1)}, f32[24,1,128,128]{3,2,1,0:T(8,128)S(1)}, u32[]{:S(2)}, u32[]{:S(2)}) %collective-permute-start.1) | collective-permute-done | bytes 1572896 | tf_op jit(solution)/shard_map/ppermute | solution.py:24
  142.2 2.2 fusion.4
  144.4 0.3 fusion.37
  144.8 1.3 collective-permute-start.2
  146.1 5.1 %collective-permute-start.3 = (f32[24,1,128,128]{3,2,1,0:T(8,128)S(1)}, f32[24,1,128,128]{3,2,1,0:T(8,128)S(1)}, u32[]{:S(2)}, u32[]{:S(2)}) collective-permute-start(f32[24,1,128,128]{3,2,1,0:T(8,128)S(1)} %get-tuple-element.8), channel_id=1, source_target_pairs={{0,1},{1,2},{2,3},{3,4},{4,5},{5,6},{6,7},{7,8},{8,9},{9,10},{10,1... | collective-permute-start | bytes 4718600 | tf_op jit(solution)/shard_map/ppermute | solution.py:24
  151.2 0.0 collective-permute-done.4
  151.2 58.4 %collective-permute-done.5 = f32[24,1,128,128]{3,2,1,0:T(8,128)S(1)} collective-permute-done((f32[24,1,128,128]{3,2,1,0:T(8,128)S(1)}, f32[24,1,128,128]{3,2,1,0:T(8,128)S(1)}, u32[]{:S(2)}, u32[]{:S(2)}) %collective-permute-start.5) | collective-permute-done | bytes 1572896 | tf_op jit(solution)/shard_map/ppermute | solution.py:24
  209.6 2.2 fusion.14
  211.8 0.0 copy-start.2
  211.8 0.0 copy-start
  211.8 0.0 copy-start.1
  211.9 0.3 fusion.39
  212.2 1.3 collective-permute-start.6
  213.5 5.1 %collective-permute-start.7 = (f32[24,1,128,128]{3,2,1,0:T(8,128)S(1)}, f32[24,1,128,128]{3,2,1,0:T(8,128)S(1)}, u32[]{:S(2)}, u32[]{:S(2)}) collective-permute-start(f32[24,1,128,128]{3,2,1,0:T(8,128)S(1)} %get-tuple-element.12), channel_id=1, source_target_pairs={{0,1},{1,2},{2,3},{3,4},{4,5},{5,6},{6,7},{7,8},{8,9},{9,10},{10,1... | collective-permute-start | bytes 4718600 | tf_op jit(solution)/shard_map/ppermute | solution.py:24
  218.6 0.0 copy-done.2
  218.6 0.7 fusion.41
  219.3 0.0 copy-done
  219.3 0.0 copy-done.1
  219.3 0.0 collective-permute-done.2
  219.4 57.7 %collective-permute-done.3 = f32[24,1,128,128]{3,2,1,0:T(8,128)S(1)} collective-permute-done((f32[24,1,128,128]{3,2,1,0:T(8,128)S(1)}, f32[24,1,128,128]{3,2,1,0:T(8,128)S(1)}, u32[]{:S(2)}, u32[]{:S(2)}) %collective-permute-start.3) | collective-permute-done | bytes 1572896 | tf_op jit(solution)/shard_map/ppermute | solution.py:24
  277.0 2.2 fusion.9
  279.2 0.0 collective-permute-done.6
  279.2 31.4 %collective-permute-done.7 = f32[24,1,128,128]{3,2,1,0:T(8,128)S(1)} collective-permute-done((f32[24,1,128,128]{3,2,1,0:T(8,128)S(1)}, f32[24,1,128,128]{3,2,1,0:T(8,128)S(1)}, u32[]{:S(2)}, u32[]{:S(2)}) %collective-permute-start.7) | collective-permute-done | bytes 1572896 | tf_op jit(solution)/shard_map/ppermute | solution.py:24
  310.6 2.2 fusion.19
  312.9 4.5 %fusion.30 = f32[12,2,128,128]{3,2,1,0:T(8,128)} fusion(f32[24,2,128,128]{3,2,1,0:T(8,128)S(1)} %fusion.19, f32[24,2,128,128]{3,2,1,0:T(8,128)S(1)} %fusion.9, f32[2,128,128]{2,1,0:T(8,128)S(1)} %get-tuple-element.22, f32[]{:T(128)} %bitcast.8, f32[2,128,128]{2,1,0:T(8,128)S(1)} %get-tuple-element.21, f32[]{:T(128)} %bitcast.5, ...), kind=kLoop, calls=%fused_computation.57 | loop fusion | flops 5111808 | bytes 8388624 | tf_op jit(solution)/shard_map/add | solution.py:64
  (1 shorter events, 0.0 us)
Async XLA Ops:
  6.5 24.7 %all-reduce.7.cloned.1.call-start = ((), (), s32[]{:S(2)}) async-start(), calls=%async_computation | async-start | bytes 1048576 | tf_op jit(solution)/shard_map/psum | solution.py:13
  35.1 39.1 %collective-permute-start = (f32[24,1,128,128]{3,2,1,0:T(8,128)S(1)}, f32[24,1,128,128]{3,2,1,0:T(8,128)S(1)}, u32[]{:S(2)}, u32[]{:S(2)}) collective-permute-start(f32[24,1,128,128]{3,2,1,0:T(8,128)S(1)} %get-tuple-element.9), channel_id=1, source_target_pairs={{1,0},{2,1},{3,2},{4,3},{5,4},{6,5},{7,6},{8,7},{9,8},{10,9},{11,1... | collective-permute-start | bytes 4718600 | tf_op jit(solution)/shard_map/ppermute | solution.py:26
  36.4 105.7 %collective-permute-start.1 = (f32[24,1,128,128]{3,2,1,0:T(8,128)S(1)}, f32[24,1,128,128]{3,2,1,0:T(8,128)S(1)}, u32[]{:S(2)}, u32[]{:S(2)}) collective-permute-start(f32[24,1,128,128]{3,2,1,0:T(8,128)S(1)} %get-tuple-element.10), channel_id=1, source_target_pairs={{0,1},{1,2},{2,3},{3,4},{4,5},{5,6},{6,7},{7,8},{8,9},{9,10},{10,1... | collective-permute-start | bytes 4718600 | tf_op jit(solution)/shard_map/ppermute | solution.py:24
  41.4 109.7 %collective-permute-start.4 = (f32[24,1,128,128]{3,2,1,0:T(8,128)S(1)}, f32[24,1,128,128]{3,2,1,0:T(8,128)S(1)}, u32[]{:S(2)}, u32[]{:S(2)}) collective-permute-start(f32[24,1,128,128]{3,2,1,0:T(8,128)S(1)} %get-tuple-element.13), channel_id=1, source_target_pairs={{1,0},{2,1},{3,2},{4,3},{5,4},{6,5},{7,6},{8,7},{9,8},{10,9},{11,1... | collective-permute-start | bytes 4718600 | tf_op jit(solution)/shard_map/ppermute | solution.py:26
  42.7 166.9 %collective-permute-start.5 = (f32[24,1,128,128]{3,2,1,0:T(8,128)S(1)}, f32[24,1,128,128]{3,2,1,0:T(8,128)S(1)}, u32[]{:S(2)}, u32[]{:S(2)}) collective-permute-start(f32[24,1,128,128]{3,2,1,0:T(8,128)S(1)} %get-tuple-element.14), channel_id=1, source_target_pairs={{0,1},{1,2},{2,3},{3,4},{4,5},{5,6},{6,7},{7,8},{8,9},{9,10},{10,1... | collective-permute-start | bytes 4718600 | tf_op jit(solution)/shard_map/ppermute | solution.py:24
  144.8 74.6 %collective-permute-start.2 = (f32[24,1,128,128]{3,2,1,0:T(8,128)S(1)}, f32[24,1,128,128]{3,2,1,0:T(8,128)S(1)}, u32[]{:S(2)}, u32[]{:S(2)}) collective-permute-start(f32[24,1,128,128]{3,2,1,0:T(8,128)S(1)} %get-tuple-element.7), channel_id=1, source_target_pairs={{1,0},{2,1},{3,2},{4,3},{5,4},{6,5},{7,6},{8,7},{9,8},{10,9},{11,1... | collective-permute-start | bytes 4718600 | tf_op jit(solution)/shard_map/ppermute | solution.py:26
  146.1 130.9 %collective-permute-start.3 = (f32[24,1,128,128]{3,2,1,0:T(8,128)S(1)}, f32[24,1,128,128]{3,2,1,0:T(8,128)S(1)}, u32[]{:S(2)}, u32[]{:S(2)}) collective-permute-start(f32[24,1,128,128]{3,2,1,0:T(8,128)S(1)} %get-tuple-element.8), channel_id=1, source_target_pairs={{0,1},{1,2},{2,3},{3,4},{4,5},{5,6},{6,7},{7,8},{8,9},{9,10},{10,1... | collective-permute-start | bytes 4718600 | tf_op jit(solution)/shard_map/ppermute | solution.py:24
  211.8 6.8 %copy-start.2 = (f32[24]{0:T(128)S(1)}, f32[24]{0:T(128)}, u32[]{:S(2)}) copy-start(f32[24]{0:T(128)} %param.3) | copy-start | bytes 292
  211.8 7.5 %copy-start = (f32[2,2,128,128]{3,2,1,0:T(8,128)S(1)}, f32[2,2,128,128]{3,2,1,0:T(8,128)}, u32[]{:S(2)}) copy-start(f32[2,2,128,128]{3,2,1,0:T(8,128)} %get-tuple-element.5) | copy-start | bytes 786436
  211.8 7.5 %copy-start.1 = (f32[2,2,128,128]{3,2,1,0:T(8,128)S(1)}, f32[2,2,128,128]{3,2,1,0:T(8,128)}, u32[]{:S(2)}) copy-start(f32[2,2,128,128]{3,2,1,0:T(8,128)} %get-tuple-element.6) | copy-start | bytes 786436
  212.2 67.0 %collective-permute-start.6 = (f32[24,1,128,128]{3,2,1,0:T(8,128)S(1)}, f32[24,1,128,128]{3,2,1,0:T(8,128)S(1)}, u32[]{:S(2)}, u32[]{:S(2)}) collective-permute-start(f32[24,1,128,128]{3,2,1,0:T(8,128)S(1)} %get-tuple-element.11), channel_id=1, source_target_pairs={{1,0},{2,1},{3,2},{4,3},{5,4},{6,5},{7,6},{8,7},{9,8},{10,9},{11,1... | collective-permute-start | bytes 4718600 | tf_op jit(solution)/shard_map/ppermute | solution.py:26
  213.5 97.1 %collective-permute-start.7 = (f32[24,1,128,128]{3,2,1,0:T(8,128)S(1)}, f32[24,1,128,128]{3,2,1,0:T(8,128)S(1)}, u32[]{:S(2)}, u32[]{:S(2)}) collective-permute-start(f32[24,1,128,128]{3,2,1,0:T(8,128)S(1)} %get-tuple-element.12), channel_id=1, source_target_pairs={{0,1},{1,2},{2,3},{3,4},{4,5},{5,6},{6,7},{7,8},{8,9},{9,10},{10,1... | collective-permute-start | bytes 4718600 | tf_op jit(solution)/shard_map/ppermute | solution.py:24
Sparse Core Ops, SparseCore 0:
  9.7 21.4 all-reduce.6
where the time goes:
time: 325 us; the launch traced here: 324 us
  waiting for transfers between devices  265 us (82%)
  starting transfers between devices  25.2 us (8%)
  other arithmetic  18.7 us (6%)
  between operations  13.6 us (4%)
    ppermute x4, waiting for transfers between devices, extended(): lax.ppermute(tail, axis, [(i, (i + 1) % count) for i in range(ends)])  215 us
    ppermute x4, waiting for transfers between devices, extended(): lax.ppermute(head, axis, [((i + 1) % count, i) for i in range(ends)])  26.3 us
    psum x1, waiting for transfers between devices, from_root(): return lax.psum(block, axis)  22.8 us
    ppermute x4, starting transfers between devices, extended(): lax.ppermute(tail, axis, [(i, (i + 1) % count) for i in range(ends)])  20 us
    div x4, other arithmetic, per_device(): potential = (density + along_x + lateral(potential)) / 6.0  8.87 us
  transfers between devices with their start and end apart: 9, of which 6 were waited for; matrix products, arithmetic and copies ran while one was open for 3% of the time, Pallas kernels for 0%

commit v1 on v0

v1 whole, which is shorter than its diff:
```python
import functools

import jax
import jax.numpy as jnp
from jax import lax
from jax.experimental import pallas as pl
from jax.experimental.pallas import tpu as pltpu
from jax.sharding import PartitionSpec as P

BLOCK = 2
STEPS = 2
CHUNKS = (3, 3, 3, 3)

ONE = 1.0 / 36.0
TWO = 1.0 / 216.0
CROSS = 2.0 / 216.0

OWN = [(0, 0), (1, 0), (-1, 0), (2, 0), (-2, 0), (0, 1), (1, 1), (-1, 1), (0, -1), (1, -1), (-1, -1), (0, 2), (0, -2)]
BESIDE = [(0, 0), (1, 0), (-1, 0), (0, 1), (0, -1)]


def shifted(field, dy, dz):
    rows, columns = field.shape
    if dy:
        field = pltpu.roll(field, (-dy) % rows, 0)
    if dz:
        field = pltpu.roll(field, (-dz) % columns, 1)
    return field


def inside(shape, dy, dz):
    y = lax.broadcasted_iota(jnp.int32, shape, 0) + dy
    z = lax.broadcasted_iota(jnp.int32, shape, 1) - dz
    return (y >= 0) & (y < shape[0]) & (z >= 0) & (z < shape[1])


def pair_weight(weights, here, there, dy, dz, scale):
    total = None
    for w, h, t in zip(weights, here, there):
        term = (w * shifted(h, 0, -dz)) * shifted(t, dy, 0)
        total = term if total is None else total + term
    total = total * (-scale)
    if dy or dz:
        total = jnp.where(inside(total.shape, dy, dz), total, 0.0)
    return total


def scale_of(dy, dz, dx):
    length = abs(dx) + abs(dy) + abs(dz)
    if length == 1:
        return ONE
    return TWO if max(abs(dx), abs(dy), abs(dz)) == 2 else CROSS


def block_weights(occ_ref, orb_count, swapped):
    groups = lax.axis_size("band")
    out = []
    for step in range(STEPS):
        if swapped:
            s = lax.rem(lax.axis_index("band") + step, STEPS)
        else:
            s = step
        first = s * (groups // STEPS) * orb_count + s * BLOCK
        out += [occ_ref[first + i] for i in range(BLOCK)]
    return out


def local_kernel(swapped, occ_ref, orb_ref, *refs):
    block_refs, acc_ref, k_ref = refs[:STEPS], refs[STEPS], refs[STEPS + 1]
    orb_count, planes, rows, columns = orb_ref.shape
    weights = block_weights(occ_ref, orb_count, swapped)
    dom, slabs = lax.axis_index("dom"), lax.axis_size("dom")
    for p in range(planes):
        here = [r[i, p] for r in block_refs for i in range(BLOCK)]
        there = [r[i, 1 - p] for r in block_refs for i in range(BLOCK)]
        outer = jnp.where(dom == (0 if p == 0 else slabs - 1), 0.0, 1.0)
        y = lax.broadcasted_iota(jnp.int32, (rows, columns), 0)
        z = lax.broadcasted_iota(jnp.int32, (rows, columns), 1)
        edges = (y > 0).astype(jnp.float32) + (y < rows - 1).astype(jnp.float32)
        edges = edges + (z > 0).astype(jnp.float32) + (z < columns - 1).astype(jnp.float32)
        centre = 1.0 / 6.0 + (edges + (1.0 + outer)) * TWO
        for k, (dy, dz) in enumerate(OWN):
            if k == 0:
                k_ref[p, k] = pair_weight(weights, here, here, 0, 0, 1.0) * centre
            else:
                k_ref[p, k] = pair_weight(weights, here, here, dy, dz, scale_of(dy, dz, 0))
        for k, (dy, dz) in enumerate(BESIDE):
            k_ref[p, len(OWN) + k] = pair_weight(weights, here, there, dy, dz, scale_of(dy, dz, 1))

    @pl.loop(0, orb_count)
    def _(j):
        for p in range(planes):
            groups = {}
            for plane, terms, base in ((p, OWN, 0), (1 - p, BESIDE, len(OWN))):
                field = orb_ref[j, plane]
                for k, (dy, dz) in enumerate(terms):
                    term = k_ref[p, base + k] * shifted(field, dy, 0)
                    groups[dz] = groups[dz] + term if dz in groups else term
            out = groups[0]
            for dz in (1, -1, 2, -2):
                out = out + shifted(groups[dz], 0, dz)
            acc_ref[j, p] = out


def sides():
    odd = lax.rem(lax.axis_index("dom"), 2)
    return odd, 1 - odd


def halo_weight_kernel(swapped, orb_count, occ_ref, *refs):
    n = STEPS
    local, first, second, k_ref = refs[:n], refs[n : 2 * n], refs[2 * n : 3 * n], refs[3 * n]
    weights = block_weights(occ_ref, orb_count, swapped)
    for h, (slab, near) in enumerate(zip((first, second), sides())):
        far = 1 - near
        here = [r[i, far] for r in local for i in range(BLOCK)]
        behind = [r[i, near] for r in local for i in range(BLOCK)]
        there = [r[i, near] for r in slab for i in range(BLOCK)]
        beyond = [r[i, far] for r in slab for i in range(BLOCK)]
        for k, (dy, dz) in enumerate(BESIDE):
            k_ref[h, k] = pair_weight(weights, here, there, dy, dz, scale_of(dy, dz, 1))
        k_ref[h, 5] = pair_weight(weights, here, beyond, 0, 0, TWO)
        k_ref[h, 6] = pair_weight(weights, behind, there, 0, 0, TWO)


def halo_kernel(k_ref, first_ref, second_ref, acc_ref, out_ref):
    @pl.loop(0, acc_ref.shape[0])
    def _(j):
        out_ref[j] = acc_ref[j]
        for h, (slab, near) in enumerate(zip((first_ref, second_ref), sides())):
            far = 1 - near
            there = slab[j, near]
            groups = {}
            for k, (dy, dz) in enumerate(BESIDE):
                term = k_ref[h, k] * shifted(there, dy, 0)
                groups[dz] = groups[dz] + term if dz in groups else term
            total = groups[0] + k_ref[h, 5] * slab[j, far]
            total = total + shifted(groups[1], 0, 1) + shifted(groups[-1], 0, -1)
            out_ref[j, far] += total
            out_ref[j, near] += k_ref[h, 6] * there


VMEM = pl.BlockSpec(memory_space=pltpu.VMEM)
SMEM = pl.BlockSpec(memory_space=pltpu.SMEM)
PARAMS = pltpu.CompilerParams(vmem_limit_bytes=32 * 1024 * 1024)


def hops(slabs):
    swap = [(i, i ^ 1) for i in range(slabs)]
    onward = [(i, i + 2 if i % 2 == 0 else i - 2) for i in range(slabs)]
    onward = [(a, b) for a, b in onward if 0 <= b < slabs]
    return swap, onward


def everywhere(field, groups):
    band = lax.axis_index("band")
    if groups == STEPS:
        own = lax.dynamic_slice_in_dim(field, band * BLOCK, BLOCK, 0)
        return [own] + [
            lax.ppermute(own, "band", [(i, (i - step) % STEPS) for i in range(STEPS)]) for step in range(1, STEPS)
        ]
    out = []
    for step in range(STEPS):
        mine = field[step * BLOCK : (step + 1) * BLOCK]
        mine = jnp.where(band == step * (groups // STEPS), mine, jnp.zeros_like(mine))
        out.append(lax.psum(mine, "band"))
    return out


def per_device(orbitals, occupations):
    orb_count, planes, rows, columns = orbitals.shape
    groups, slabs = lax.axis_size("band"), lax.axis_size("dom")
    assert planes == 2 and slabs % 2 == 0 and sum(CHUNKS) == orb_count
    swapped = groups == STEPS
    swap, onward = hops(slabs)

    first, second, start = [], [], 0
    for size in CHUNKS:
        first.append(lax.ppermute(orbitals[start : start + size], "dom", swap))
        start += size
    for slab in first:
        second.append(lax.ppermute(slab, "dom", onward))

    local = everywhere(orbitals[: STEPS * BLOCK], groups)
    acc = pl.pallas_call(
        functools.partial(local_kernel, swapped),
        out_shape=jax.ShapeDtypeStruct(orbitals.shape, jnp.float32),
        in_specs=[SMEM] + [VMEM] * (1 + STEPS),
        out_specs=VMEM,
        scratch_shapes=[pltpu.VMEM((planes, len(OWN) + len(BESIDE), rows, columns), jnp.float32)],
        compiler_params=PARAMS,
        cost_estimate=pl.CostEstimate(flops=50_000_000, bytes_accessed=4_000_000, transcendentals=0),
        name="local",
    )(occupations, orbitals, *local)

    count = 0
    while sum(CHUNKS[:count]) < STEPS * BLOCK:
        count += 1
    near = [everywhere(jnp.concatenate(part[:count])[: STEPS * BLOCK], groups) for part in (first, second)]
    weights = pl.pallas_call(
        functools.partial(halo_weight_kernel, swapped, orb_count),
        out_shape=jax.ShapeDtypeStruct((2, 7, rows, columns), jnp.float32),
        in_specs=[SMEM] + [VMEM] * (3 * STEPS),
        out_specs=VMEM,
        compiler_params=PARAMS,
        name="halo_weights",
    )(occupations, *local, *near[0], *near[1])

    start = 0
    for slab_a, slab_b in zip(first, second):
        size = slab_a.shape[0]
        index = start // size
        spec = pl.BlockSpec((size, planes, rows, columns), lambda i, index=index: (index, 0, 0, 0))
        whole = lambda a: pl.BlockSpec(a.shape, lambda i, n=a.ndim: (0,) * n)
        acc = pl.pallas_call(
            halo_kernel,
            grid=(1,),
            out_shape=jax.ShapeDtypeStruct(orbitals.shape, jnp.float32),
            in_specs=[whole(weights), whole(slab_a), whole(slab_b), spec],
            out_specs=spec,
            input_output_aliases={3: 0},
            compiler_params=PARAMS,
            name="halo",
        )(weights, slab_a, slab_b, acc)
        start += size
    return acc


def solution(mesh):
    in_specs = (P("band", "dom", None, None), P())
    out_specs = P("band", "dom", None, None)
    return jax.shard_map(
        per_device, mesh=mesh, in_specs=in_specs, out_specs=out_specs, check_vma=False
    )
```

time: 325 us -> 61.7 us (0.19)
  waiting for transfers between devices: 265 us -> 19.5 us
  other arithmetic: 18.7 us -> 0.1 us
  Pallas kernels: 0 us -> 16.2 us
  between operations: 13.6 us -> 0.09 us
    ppermute x8 -> x11, waiting for transfers between devices: 242 us -> 19.5 us  [the longest x4 19.5 us: per_device(): first.append(lax.ppermute(orbitals[start:start + size], 'dom', swap))]
    psum x1 -> x0, waiting for transfers between devices: 22.8 us -> none  [from_root(): return lax.psum(block, axis)]
    pallas_call x0 -> x6, Pallas kernels: none -> 16.2 us  [the longest x4 9.17 us: per_device(): pl.pallas_call(halo_kernel, grid=(1,), out_shape=jax.ShapeDtypeStruct(orb...]
    div x5 -> x0, other arithmetic: 10.1 us -> none  [the longest x4 8.87 us: per_device(): potential = (density + along_x + lateral(potential)) / 6.0]
    add x1 -> x0, other arithmetic: 4.49 us -> none  [per_device(): exchange_terms = exchange_terms + step_sum]
    ppermute x8 -> x11, starting transfers between devices: 25.2 us -> 23.1 us  [the longest x4 16.5 us: per_device(): second.append(lax.ppermute(slab, 'dom', onward))]
  transfers between devices with their start and end apart: 9 -> 11, of which waited for: 6 -> 4; matrix products, arithmetic and copies ran while one was open for 3% -> 0% of each run, Pallas kernels for 0% -> 23%
where the time goes in v1:
time: 61.7 us; the launch traced here: 61.4 us
  starting transfers between devices  23.1 us (37%)
  waiting for transfers between devices  19.5 us (32%)
  Pallas kernels  16.2 us (26%)
  local copies, waits for them, and re-layouts  2.44 us (4%)
    ppermute x4, waiting for transfers between devices, per_device(): first.append(lax.ppermute(orbitals[start:start + size], 'dom', swap))  19.5 us
    ppermute x4, starting transfers between devices, per_device(): second.append(lax.ppermute(slab, 'dom', onward))  16.5 us
    pallas_call x4, Pallas kernels, per_device(): pl.pallas_call(halo_kernel, grid=(1,), out_shape=jax.ShapeDtypeStruct(orb...  9.17 us
    pallas_call x1, Pallas kernels, per_device(): pl.pallas_call(functools.partial(local_kernel, swapped), out_shape=jax.Sh...  5.97 us
    ppermute x4, starting transfers between devices, per_device(): first.append(lax.ppermute(orbitals[start:start + size], 'dom', swap))  5.01 us
    slice x1, local copies, waits for them, and re-layouts, per_device(): first.append(lax.ppermute(orbitals[start:start + size], 'dom', swap))  2.41 us
    ppermute x3, starting transfers between devices, everywhere(): lax.ppermute(own, 'band', [(i, (i - step) % STEPS) for i in range(STEPS)])  1.58 us
  transfers between devices with their start and end apart: 11, of which 4 were waited for; matrix products, arithmetic and copies ran while one was open for 0% of the time, Pallas kernels for 23%

profile of v1, /device:TPU:0, one launch (start us, length us, event | category | flops | bytes accessed | tf_op | source)
XLA Modules:
  0.0 61.4 jit_solution(5920425101845105634)
XLA Ops:
  0.0 0.0 slice-start
  0.0 2.4 %fusion.2 = (f32[3,2,128,128]{3,2,1,0:T(8,128)}, f32[3,2,128,128]{3,2,1,0:T(8,128)}, f32[3,2,128,128]{3,2,1,0:T(8,128)S(1)}, f32[3,2,128,128]{3,2,1,0:T(8,128)S(1)}) fusion(f32[12,2,128,128]{3,2,1,0:T(8,128)} %orb_ref.1), kind=kLoop, calls=%fused_computation.7 | loop fusion | bytes 3145728 | tf_op jit(solution)/shard_map/slice | solution.py:179
  2.4 2.9 %collective-permute-start.1 = (f32[3,2,128,128]{3,2,1,0:T(8,128)S(1)}, f32[3,2,128,128]{3,2,1,0:T(8,128)S(1)}, u32[]{:S(2)}, u32[]{:S(2)}) collective-permute-start(f32[3,2,128,128]{3,2,1,0:T(8,128)S(1)} %get-tuple-element.8), channel_id=1, source_target_pairs={{0,1},{1,0},{2,3},{3,2},{4,5},{5,4},{6,7},{7,6},{8,9},{9,8},{10,11... | collective-permute-start | bytes 1179656 | tf_op jit(solution)/shard_map/ppermute | solution.py:179
  5.4 0.0 collective-permute-start.2
  5.4 2.0 %collective-permute-start.9 = (f32[3,2,128,128]{3,2,1,0:T(8,128)}, f32[3,2,128,128]{3,2,1,0:T(8,128)}, u32[]{:S(2)}, u32[]{:S(2)}) collective-permute-start(f32[3,2,128,128]{3,2,1,0:T(8,128)} %get-tuple-element.5), channel_id=1, source_target_pairs={{0,1},{1,0},{2,3},{3,2},{4,5},{5,4},{6,7},{7,6},{8,9},{9,8},{10,11... | collective-permute-start | bytes 1179656 | tf_op jit(solution)/shard_map/ppermute | solution.py:179
  7.4 0.0 collective-permute-start.7
  7.4 7.9 %collective-permute-done.1.first_ref = f32[3,2,128,128]{3,2,1,0:T(8,128)S(1)} collective-permute-done((f32[3,2,128,128]{3,2,1,0:T(8,128)S(1)}, f32[3,2,128,128]{3,2,1,0:T(8,128)S(1)}, u32[]{:S(2)}, u32[]{:S(2)}) %collective-permute-start.1) | collective-permute-done | bytes 393248 | tf_op jit(solution)/shard_map/ppermute | solution.py:179
  15.3 4.0 %collective-permute-start.4 = (f32[3,2,128,128]{3,2,1,0:T(8,128)S(1)}, f32[3,2,128,128]{3,2,1,0:T(8,128)S(1)}, u32[]{:S(2)}, u32[]{:S(2)}) collective-permute-start(f32[3,2,128,128]{3,2,1,0:T(8,128)S(1)} %collective-permute-done.1.first_ref), channel_id=1, source_target_pairs={{0,2},{2,4},{3,1},{4,6},{5,3},{6,8},{7,5},{8,10},{9,7},{10,12},{11... | collective-permute-start | bytes 1179656 | tf_op jit(solution)/shard_map/ppermute | solution.py:182
  19.3 4.4 %collective-permute-done.2.first_ref = f32[3,2,128,128]{3,2,1,0:T(8,128)S(1)} collective-permute-done((f32[3,2,128,128]{3,2,1,0:T(8,128)S(1)}, f32[3,2,128,128]{3,2,1,0:T(8,128)S(1)}, u32[]{:S(2)}, u32[]{:S(2)}) %collective-permute-start.2) | collective-permute-done | bytes 393248 | tf_op jit(solution)/shard_map/ppermute | solution.py:179
  23.7 4.8 %collective-permute-start.5 = (f32[3,2,128,128]{3,2,1,0:T(8,128)S(1)}, f32[3,2,128,128]{3,2,1,0:T(8,128)}, u32[]{:S(2)}, u32[]{:S(2)}) collective-permute-start(f32[3,2,128,128]{3,2,1,0:T(8,128)S(1)} %collective-permute-done.2.first_ref), channel_id=1, source_target_pairs={{0,2},{2,4},{3,1},{4,6},{5,3},{6,8},{7,5},{8,10},{9,7},{10,12},{11... | collective-permute-start | bytes 1179656 | tf_op jit(solution)/shard_map/ppermute | solution.py:182
  28.5 0.0 copy-start
  28.5 0.0 copy-start.1
  28.5 0.0 slice-done
  28.5 0.1 collective-permute-start
  28.6 3.7 %collective-permute-done.9.first_ref = f32[3,2,128,128]{3,2,1,0:T(8,128)} collective-permute-done((f32[3,2,128,128]{3,2,1,0:T(8,128)}, f32[3,2,128,128]{3,2,1,0:T(8,128)}, u32[]{:S(2)}, u32[]{:S(2)}) %collective-permute-start.9) | collective-permute-done | bytes 393248 | tf_op jit(solution)/shard_map/ppermute | solution.py:179
  32.2 4.0 %collective-permute-start.10 = (f32[3,2,128,128]{3,2,1,0:T(8,128)}, f32[3,2,128,128]{3,2,1,0:T(8,128)S(1)}, u32[]{:S(2)}, u32[]{:S(2)}) collective-permute-start(f32[3,2,128,128]{3,2,1,0:T(8,128)} %collective-permute-done.9.first_ref), channel_id=1, source_target_pairs={{0,2},{2,4},{3,1},{4,6},{5,3},{6,8},{7,5},{8,10},{9,7},{10,12},{11... | collective-permute-start | bytes 1179656 | tf_op jit(solution)/shard_map/ppermute | solution.py:182
  36.3 3.6 %collective-permute-done.7.first_ref = f32[3,2,128,128]{3,2,1,0:T(8,128)} collective-permute-done((f32[3,2,128,128]{3,2,1,0:T(8,128)}, f32[3,2,128,128]{3,2,1,0:T(8,128)}, u32[]{:S(2)}, u32[]{:S(2)}) %collective-permute-start.7) | collective-permute-done | bytes 393248 | tf_op jit(solution)/shard_map/ppermute | solution.py:179
  39.8 3.7 %collective-permute-start.8 = (f32[3,2,128,128]{3,2,1,0:T(8,128)}, f32[3,2,128,128]{3,2,1,0:T(8,128)S(1)}, u32[]{:S(2)}, u32[]{:S(2)}) collective-permute-start(f32[3,2,128,128]{3,2,1,0:T(8,128)} %collective-permute-done.7.first_ref), channel_id=1, source_target_pairs={{0,2},{2,4},{3,1},{4,6},{5,3},{6,8},{7,5},{8,10},{9,7},{10,12},{11... | collective-permute-start | bytes 1179656 | tf_op jit(solution)/shard_map/ppermute | solution.py:182
  43.5 0.1 fusion.refs_2_
  43.6 0.0 collective-permute-done.4.second_ref
  43.6 0.1 collective-permute-start.3
  43.7 0.0 collective-permute-done.5.second_ref
  43.8 1.4 %collective-permute-start.6 = (f32[2,2,128,128]{3,2,1,0:T(8,128)S(1)}, f32[2,2,128,128]{3,2,1,0:T(8,128)S(1)}, u32[]{:S(2)}, u32[]{:S(2)}) collective-permute-start(f32[2,2,128,128]{3,2,1,0:T(8,128)S(1)} %fusion.1.refs_4_), channel_id=1, source_target_pairs={{0,16},{16,0},{1,17},{17,1},{2,18},{18,2},{3,19},{19,3},{4,20},{20... | collective-permute-start | bytes 786440 | tf_op jit(solution)/shard_map/ppermute | solution.py:160
  45.2 0.0 collective-permute-done.refs_1_
  45.2 0.0 copy-done
  45.2 0.0 copy-done.1
  45.2 6.0 %local.1.acc_ref = f32[12,2,128,128]{3,2,1,0:T(8,128)} custom-call(f32[24]{0:T(128)S(1)} %copy-done.1, f32[12,2,128,128]{3,2,1,0:T(8,128)S(1)} %copy-done, f32[2,2,128,128]{3,2,1,0:T(8,128)S(1)} %constant_dynamic-slice_fusion.refs_0_, f32[2,2,128,128]{3,2,1,0:T(8,128)S(1)} %collective-permute-done.refs_1_), custom_call_target="tpu_custom_call" | custom-call | flops 50000000 | bytes 4000000 | tf_op jit(solution)/shard_map/local/pallas_call | solution.py:185
  51.2 0.0 collective-permute-done.3.refs_3_
  51.2 0.0 collective-permute-done.6.refs_5_
  51.2 1.1 %halo_weights.1.k_ref = f32[2,7,128,128]{3,2,1,0:T(8,128)S(1)} custom-call(f32[24]{0:T(128)S(1)} %copy-done.1, f32[2,2,128,128]{3,2,1,0:T(8,128)S(1)} %constant_dynamic-slice_fusion.refs_0_, f32[2,2,128,128]{3,2,1,0:T(8,128)S(1)} %collective-permute-done.refs_1_, f32[2,2,128,128]{3,2,1,0:T(8,128)S(1)} %fusion.refs_2_, ...), custom_call_target="tpu_custom_call" | custom-call | tf_op jit(solution)/shard_map/halo_weights/pallas_call | solution.py:200
  52.2 2.2 %halo.4.acc_ref = f32[12,2,128,128]{3,2,1,0:T(8,128)} custom-call(f32[2,7,128,128]{3,2,1,0:T(8,128)S(1)} %halo_weights.1.k_ref, f32[3,2,128,128]{3,2,1,0:T(8,128)S(1)} %collective-permute-done.1.first_ref, f32[3,2,128,128]{3,2,1,0:T(8,128)S(1)} %collective-permute-done.4.second_ref, f32[12,2,128,128]{3,2,1,0:T(8,128)} %local.1.acc_ref), custom_call_target="tpu_custom_call", output_to_operand_aliasing={{}: (3, {})} | custom-call | tf_op jit(solution)/shard_map/halo/pallas_call | solution.py:215
  54.5 2.3 %halo.5.acc_ref = f32[12,2,128,128]{3,2,1,0:T(8,128)} custom-call(f32[2,7,128,128]{3,2,1,0:T(8,128)S(1)} %halo_weights.1.k_ref, f32[3,2,128,128]{3,2,1,0:T(8,128)S(1)} %collective-permute-done.2.first_ref, f32[3,2,128,128]{3,2,1,0:T(8,128)} %collective-permute-done.5.second_ref, f32[12,2,128,128]{3,2,1,0:T(8,128)} %halo.4.acc_ref), custom_call_target="tpu_custom_call", output_to_operand_aliasing={{}: (3, {})} | custom-call | tf_op jit(solution)/shard_map/halo/pallas_call | solution.py:215
  56.8 0.0 collective-permute-done.10.second_ref
  56.8 2.3 %halo.6.acc_ref = f32[12,2,128,128]{3,2,1,0:T(8,128)} custom-call(f32[2,7,128,128]{3,2,1,0:T(8,128)S(1)} %halo_weights.1.k_ref, f32[3,2,128,128]{3,2,1,0:T(8,128)} %collective-permute-done.9.first_ref, f32[3,2,128,128]{3,2,1,0:T(8,128)S(1)} %collective-permute-done.10.second_ref, f32[12,2,128,128]{3,2,1,0:T(8,128)} %halo.5.acc_ref), custom_call_target="tpu_custom_call", output_to_operand_aliasing={{}: (3, {})} | custom-call | tf_op jit(solution)/shard_map/halo/pallas_call | solution.py:215
  59.1 0.0 collective-permute-done.8.second_ref
  59.1 2.3 %halo.7 = f32[12,2,128,128]{3,2,1,0:T(8,128)} custom-call(f32[2,7,128,128]{3,2,1,0:T(8,128)S(1)} %halo_weights.1.k_ref, f32[3,2,128,128]{3,2,1,0:T(8,128)} %collective-permute-done.7.first_ref, f32[3,2,128,128]{3,2,1,0:T(8,128)S(1)} %collective-permute-done.8.second_ref, f32[12,2,128,128]{3,2,1,0:T(8,128)} %halo.6.acc_ref), custom_call_target="tpu_custom_call", output_to_operand_aliasing={{}: (3, {})} | custom-call | tf_op jit(solution)/shard_map/halo/pallas_call | solution.py:215
  (2 shorter events, 0.1 us)
Async XLA Ops:
  0.0 28.5 %slice-start = ((f32[12,2,128,128]{3,2,1,0:T(8,128)}), f32[4,2,128,128]{3,2,1,0:T(8,128)S(1)}, s32[]{:S(2)}) async-start(f32[12,2,128,128]{3,2,1,0:T(8,128)} %orb_ref.1), calls=%async_computation | async-start | bytes 1048576 | tf_op jit(solution)/shard_map/slice | solution.py:184
  2.4 12.9 %collective-permute-start.1 = (f32[3,2,128,128]{3,2,1,0:T(8,128)S(1)}, f32[3,2,128,128]{3,2,1,0:T(8,128)S(1)}, u32[]{:S(2)}, u32[]{:S(2)}) collective-permute-start(f32[3,2,128,128]{3,2,1,0:T(8,128)S(1)} %get-tuple-element.8), channel_id=1, source_target_pairs={{0,1},{1,0},{2,3},{3,2},{4,5},{5,4},{6,7},{7,6},{8,9},{9,8},{10,11... | collective-permute-start | bytes 1179656 | tf_op jit(solution)/shard_map/ppermute | solution.py:179
  5.4 18.4 %collective-permute-start.2 = (f32[3,2,128,128]{3,2,1,0:T(8,128)S(1)}, f32[3,2,128,128]{3,2,1,0:T(8,128)S(1)}, u32[]{:S(2)}, u32[]{:S(2)}) collective-permute-start(f32[3,2,128,128]{3,2,1,0:T(8,128)S(1)} %get-tuple-element.7), channel_id=1, source_target_pairs={{0,1},{1,0},{2,3},{3,2},{4,5},{5,4},{6,7},{7,6},{8,9},{9,8},{10,11... | collective-permute-start | bytes 1179656 | tf_op jit(solution)/shard_map/ppermute | solution.py:179
  5.4 26.9 %collective-permute-start.9 = (f32[3,2,128,128]{3,2,1,0:T(8,128)}, f32[3,2,128,128]{3,2,1,0:T(8,128)}, u32[]{:S(2)}, u32[]{:S(2)}) collective-permute-start(f32[3,2,128,128]{3,2,1,0:T(8,128)} %get-tuple-element.5), channel_id=1, source_target_pairs={{0,1},{1,0},{2,3},{3,2},{4,5},{5,4},{6,7},{7,6},{8,9},{9,8},{10,11... | collective-permute-start | bytes 1179656 | tf_op jit(solution)/shard_map/ppermute | solution.py:179
  7.4 32.5 %collective-permute-start.7 = (f32[3,2,128,128]{3,2,1,0:T(8,128)}, f32[3,2,128,128]{3,2,1,0:T(8,128)}, u32[]{:S(2)}, u32[]{:S(2)}) collective-permute-start(f32[3,2,128,128]{3,2,1,0:T(8,128)} %get-tuple-element.6), channel_id=1, source_target_pairs={{0,1},{1,0},{2,3},{3,2},{4,5},{5,4},{6,7},{7,6},{8,9},{9,8},{10,11... | collective-permute-start | bytes 1179656 | tf_op jit(solution)/shard_map/ppermute | solution.py:179
  15.3 28.3 %collective-permute-start.4 = (f32[3,2,128,128]{3,2,1,0:T(8,128)S(1)}, f32[3,2,128,128]{3,2,1,0:T(8,128)S(1)}, u32[]{:S(2)}, u32[]{:S(2)}) collective-permute-start(f32[3,2,128,128]{3,2,1,0:T(8,128)S(1)} %collective-permute-done.1.first_ref), channel_id=1, source_target_pairs={{0,2},{2,4},{3,1},{4,6},{5,3},{6,8},{7,5},{8,10},{9,7},{10,12},{11... | collective-permute-start | bytes 1179656 | tf_op jit(solution)/shard_map/ppermute | solution.py:182
  23.7 20.0 %collective-permute-start.5 = (f32[3,2,128,128]{3,2,1,0:T(8,128)S(1)}, f32[3,2,128,128]{3,2,1,0:T(8,128)}, u32[]{:S(2)}, u32[]{:S(2)}) collective-permute-start(f32[3,2,128,128]{3,2,1,0:T(8,128)S(1)} %collective-permute-done.2.first_ref), channel_id=1, source_target_pairs={{0,2},{2,4},{3,1},{4,6},{5,3},{6,8},{7,5},{8,10},{9,7},{10,12},{11... | collective-permute-start | bytes 1179656 | tf_op jit(solution)/shard_map/ppermute | solution.py:182
  28.5 16.7 %copy-start = (f32[12,2,128,128]{3,2,1,0:T(8,128)S(1)}, f32[12,2,128,128]{3,2,1,0:T(8,128)}, u32[]{:S(2)}) copy-start(f32[12,2,128,128]{3,2,1,0:T(8,128)} %orb_ref.1) | copy-start | bytes 4718596
  28.5 16.7 %copy-start.1 = (f32[24]{0:T(128)S(1)}, f32[24]{0:T(128)}, u32[]{:S(2)}) copy-start(f32[24]{0:T(128)} %occ_ref.3) | copy-start | bytes 292
  28.5 16.7 %collective-permute-start = (f32[2,2,128,128]{3,2,1,0:T(8,128)S(1)}, f32[2,2,128,128]{3,2,1,0:T(8,128)S(1)}, u32[]{:S(2)}, u32[]{:S(2)}) collective-permute-start(f32[2,2,128,128]{3,2,1,0:T(8,128)S(1)} %constant_dynamic-slice_fusion.refs_0_), channel_id=1, source_target_pairs={{0,16},{16,0},{1,17},{17,1},{2,18},{18,2},{3,19},{19,3},{4,20},{20... | collective-permute-start | bytes 786440 | tf_op jit(solution)/shard_map/ppermute | solution.py:160
  32.2 24.5 %collective-permute-start.10 = (f32[3,2,128,128]{3,2,1,0:T(8,128)}, f32[3,2,128,128]{3,2,1,0:T(8,128)S(1)}, u32[]{:S(2)}, u32[]{:S(2)}) collective-permute-start(f32[3,2,128,128]{3,2,1,0:T(8,128)} %collective-permute-done.9.first_ref), channel_id=1, source_target_pairs={{0,2},{2,4},{3,1},{4,6},{5,3},{6,8},{7,5},{8,10},{9,7},{10,12},{11... | collective-permute-start | bytes 1179656 | tf_op jit(solution)/shard_map/ppermute | solution.py:182
  39.8 19.3 %collective-permute-start.8 = (f32[3,2,128,128]{3,2,1,0:T(8,128)}, f32[3,2,128,128]{3,2,1,0:T(8,128)S(1)}, u32[]{:S(2)}, u32[]{:S(2)}) collective-permute-start(f32[3,2,128,128]{3,2,1,0:T(8,128)} %collective-permute-done.7.first_ref), channel_id=1, source_target_pairs={{0,2},{2,4},{3,1},{4,6},{5,3},{6,8},{7,5},{8,10},{9,7},{10,12},{11... | collective-permute-start | bytes 1179656 | tf_op jit(solution)/shard_map/ppermute | solution.py:182
  43.6 7.6 %collective-permute-start.3 = (f32[2,2,128,128]{3,2,1,0:T(8,128)S(1)}, f32[2,2,128,128]{3,2,1,0:T(8,128)S(1)}, u32[]{:S(2)}, u32[]{:S(2)}) collective-permute-start(f32[2,2,128,128]{3,2,1,0:T(8,128)S(1)} %fusion.refs_2_), channel_id=1, source_target_pairs={{0,16},{16,0},{1,17},{17,1},{2,18},{18,2},{3,19},{19,3},{4,20},{20... | collective-permute-start | bytes 786440 | tf_op jit(solution)/shard_map/ppermute | solution.py:160
  43.8 7.4 %collective-permute-start.6 = (f32[2,2,128,128]{3,2,1,0:T(8,128)S(1)}, f32[2,2,128,128]{3,2,1,0:T(8,128)S(1)}, u32[]{:S(2)}, u32[]{:S(2)}) collective-permute-start(f32[2,2,128,128]{3,2,1,0:T(8,128)S(1)} %fusion.1.refs_4_), channel_id=1, source_target_pairs={{0,16},{16,0},{1,17},{17,1},{2,18},{18,2},{3,19},{19,3},{4,20},{20... | collective-permute-start | bytes 786440 | tf_op jit(solution)/shard_map/ppermute | solution.py:160

commit v2 on v1

v2 whole, which is shorter than its diff:
```python
import functools

import jax
import jax.numpy as jnp
from jax import lax
from jax.experimental import pallas as pl
from jax.experimental.pallas import tpu as pltpu
from jax.sharding import PartitionSpec as P

BLOCK = 2
STEPS = 2
PLANES = 2
CHUNKS = (5, 4, 5, 5, 5)

ONE = 1.0 / 36.0
TWO = 1.0 / 216.0
CROSS = 2.0 / 216.0

OWN = [(0, 0), (1, 0), (-1, 0), (2, 0), (-2, 0), (0, 1), (1, 1), (-1, 1), (0, -1), (1, -1), (-1, -1), (0, 2), (0, -2)]
BESIDE = [(0, 0), (1, 0), (-1, 0), (0, 1), (0, -1)]
BEYOND, ACROSS = len(BESIDE), len(BESIDE) + 1


def shifted(field, dy, dz):
    rows, columns = field.shape
    if dy:
        field = pltpu.roll(field, (-dy) % rows, 0)
    if dz:
        field = pltpu.roll(field, (-dz) % columns, 1)
    return field


def inside(shape, dy, dz):
    y = lax.broadcasted_iota(jnp.int32, shape, 0) + dy
    z = lax.broadcasted_iota(jnp.int32, shape, 1) - dz
    return (y >= 0) & (y < shape[0]) & (z >= 0) & (z < shape[1])


def pair_weight(here, there, dy, dz, scale):
    total = None
    for h, t in zip(here, there):
        term = shifted(h, 0, -dz) * shifted(t, dy, 0)
        total = term if total is None else total + term
    total = total * (-scale)
    if dy or dz:
        total = jnp.where(inside(total.shape, dy, dz), total, 0.0)
    return total


def scale_of(dy, dz, dx):
    length = abs(dx) + abs(dy) + abs(dz)
    if length == 1:
        return ONE
    return TWO if max(abs(dx), abs(dy), abs(dz)) == 2 else CROSS


def block_weights(occ_ref, orb_count):
    groups = lax.axis_size("band")
    out = []
    for step in range(STEPS):
        s = lax.rem(lax.axis_index("band") + step, STEPS) if groups == STEPS else step
        first = s * (groups // STEPS) * orb_count + s * BLOCK
        out += [occ_ref[first + i] for i in range(BLOCK)]
    return out


def local_weight_kernel(orb_count, occ_ref, *refs):
    block_refs, k_ref = refs[:STEPS], refs[STEPS]
    rows, columns = k_ref.shape[2:]
    weights = block_weights(occ_ref, orb_count)
    dom, slabs = lax.axis_index("dom"), lax.axis_size("dom")
    for p in range(PLANES):
        here = [r[i, p] for r in block_refs for i in range(BLOCK)]
        there = [r[i, 1 - p] for r in block_refs for i in range(BLOCK)]
        weighted = [w * h for w, h in zip(weights, here)]
        outer = jnp.where(dom == (0 if p == 0 else slabs - 1), 0.0, 1.0)
        y = lax.broadcasted_iota(jnp.int32, (rows, columns), 0)
        z = lax.broadcasted_iota(jnp.int32, (rows, columns), 1)
        edges = (y > 0).astype(jnp.float32) + (y < rows - 1).astype(jnp.float32)
        edges = edges + (z > 0).astype(jnp.float32) + (z < columns - 1).astype(jnp.float32)
        centre = 1.0 / 6.0 + (edges + (1.0 + outer)) * TWO
        for k, (dy, dz) in enumerate(OWN):
            if k == 0:
                k_ref[p, k] = pair_weight(weighted, here, 0, 0, 1.0) * centre
            else:
                k_ref[p, k] = pair_weight(weighted, here, dy, dz, scale_of(dy, dz, 0))
        for k, (dy, dz) in enumerate(BESIDE):
            k_ref[p, len(OWN) + k] = pair_weight(weighted, there, dy, dz, scale_of(dy, dz, 1))


def local_kernel(k_ref, orb_ref, *acc_refs):
    base = 0
    for acc_ref in acc_refs:

        @pl.loop(0, acc_ref.shape[0])
        def _(j, acc_ref=acc_ref, base=base):
            for p in range(PLANES):
                groups = {}
                for plane, terms, first in ((p, OWN, 0), (1 - p, BESIDE, len(OWN))):
                    field = orb_ref[base + j, plane]
                    for k, (dy, dz) in enumerate(terms):
                        term = k_ref[p, first + k] * shifted(field, dy, 0)
                        groups[dz] = groups[dz] + term if dz in groups else term
                out = groups[0]
                for dz in (1, -1, 2, -2):
                    out = out + shifted(groups[dz], 0, dz)
                acc_ref[j, p] = out

        base += acc_ref.shape[0]


def nearest():
    odd = lax.rem(lax.axis_index("dom"), 2)
    return odd, 1 - odd


def halo_weight_kernel(orb_count, occ_ref, *refs):
    n = STEPS
    local, slabs = refs[:n], refs[n : 3 * n]
    k_refs = refs[3 * n :]
    weights = block_weights(occ_ref, orb_count)
    dom, count = lax.axis_index("dom"), lax.axis_size("dom")
    real = (1.0, jnp.where((dom == 0) | (dom == count - 1), 0.0, 1.0))
    for h, near in enumerate(nearest()):
        far = 1 - near
        here = [w * r[i, far] for w, (r, i) in zip(weights, [(r, i) for r in local for i in range(BLOCK)])]
        behind = [w * r[i, near] for w, (r, i) in zip(weights, [(r, i) for r in local for i in range(BLOCK)])]
        there = [r[i, near] for r in slabs[h::2] for i in range(BLOCK)]
        beyond = [r[i, far] for r in slabs[h::2] for i in range(BLOCK)]
        for k, (dy, dz) in enumerate(BESIDE):
            k_refs[h][k] = pair_weight(here, there, dy, dz, scale_of(dy, dz, 1) * real[h])
        k_refs[h][BEYOND] = pair_weight(here, beyond, 0, 0, TWO * real[h])
        k_refs[h][ACROSS] = pair_weight(behind, there, 0, 0, TWO * real[h])


def add_near(out_ref, j, k_ref, plane, near):
    groups = {}
    for k, (dy, dz) in enumerate(BESIDE):
        term = k_ref[k] * shifted(plane, dy, 0)
        groups[dz] = groups[dz] + term if dz in groups else term
    out_ref[j, 1 - near] += groups[0] + shifted(groups[1], 0, 1) + shifted(groups[-1], 0, -1)
    out_ref[j, near] += k_ref[ACROSS] * plane


def add_far(out_ref, j, k_ref, plane, near):
    out_ref[j, 1 - near] += k_ref[BEYOND] * plane


def add_chunk(out_ref, origin, k_ref, chunk_ref, start, near):
    size = chunk_ref.shape[0]
    head = start % PLANES
    full = (size - head) // PLANES
    for at in ([0] if head else []) + ([size - 1] if (size - head) % PLANES else []):
        j, m = (start + at) // PLANES - origin, (start + at) % PLANES

        @pl.when(near == m)
        def _(j=j, at=at):
            add_near(out_ref, j, k_ref, chunk_ref[at], near)

        @pl.when(near != m)
        def _(j=j, at=at):
            add_far(out_ref, j, k_ref, chunk_ref[at], near)

    first = (start + head) // PLANES - origin

    @pl.loop(0, full)
    def _(i):
        at = head + PLANES * i
        add_near(out_ref, first + i, k_ref, chunk_ref[at + near], near)
        add_far(out_ref, first + i, k_ref, chunk_ref[at + 1 - near], near)


def finish_kernel(parts, origin, written, chained, *refs):
    n = len(parts)
    k_refs, chunk_refs, acc_ref = refs[:2], refs[2 : 2 + n], refs[2 + n]
    refs = refs[3 + n + chained :]
    out_ref, refs = refs[0], refs[1:]
    rest = acc_ref.shape[0] - written
    sum_ref, sems = refs[-2:]
    sum_ref[...] = acc_ref[...]
    near = nearest()
    for (hop, start), chunk_ref in zip(parts, chunk_refs):
        add_chunk(sum_ref, origin, k_refs[hop], chunk_ref, start, near[hop])
    copies = [
        pltpu.make_async_copy(sum_ref.at[j], out_ref.at[origin + j], sems.at[j]) for j in range(written)
    ]
    for copy in copies:
        copy.start()
    if rest:
        refs[0][...] = sum_ref[pl.ds(written, rest)]
    for copy in copies:
        copy.wait()


VMEM = pl.BlockSpec(memory_space=pltpu.VMEM)
SMEM = pl.BlockSpec(memory_space=pltpu.SMEM)
ANY = pl.BlockSpec(memory_space=pl.ANY)
PARAMS = pltpu.CompilerParams(vmem_limit_bytes=16 * 1024 * 1024)


def finish(name, parts, origin, written, weights, chunks, acc, out, shape):
    rest = acc.shape[0] - written
    out_shape, out_specs = [jax.ShapeDtypeStruct(shape, jnp.float32)], [ANY]
    if rest:
        out_shape.append(jax.ShapeDtypeStruct((rest, *acc.shape[1:]), jnp.float32))
        out_specs.append(VMEM)
    chained = out is not None
    result = pl.pallas_call(
        functools.partial(finish_kernel, parts, origin, written, chained),
        out_shape=out_shape,
        in_specs=[VMEM] * (3 + len(parts)) + [ANY] * chained,
        out_specs=out_specs,
        input_output_aliases={3 + len(parts): 0} if chained else {},
        scratch_shapes=[pltpu.VMEM(acc.shape, jnp.float32), pltpu.SemaphoreType.DMA((written,))],
        compiler_params=PARAMS,
        cost_estimate=pl.CostEstimate(flops=1, bytes_accessed=1, transcendentals=0),
        name=name,
    )(*weights, *chunks, acc, *([out] if chained else []))
    return result


def hops(slabs):
    swap = [(i, i ^ 1) for i in range(slabs)]
    onward = [(i, i + 2 if i % 2 == 0 else i - 2) for i in range(slabs)]
    ring = [(a, b % slabs) for a, b in onward]
    closed = [(a, b if 0 <= b < slabs else a ^ 1) for a, b in onward]
    return swap, ring, closed


def everywhere(field, groups):
    band, axis = lax.axis_index("band"), field.ndim - 4
    if groups == STEPS:
        own = lax.dynamic_slice_in_dim(field, band * BLOCK, BLOCK, axis)
        with jax.named_scope("band_swap"):
            return [own] + [
                lax.ppermute(own, "band", [(i, (i - step) % STEPS) for i in range(STEPS)]) for step in range(1, STEPS)
            ]
    out = []
    for step in range(STEPS):
        mine = lax.slice_in_dim(field, step * BLOCK, (step + 1) * BLOCK, axis=axis)
        mine = jnp.where(band == step * (groups // STEPS), mine, jnp.zeros_like(mine))
        out.append(lax.psum(mine, "band"))
    return out


def after(value, *others):
    return lax.optimization_barrier((value, *others))[0]


def per_device(orbitals, occupations):
    orb_count, planes, rows, columns = orbitals.shape
    groups, slabs = lax.axis_size("band"), lax.axis_size("dom")
    assert planes == PLANES and slabs % 2 == 0 and slabs > 2 and sum(CHUNKS) == orb_count * planes
    swap, ring, closed = hops(slabs)
    starts = [sum(CHUNKS[:i]) for i in range(len(CHUNKS))]
    cuts = (0, starts[-2] // planes, starts[-1] // planes, orb_count)
    assert starts[-2] % planes == 0
    f32 = lambda *shape: jax.ShapeDtypeStruct(shape, jnp.float32)

    flat = orbitals.reshape(-1, rows, columns)
    head = flat[: CHUNKS[0]]
    sent = [head] + [flat[s : s + n] for s, n in zip(starts[1:], CHUNKS[1:])]
    first = []
    for i, part in enumerate(sent):
        with jax.named_scope(f"hop1_part{i}"):
            first.append(lax.ppermute(part, "dom", swap))

    local = everywhere(orbitals[: STEPS * BLOCK], groups)
    k_local = pl.pallas_call(
        functools.partial(local_weight_kernel, orb_count),
        out_shape=f32(planes, len(OWN) + len(BESIDE), rows, columns),
        in_specs=[SMEM] + [VMEM] * STEPS,
        out_specs=VMEM,
        compiler_params=PARAMS,
        cost_estimate=pl.CostEstimate(flops=1, bytes_accessed=1, transcendentals=0),
        name="local_weights",
    )(occupations, *local)
    acc = pl.pallas_call(
        local_kernel,
        out_shape=[f32(b - a, planes, rows, columns) for a, b in ((0, cuts[1]), (cuts[1], orb_count))],
        in_specs=[VMEM] * 2,
        out_specs=[VMEM] * 2,
        compiler_params=PARAMS,
        cost_estimate=pl.CostEstimate(flops=1, bytes_accessed=1, transcendentals=0),
        name="local",
    )(k_local, orbitals)

    second = []
    for i, part in enumerate(first):
        if i == 1:
            part = after(part, k_local)
        if i == 2:
            part = after(part, acc)
        with jax.named_scope(f"hop2_part{i}"):
            second.append(lax.ppermute(part, "dom", closed if i == len(CHUNKS) - 1 else ring))

    count = 0
    while sum(CHUNKS[:count]) < STEPS * BLOCK * planes:
        count += 1
    near = [
        jnp.concatenate(part[:count])[: STEPS * BLOCK * planes].reshape(-1, planes, rows, columns)
        for part in (first, second)
    ]
    near[0] = after(near[0], second[0])
    near = [x for part in zip(*[everywhere(f, groups) for f in near]) for x in part]
    k_halo = pl.pallas_call(
        functools.partial(halo_weight_kernel, orb_count),
        out_shape=[f32(ACROSS + 1, rows, columns)] * 2,
        in_specs=[SMEM] + [VMEM] * (3 * STEPS),
        out_specs=[VMEM] * 2,
        compiler_params=PARAMS,
        cost_estimate=pl.CostEstimate(flops=1, bytes_accessed=1, transcendentals=0),
        name="halo_weights",
    )(occupations, *local, *near)

    n = len(CHUNKS)
    early = [(hop, i) for i in range(n - 2) for hop in (0, 1)]
    later = [(0, n - 2), (0, n - 1), (1, n - 2)]
    last = [(1, n - 1)]
    out, origin, rest = None, 0, None
    for name, parts, upto in (("early", early, cuts[1]), ("later", later, cuts[2]), ("last", last, orb_count)):
        chunks = [(first, second)[hop][i] for hop, i in parts]
        part_acc = {"early": acc[0], "later": acc[1], "last": rest}[name]
        result = finish(
            name, [(hop, starts[i]) for hop, i in parts], origin, upto - origin, k_halo, chunks, part_acc, out, orbitals.shape
        )
        out, rest = result[0], result[-1]
        origin = upto
    return out


def solution(mesh):
    in_specs = (P("band", "dom", None, None), P())
    out_specs = P("band", "dom", None, None)
    return jax.shard_map(
        per_device, mesh=mesh, in_specs=in_specs, out_specs=out_specs, check_vma=False
    )
```

time: 61.7 us -> 50.1 us (0.81)
  starting transfers between devices: 23.1 us -> 18.2 us
  Pallas kernels: 16.2 us -> 11.4 us
  local copies, waits for them, and re-layouts: 2.44 us -> 1.38 us
  waiting for transfers between devices: 19.5 us -> 18.8 us
    pallas_call x6, Pallas kernels: 16.2 us -> 11.4 us  [the longest x3 5.53 us: finish(): pl.pallas_call(functools.partial(finish_kernel, parts, origin, written, c...]
    ppermute x8 -> x10, starting transfers between devices: 21.5 us -> 17 us  [the longest x5 10.1 us: per_device(): lax.ppermute(part, 'dom', closed if i == len(CHUNKS) - 1 else ring)]
    slice x1 -> x2, local copies, waits for them, and re-layouts: 2.41 us -> 0.1 us  [per_device(): sent = [head] + [flat[s:s + n] for s, n in zip(starts[1:], CHUNKS[1:])]]
    ppermute x8 -> x10, waiting for transfers between devices: 19.5 us -> 17.5 us  [the longest x5 17.4 us: per_device(): first.append(lax.ppermute(part, 'dom', swap))]
    ppermute x3, waiting for transfers between devices: 0.01 us -> 1.32 us  [everywhere(): lax.ppermute(own, 'band', [(i, (i - step) % STEPS) for i in range(STEPS)])]
    slice x2 -> x1, local copies, waits for them, and re-layouts: 0.01 us -> 1.2 us  [per_device(): local = everywhere(orbitals[:STEPS * BLOCK], groups)]
  transfers between devices with their start and end apart: 11 -> 13, of which waited for: 4 -> 8; matrix products, arithmetic and copies ran while one was open for 0% -> 0% of each run, Pallas kernels for 23% -> 20%
where the time goes in v2:
time: 50.1 us; the launch traced here: 50 us
  waiting for transfers between devices  18.8 us (38%)
  starting transfers between devices  18.2 us (36%)
  Pallas kernels  11.4 us (23%)
  local copies, waits for them, and re-layouts  1.38 us (3%)
    ppermute x5, waiting for transfers between devices, per_device(): first.append(lax.ppermute(part, 'dom', swap))  17.4 us
    ppermute x5, starting transfers between devices, per_device(): lax.ppermute(part, 'dom', closed if i == len(CHUNKS) - 1 else ring)  10.1 us
    ppermute x5, starting transfers between devices, per_device(): first.append(lax.ppermute(part, 'dom', swap))  6.93 us
    pallas_call x3, Pallas kernels, finish(): pl.pallas_call(functools.partial(finish_kernel, parts, origin, written, c...  5.53 us
    pallas_call x1, Pallas kernels, per_device(): pl.pallas_call(local_kernel, out_shape=[f32(b - a, planes, rows, columns)...  3.07 us
    pallas_call x1, Pallas kernels, per_device(): pl.pallas_call(functools.partial(local_weight_kernel, orb_count), out_sha...  1.79 us
    ppermute x3, waiting for transfers between devices, everywhere(): lax.ppermute(own, 'band', [(i, (i - step) % STEPS) for i in range(STEPS)])  1.32 us
    slice x1, local copies, waits for them, and re-layouts, per_device(): local = everywhere(orbitals[:STEPS * BLOCK], groups)  1.2 us
  transfers between devices with their start and end apart: 13, of which 8 were waited for; matrix products, arithmetic and copies ran while one was open for 0% of the time, Pallas kernels for 20%

profile of v2, /device:TPU:0, one launch (start us, length us, event | category | flops | bytes accessed | tf_op | source)
XLA Modules:
  0.0 50.0 jit_solution(5540435880003555782)
XLA Ops:
  0.0 0.0 copy-start
  0.0 1.2 %slice.24 = f32[4,2,128,128]{3,2,1,0:T(8,128)S(1)} slice(f32[12,2,128,128]{3,2,1,0:T(8,128)} %orb_ref.1), slice={[0:4], [0:2], [0:128], [0:128]} | slice | bytes 1048576 | tf_op jit(solution)/shard_map/slice | solution.py:268
  1.2 0.5 %collective-permute-start = (f32[2,2,128,128]{3,2,1,0:T(8,128)S(1)}, f32[2,2,128,128]{3,2,1,0:T(8,128)S(1)}, u32[]{:S(2)}, u32[]{:S(2)}) collective-permute-start(f32[2,2,128,128]{3,2,1,0:T(8,128)S(1)} %constant_dynamic-slice_fusion.2.refs_0_), channel_id=1, source_target_pairs={{0,16},{16,0},{1,17},{17,1},{2,18},{18,2},{3,19},{19,3},{4,20},{20... | collective-permute-start | bytes 786440 | tf_op jit(solution)/shard_map/band_swap/ppermute | solution.py:236
  1.8 0.0 copy-done
  1.8 0.0 copy-start.1
  1.8 0.1 fusion
  1.9 2.8 %collective-permute-start.1 = (f32[5,128,128]{2,1,0:T(8,128)S(1)}, f32[5,128,128]{2,1,0:T(8,128)S(1)}, u32[]{:S(2)}, u32[]{:S(2)}) collective-permute-start(f32[5,128,128]{2,1,0:T(8,128)S(1)} %get-tuple-element.26), channel_id=1, source_target_pairs={{0,1},{1,0},{2,3},{3,2},{4,5},{5,4},{6,7},{7,6},{8,9},{9,8},{10,11... | collective-permute-start | bytes 983048 | tf_op jit(solution)/shard_map/hop1_part0/ppermute | solution.py:266
  4.7 0.1 collective-permute-start.2
  4.8 2.0 %collective-permute-start.11 = (f32[5,128,128]{2,1,0:T(8,128)S(1)}, f32[5,128,128]{2,1,0:T(8,128)S(1)}, u32[]{:S(2)}, u32[]{:S(2)}) collective-permute-start(f32[5,128,128]{2,1,0:T(8,128)S(1)} %get-tuple-element.23), channel_id=1, source_target_pairs={{0,1},{1,0},{2,3},{3,2},{4,5},{5,4},{6,7},{7,6},{8,9},{9,8},{10,11... | collective-permute-start | bytes 983048 | tf_op jit(solution)/shard_map/hop1_part2/ppermute | solution.py:266
  6.8 0.1 collective-permute-start.9
  6.9 0.0 collective-permute-done.refs_1_
  6.9 1.9 %collective-permute-start.7 = (f32[5,128,128]{2,1,0:T(8,128)S(1)}, f32[5,128,128]{2,1,0:T(8,128)S(1)}, u32[]{:S(2)}, u32[]{:S(2)}) collective-permute-start(f32[5,128,128]{2,1,0:T(8,128)S(1)} %get-tuple-element.25), channel_id=1, source_target_pairs={{0,1},{1,0},{2,3},{3,2},{4,5},{5,4},{6,7},{7,6},{8,9},{9,8},{10,11... | collective-permute-start | bytes 983048 | tf_op jit(solution)/shard_map/hop1_part4/ppermute | solution.py:266
  8.8 4.3 %collective-permute-done.1.refs_2_ = f32[5,128,128]{2,1,0:T(8,128)S(1)} collective-permute-done((f32[5,128,128]{2,1,0:T(8,128)S(1)}, f32[5,128,128]{2,1,0:T(8,128)S(1)}, u32[]{:S(2)}, u32[]{:S(2)}) %collective-permute-start.1) | collective-permute-done | bytes 327712 | tf_op jit(solution)/shard_map/hop1_part0/ppermute | solution.py:266
  13.1 2.1 %collective-permute-start.3 = (f32[5,128,128]{2,1,0:T(8,128)S(1)}, f32[5,128,128]{2,1,0:T(8,128)S(1)}, u32[]{:S(2)}, u32[]{:S(2)}) collective-permute-start(f32[5,128,128]{2,1,0:T(8,128)S(1)} %collective-permute-done.1.refs_2_), channel_id=1, source_target_pairs={{0,2},{1,15},{2,4},{3,1},{4,6},{5,3},{6,8},{7,5},{8,10},{9,7},{10,... | collective-permute-start | bytes 983048 | tf_op jit(solution)/shard_map/hop2_part0/ppermute | solution.py:295
  15.2 0.0 copy-done.1
  15.2 1.8 %local_weights.1.k_ref = f32[2,18,128,128]{3,2,1,0:T(8,128)S(1)} custom-call(f32[24]{0:T(128)S(1)} %copy-done.1, f32[2,2,128,128]{3,2,1,0:T(8,128)S(1)} %constant_dynamic-slice_fusion.2.refs_0_, f32[2,2,128,128]{3,2,1,0:T(8,128)S(1)} %collective-permute-done.refs_1_), custom_call_target="tpu_custom_call" | custom-call | flops 1 | bytes 1 | tf_op jit(solution)/shard_map/local_weights/pallas_call | solution.py:269
  17.0 1.7 %collective-permute-done.2.refs_4_ = f32[4,128,128]{2,1,0:T(8,128)S(1)} collective-permute-done((f32[4,128,128]{2,1,0:T(8,128)S(1)}, f32[4,128,128]{2,1,0:T(8,128)S(1)}, u32[]{:S(2)}, u32[]{:S(2)}) %collective-permute-start.2) | collective-permute-done | bytes 262176 | tf_op jit(solution)/shard_map/hop1_part1/ppermute | solution.py:266
  18.8 2.1 %collective-permute-start.4 = (f32[4,128,128]{2,1,0:T(8,128)S(1)}, f32[4,128,128]{2,1,0:T(8,128)S(1)}, u32[]{:S(2)}, u32[]{:S(2)}) collective-permute-start(f32[4,128,128]{2,1,0:T(8,128)S(1)} %collective-permute-done.2.refs_4_), channel_id=1, source_target_pairs={{0,2},{1,15},{2,4},{3,1},{4,6},{5,3},{6,8},{7,5},{8,10},{9,7},{10,... | collective-permute-start | bytes 786440 | tf_op jit(solution)/shard_map/hop2_part1/ppermute | solution.py:295
  20.9 3.1 %local.1 = (f32[7,2,128,128]{3,2,1,0:T(8,128)S(1)}, f32[5,2,128,128]{3,2,1,0:T(8,128)S(1)}) custom-call(f32[2,18,128,128]{3,2,1,0:T(8,128)S(1)} %local_weights.1.k_ref, f32[12,2,128,128]{3,2,1,0:T(8,128)S(1)} %copy-done), custom_call_target="tpu_custom_call" | custom-call | flops 1 | bytes 1 | tf_op jit(solution)/shard_map/local/pallas_call | solution.py:278
  23.9 1.9 %collective-permute-done.11.refs_6_ = f32[5,128,128]{2,1,0:T(8,128)S(1)} collective-permute-done((f32[5,128,128]{2,1,0:T(8,128)S(1)}, f32[5,128,128]{2,1,0:T(8,128)S(1)}, u32[]{:S(2)}, u32[]{:S(2)}) %collective-permute-start.11) | collective-permute-done | bytes 327712 | tf_op jit(solution)/shard_map/hop1_part2/ppermute | solution.py:266
  25.8 2.1 %collective-permute-start.12 = (f32[5,128,128]{2,1,0:T(8,128)S(1)}, f32[5,128,128]{2,1,0:T(8,128)S(1)}, u32[]{:S(2)}, u32[]{:S(2)}) collective-permute-start(f32[5,128,128]{2,1,0:T(8,128)S(1)} %collective-permute-done.11.refs_6_), channel_id=1, source_target_pairs={{0,2},{1,15},{2,4},{3,1},{4,6},{5,3},{6,8},{7,5},{8,10},{9,7},{10,... | collective-permute-start | bytes 983048 | tf_op jit(solution)/shard_map/hop2_part2/ppermute | solution.py:295
  27.9 4.9 %collective-permute-done.9.refs_2_ = f32[5,128,128]{2,1,0:T(8,128)S(1)} collective-permute-done((f32[5,128,128]{2,1,0:T(8,128)S(1)}, f32[5,128,128]{2,1,0:T(8,128)S(1)}, u32[]{:S(2)}, u32[]{:S(2)}) %collective-permute-start.9) | collective-permute-done | bytes 327712 | tf_op jit(solution)/shard_map/hop1_part3/ppermute | solution.py:266
  32.8 2.1 %collective-permute-start.10 = (f32[5,128,128]{2,1,0:T(8,128)S(1)}, f32[5,128,128]{2,1,0:T(8,128)S(1)}, u32[]{:S(2)}, u32[]{:S(2)}) collective-permute-start(f32[5,128,128]{2,1,0:T(8,128)S(1)} %collective-permute-done.9.refs_2_), channel_id=1, source_target_pairs={{0,2},{1,15},{2,4},{3,1},{4,6},{5,3},{6,8},{7,5},{8,10},{9,7},{10,... | collective-permute-start | bytes 983048 | tf_op jit(solution)/shard_map/hop2_part3/ppermute | solution.py:295
  34.9 4.6 %collective-permute-done.7.refs_3_ = f32[5,128,128]{2,1,0:T(8,128)S(1)} collective-permute-done((f32[5,128,128]{2,1,0:T(8,128)S(1)}, f32[5,128,128]{2,1,0:T(8,128)S(1)}, u32[]{:S(2)}, u32[]{:S(2)}) %collective-permute-start.7) | collective-permute-done | bytes 327712 | tf_op jit(solution)/shard_map/hop1_part4/ppermute | solution.py:266
  39.5 1.8 %collective-permute-start.8 = (f32[5,128,128]{2,1,0:T(8,128)S(1)}, f32[5,128,128]{2,1,0:T(8,128)S(1)}, u32[]{:S(2)}, u32[]{:S(2)}) collective-permute-start(f32[5,128,128]{2,1,0:T(8,128)S(1)} %collective-permute-done.7.refs_3_), channel_id=1, source_target_pairs={{0,2},{1,0},{2,4},{3,1},{4,6},{5,3},{6,8},{7,5},{8,10},{9,7},{10,1... | collective-permute-start | bytes 983048 | tf_op jit(solution)/shard_map/hop2_part4/ppermute | solution.py:295
  41.3 0.0 collective-permute-done.4.refs_5_
  41.3 0.0 collective-permute-done.3.refs_3_
  41.4 0.1 collective-permute-start.6
  41.5 0.5 %collective-permute-start.5 = (f32[2,2,128,128]{3,2,1,0:T(8,128)S(1)}, f32[2,2,128,128]{3,2,1,0:T(8,128)S(1)}, u32[]{:S(2)}, u32[]{:S(2)}) collective-permute-start(f32[2,2,128,128]{3,2,1,0:T(8,128)S(1)} %constant_dynamic-slice_fusion.1.refs_2_), channel_id=1, source_target_pairs={{0,16},{16,0},{1,17},{17,1},{2,18},{18,2},{3,19},{19,3},{4,20},{20... | collective-permute-start | bytes 786440 | tf_op jit(solution)/shard_map/band_swap/ppermute | solution.py:236
  42.0 0.9 %collective-permute-done.6.refs_5_ = f32[2,2,128,128]{3,2,1,0:T(8,128)S(1)} collective-permute-done((f32[2,2,128,128]{3,2,1,0:T(8,128)S(1)}, f32[2,2,128,128]{3,2,1,0:T(8,128)S(1)}, u32[]{:S(2)}, u32[]{:S(2)}) %collective-permute-start.6) | collective-permute-done | bytes 262176 | tf_op jit(solution)/shard_map/band_swap/ppermute | solution.py:236
  43.0 0.4 collective-permute-done.5.refs_4_
  43.4 1.0 %halo_weights.1 = (f32[7,128,128]{2,1,0:T(8,128)S(1)}, f32[7,128,128]{2,1,0:T(8,128)S(1)}) custom-call(f32[24]{0:T(128)S(1)} %copy-done.1, f32[2,2,128,128]{3,2,1,0:T(8,128)S(1)} %constant_dynamic-slice_fusion.2.refs_0_, f32[2,2,128,128]{3,2,1,0:T(8,128)S(1)} %collective-permute-done.refs_1_, f32[2,2,128,128]{3,2,1,0:T(8,128)S(1)} %constant_dynamic-slice_fusion.1.refs_2_, ...), custom_call_target="tpu_custom_call" | custom-call | flops 1 | bytes 1 | tf_op jit(solution)/shard_map/halo_weights/pallas_call | solution.py:306
  44.4 0.0 collective-permute-done.12.refs_7_
  44.4 2.8 %early.1.refs_6_ = f32[12,2,128,128]{3,2,1,0:T(8,128)} custom-call(f32[7,128,128]{2,1,0:T(8,128)S(1)} %get-tuple-element.16.refs_0_, f32[7,128,128]{2,1,0:T(8,128)S(1)} %get-tuple-element.17.refs_1_, f32[5,128,128]{2,1,0:T(8,128)S(1)} %collective-permute-done.1.refs_2_, f32[5,128,128]{2,1,0:T(8,128)S(1)} %collective-permute-done.3.refs_3_, ...), custom_call_target="tpu_custom_call" | custom-call | flops 1 | bytes 1 | tf_op jit(solution)/shard_map/early/pallas_call | solution.py:208
  47.1 0.0 collective-permute-done.10.refs_4_
  47.2 1.6 %later.1 = (f32[12,2,128,128]{3,2,1,0:T(8,128)}, f32[3,2,128,128]{3,2,1,0:T(8,128)S(1)}) custom-call(f32[7,128,128]{2,1,0:T(8,128)S(1)} %get-tuple-element.16.refs_0_, f32[7,128,128]{2,1,0:T(8,128)S(1)} %get-tuple-element.17.refs_1_, f32[5,128,128]{2,1,0:T(8,128)S(1)} %collective-permute-done.9.refs_2_, ...), custom_call_target="tpu_custom_call", output_to_operand_aliasing={{0}: (6, {})} | custom-call | flops 1 | bytes 1 | tf_op jit(solution)/shard_map/later/pallas_call | solution.py:208
  48.8 0.1 collective-permute-done.8.refs_2_
  48.8 1.1 %last.1 = f32[12,2,128,128]{3,2,1,0:T(8,128)} custom-call(f32[7,128,128]{2,1,0:T(8,128)S(1)} %get-tuple-element.16.refs_0_, f32[7,128,128]{2,1,0:T(8,128)S(1)} %get-tuple-element.17.refs_1_, f32[5,128,128]{2,1,0:T(8,128)S(1)} %collective-permute-done.8.refs_2_, f32[3,2,128,128]{3,2,1,0:T(8,128)S(1)} %get-tuple-element.21.refs_3_, ...), custom_call_target="tpu_custom_call", output_to_operand_aliasing={{}: (4, {})} | custom-call | flops 1 | bytes 1 | tf_op jit(solution)/shard_map/last/pallas_call | solution.py:208
  (6 shorter events, 0.2 us)
Async XLA Ops:
  0.0 1.8 %copy-start = (f32[12,2,128,128]{3,2,1,0:T(8,128)S(1)}, f32[12,2,128,128]{3,2,1,0:T(8,128)}, u32[]{:S(2)}) copy-start(f32[12,2,128,128]{3,2,1,0:T(8,128)} %orb_ref.1) | copy-start | bytes 4718596
  1.2 5.6 %collective-permute-start = (f32[2,2,128,128]{3,2,1,0:T(8,128)S(1)}, f32[2,2,128,128]{3,2,1,0:T(8,128)S(1)}, u32[]{:S(2)}, u32[]{:S(2)}) collective-permute-start(f32[2,2,128,128]{3,2,1,0:T(8,128)S(1)} %constant_dynamic-slice_fusion.2.refs_0_), channel_id=1, source_target_pairs={{0,16},{16,0},{1,17},{17,1},{2,18},{18,2},{3,19},{19,3},{4,20},{20... | collective-permute-start | bytes 786440 | tf_op jit(solution)/shard_map/band_swap/ppermute | solution.py:236
  1.8 13.5 %copy-start.1 = (f32[24]{0:T(128)S(1)}, f32[24]{0:T(128)}, u32[]{:S(2)}) copy-start(f32[24]{0:T(128)} %occ_ref.3) | copy-start | bytes 292
  1.9 11.3 %collective-permute-start.1 = (f32[5,128,128]{2,1,0:T(8,128)S(1)}, f32[5,128,128]{2,1,0:T(8,128)S(1)}, u32[]{:S(2)}, u32[]{:S(2)}) collective-permute-start(f32[5,128,128]{2,1,0:T(8,128)S(1)} %get-tuple-element.26), channel_id=1, source_target_pairs={{0,1},{1,0},{2,3},{3,2},{4,5},{5,4},{6,7},{7,6},{8,9},{9,8},{10,11... | collective-permute-start | bytes 983048 | tf_op jit(solution)/shard_map/hop1_part0/ppermute | solution.py:266
  4.7 14.1 %collective-permute-start.2 = (f32[4,128,128]{2,1,0:T(8,128)S(1)}, f32[4,128,128]{2,1,0:T(8,128)S(1)}, u32[]{:S(2)}, u32[]{:S(2)}) collective-permute-start(f32[4,128,128]{2,1,0:T(8,128)S(1)} %slice.33), channel_id=1, source_target_pairs={{0,1},{1,0},{2,3},{3,2},{4,5},{5,4},{6,7},{7,6},{8,9},{9,8},{10,11... | collective-permute-start | bytes 786440 | tf_op jit(solution)/shard_map/hop1_part1/ppermute | solution.py:266
  4.8 21.0 %collective-permute-start.11 = (f32[5,128,128]{2,1,0:T(8,128)S(1)}, f32[5,128,128]{2,1,0:T(8,128)S(1)}, u32[]{:S(2)}, u32[]{:S(2)}) collective-permute-start(f32[5,128,128]{2,1,0:T(8,128)S(1)} %get-tuple-element.23), channel_id=1, source_target_pairs={{0,1},{1,0},{2,3},{3,2},{4,5},{5,4},{6,7},{7,6},{8,9},{9,8},{10,11... | collective-permute-start | bytes 983048 | tf_op jit(solution)/shard_map/hop1_part2/ppermute | solution.py:266
  6.8 26.0 %collective-permute-start.9 = (f32[5,128,128]{2,1,0:T(8,128)S(1)}, f32[5,128,128]{2,1,0:T(8,128)S(1)}, u32[]{:S(2)}, u32[]{:S(2)}) collective-permute-start(f32[5,128,128]{2,1,0:T(8,128)S(1)} %get-tuple-element.24), channel_id=1, source_target_pairs={{0,1},{1,0},{2,3},{3,2},{4,5},{5,4},{6,7},{7,6},{8,9},{9,8},{10,11... | collective-permute-start | bytes 983048 | tf_op jit(solution)/shard_map/hop1_part3/ppermute | solution.py:266
  6.9 32.6 %collective-permute-start.7 = (f32[5,128,128]{2,1,0:T(8,128)S(1)}, f32[5,128,128]{2,1,0:T(8,128)S(1)}, u32[]{:S(2)}, u32[]{:S(2)}) collective-permute-start(f32[5,128,128]{2,1,0:T(8,128)S(1)} %get-tuple-element.25), channel_id=1, source_target_pairs={{0,1},{1,0},{2,3},{3,2},{4,5},{5,4},{6,7},{7,6},{8,9},{9,8},{10,11... | collective-permute-start | bytes 983048 | tf_op jit(solution)/shard_map/hop1_part4/ppermute | solution.py:266
  13.1 28.2 %collective-permute-start.3 = (f32[5,128,128]{2,1,0:T(8,128)S(1)}, f32[5,128,128]{2,1,0:T(8,128)S(1)}, u32[]{:S(2)}, u32[]{:S(2)}) collective-permute-start(f32[5,128,128]{2,1,0:T(8,128)S(1)} %collective-permute-done.1.refs_2_), channel_id=1, source_target_pairs={{0,2},{1,15},{2,4},{3,1},{4,6},{5,3},{6,8},{7,5},{8,10},{9,7},{10,... | collective-permute-start | bytes 983048 | tf_op jit(solution)/shard_map/hop2_part0/ppermute | solution.py:295
  18.8 22.5 %collective-permute-start.4 = (f32[4,128,128]{2,1,0:T(8,128)S(1)}, f32[4,128,128]{2,1,0:T(8,128)S(1)}, u32[]{:S(2)}, u32[]{:S(2)}) collective-permute-start(f32[4,128,128]{2,1,0:T(8,128)S(1)} %collective-permute-done.2.refs_4_), channel_id=1, source_target_pairs={{0,2},{1,15},{2,4},{3,1},{4,6},{5,3},{6,8},{7,5},{8,10},{9,7},{10,... | collective-permute-start | bytes 786440 | tf_op jit(solution)/shard_map/hop2_part1/ppermute | solution.py:295
  25.8 18.6 %collective-permute-start.12 = (f32[5,128,128]{2,1,0:T(8,128)S(1)}, f32[5,128,128]{2,1,0:T(8,128)S(1)}, u32[]{:S(2)}, u32[]{:S(2)}) collective-permute-start(f32[5,128,128]{2,1,0:T(8,128)S(1)} %collective-permute-done.11.refs_6_), channel_id=1, source_target_pairs={{0,2},{1,15},{2,4},{3,1},{4,6},{5,3},{6,8},{7,5},{8,10},{9,7},{10,... | collective-permute-start | bytes 983048 | tf_op jit(solution)/shard_map/hop2_part2/ppermute | solution.py:295
  32.8 14.3 %collective-permute-start.10 = (f32[5,128,128]{2,1,0:T(8,128)S(1)}, f32[5,128,128]{2,1,0:T(8,128)S(1)}, u32[]{:S(2)}, u32[]{:S(2)}) collective-permute-start(f32[5,128,128]{2,1,0:T(8,128)S(1)} %collective-permute-done.9.refs_2_), channel_id=1, source_target_pairs={{0,2},{1,15},{2,4},{3,1},{4,6},{5,3},{6,8},{7,5},{8,10},{9,7},{10,... | collective-permute-start | bytes 983048 | tf_op jit(solution)/shard_map/hop2_part3/ppermute | solution.py:295
  39.5 9.4 %collective-permute-start.8 = (f32[5,128,128]{2,1,0:T(8,128)S(1)}, f32[5,128,128]{2,1,0:T(8,128)S(1)}, u32[]{:S(2)}, u32[]{:S(2)}) collective-permute-start(f32[5,128,128]{2,1,0:T(8,128)S(1)} %collective-permute-done.7.refs_3_), channel_id=1, source_target_pairs={{0,2},{1,0},{2,4},{3,1},{4,6},{5,3},{6,8},{7,5},{8,10},{9,7},{10,1... | collective-permute-start | bytes 983048 | tf_op jit(solution)/shard_map/hop2_part4/ppermute | solution.py:295
  41.4 1.6 %collective-permute-start.6 = (f32[2,2,128,128]{3,2,1,0:T(8,128)S(1)}, f32[2,2,128,128]{3,2,1,0:T(8,128)S(1)}, u32[]{:S(2)}, u32[]{:S(2)}) collective-permute-start(f32[2,2,128,128]{3,2,1,0:T(8,128)S(1)} %constant_dynamic-slice_fusion.refs_3_), channel_id=1, source_target_pairs={{0,16},{16,0},{1,17},{17,1},{2,18},{18,2},{3,19},{19,3},{4,20},{20... | collective-permute-start | bytes 786440 | tf_op jit(solution)/shard_map/band_swap/ppermute | solution.py:236
  41.5 1.9 %collective-permute-start.5 = (f32[2,2,128,128]{3,2,1,0:T(8,128)S(1)}, f32[2,2,128,128]{3,2,1,0:T(8,128)S(1)}, u32[]{:S(2)}, u32[]{:S(2)}) collective-permute-start(f32[2,2,128,128]{3,2,1,0:T(8,128)S(1)} %constant_dynamic-slice_fusion.1.refs_2_), channel_id=1, source_target_pairs={{0,16},{16,0},{1,17},{17,1},{2,18},{18,2},{3,19},{19,3},{4,20},{20... | collective-permute-start | bytes 786440 | tf_op jit(solution)/shard_map/band_swap/ppermute | solution.py:236

commit v3 on v2

v3 whole, which is shorter than its diff:
```python
import functools

import jax
import jax.numpy as jnp
from jax import lax
from jax.experimental import pallas as pl
from jax.experimental.pallas import tpu as pltpu
from jax.sharding import PartitionSpec as P

BLOCK = 2
STEPS = 2
PLANES = 2
CHUNKS = (4, 6, 6, 4, 4)
GROUPS = (3, 5)

ONE = 1.0 / 36.0
TWO = 1.0 / 216.0
CROSS = 2.0 / 216.0

OWN = [(0, 0), (1, 0), (-1, 0), (2, 0), (-2, 0), (0, 1), (1, 1), (-1, 1), (0, -1), (1, -1), (-1, -1), (0, 2), (0, -2)]
BESIDE = [(0, 0), (1, 0), (-1, 0), (0, 1), (0, -1)]
BEYOND, ACROSS = len(BESIDE), len(BESIDE) + 1


def shifted(field, dy, dz):
    rows, columns = field.shape
    if dy:
        field = pltpu.roll(field, (-dy) % rows, 0)
    if dz:
        field = pltpu.roll(field, (-dz) % columns, 1)
    return field


def inside(shape, dy, dz):
    y = lax.broadcasted_iota(jnp.int32, shape, 0) + dy
    z = lax.broadcasted_iota(jnp.int32, shape, 1) - dz
    return (y >= 0) & (y < shape[0]) & (z >= 0) & (z < shape[1])


def pair_weight(here, there, dy, dz, scale):
    total = None
    for h, t in zip(here, there):
        term = shifted(h, 0, -dz) * shifted(t, dy, 0)
        total = term if total is None else total + term
    total = total * (-scale)
    if dy or dz:
        total = jnp.where(inside(total.shape, dy, dz), total, 0.0)
    return total


def scale_of(dy, dz, dx):
    length = abs(dx) + abs(dy) + abs(dz)
    if length == 1:
        return ONE
    return TWO if max(abs(dx), abs(dy), abs(dz)) == 2 else CROSS


def block_weights(occ_ref, orb_count):
    groups = lax.axis_size("band")
    out = []
    for step in range(STEPS):
        s = lax.rem(lax.axis_index("band") + step, STEPS) if groups == STEPS else step
        first = s * (groups // STEPS) * orb_count + s * BLOCK
        out += [occ_ref[first + i] for i in range(BLOCK)]
    return out


def cut_kernel(starts, orb_ref, *refs):
    part_refs, sems = refs[:-1], refs[-1]
    flat = orb_ref.reshape(-1, *orb_ref.shape[2:])
    copies = [
        pltpu.make_async_copy(flat.at[pl.ds(start, part.shape[0])], part, sems.at[i])
        for i, (start, part) in enumerate(zip(starts, part_refs))
    ]
    for copy in copies:
        copy.start()
    for copy in copies:
        copy.wait()


def local_weight_kernel(orb_count, occ_ref, *refs):
    block_refs, k_ref = refs[:STEPS], refs[STEPS]
    rows, columns = k_ref.shape[2:]
    weights = block_weights(occ_ref, orb_count)
    dom, slabs = lax.axis_index("dom"), lax.axis_size("dom")
    for p in range(PLANES):
        here = [r[i, p] for r in block_refs for i in range(BLOCK)]
        there = [r[i, 1 - p] for r in block_refs for i in range(BLOCK)]
        weighted = [w * h for w, h in zip(weights, here)]
        outer = jnp.where(dom == (0 if p == 0 else slabs - 1), 0.0, 1.0)
        y = lax.broadcasted_iota(jnp.int32, (rows, columns), 0)
        z = lax.broadcasted_iota(jnp.int32, (rows, columns), 1)
        edges = (y > 0).astype(jnp.float32) + (y < rows - 1).astype(jnp.float32)
        edges = edges + (z > 0).astype(jnp.float32) + (z < columns - 1).astype(jnp.float32)
        centre = 1.0 / 6.0 + (edges + (1.0 + outer)) * TWO
        for k, (dy, dz) in enumerate(OWN):
            if k == 0:
                k_ref[p, k] = pair_weight(weighted, here, 0, 0, 1.0) * centre
            else:
                k_ref[p, k] = pair_weight(weighted, here, dy, dz, scale_of(dy, dz, 0))
        for k, (dy, dz) in enumerate(BESIDE):
            k_ref[p, len(OWN) + k] = pair_weight(weighted, there, dy, dz, scale_of(dy, dz, 1))


def local_kernel(k_ref, orb_ref, *acc_refs):
    base = 0
    for acc_ref in acc_refs:

        @pl.loop(0, acc_ref.shape[0])
        def _(j, acc_ref=acc_ref, base=base):
            for p in range(PLANES):
                groups = {}
                for plane, terms, first in ((p, OWN, 0), (1 - p, BESIDE, len(OWN))):
                    field = orb_ref[base + j, plane]
                    for k, (dy, dz) in enumerate(terms):
                        term = k_ref[p, first + k] * shifted(field, dy, 0)
                        groups[dz] = groups[dz] + term if dz in groups else term
                out = groups[0]
                for dz in (1, -1, 2, -2):
                    out = out + shifted(groups[dz], 0, dz)
                acc_ref[j, p] = out

        base += acc_ref.shape[0]


def nearest():
    odd = lax.rem(lax.axis_index("dom"), 2)
    return odd, 1 - odd


def halo_weight_kernel(hop, orb_count, occ_ref, *refs):
    n = STEPS
    local, slabs, k_ref = refs[:n], refs[n : 2 * n], refs[2 * n]
    weights = block_weights(occ_ref, orb_count)
    near = nearest()[hop]
    far = 1 - near
    pairs = [(r, i) for r in local for i in range(BLOCK)]
    here = [w * r[i, far] for w, (r, i) in zip(weights, pairs)]
    behind = [w * r[i, near] for w, (r, i) in zip(weights, pairs)]
    there = [r[i, near] for r in slabs for i in range(BLOCK)]
    beyond = [r[i, far] for r in slabs for i in range(BLOCK)]
    for k, (dy, dz) in enumerate(BESIDE):
        k_ref[k] = pair_weight(here, there, dy, dz, scale_of(dy, dz, 1))
    k_ref[BEYOND] = pair_weight(here, beyond, 0, 0, TWO)
    k_ref[ACROSS] = pair_weight(behind, there, 0, 0, TWO)


def side_terms(k_ref, near_plane, far_plane):
    groups = {}
    for k, (dy, dz) in enumerate(BESIDE):
        term = k_ref[k] * shifted(near_plane, dy, 0)
        groups[dz] = groups[dz] + term if dz in groups else term
    beside = groups[0] + shifted(groups[1], 0, 1) + shifted(groups[-1], 0, -1)
    return beside + k_ref[BEYOND] * far_plane, k_ref[ACROSS] * near_plane


def finish_kernel(origin, chained, *refs):
    k_refs, acc_ref, refs = refs[:2], refs[2], refs[3:]
    sum_ref, sems = refs[-2:]
    out_ref = refs[-3]
    chunk_refs = refs[: -3 - chained]
    half = len(chunk_refs) // 2
    odd = nearest()[0]
    even = 1 - odd
    base = 0
    for first_ref, second_ref in zip(chunk_refs[:half], chunk_refs[half:]):
        size = first_ref.shape[0] // PLANES

        @pl.loop(0, size, unroll=size)
        def _(i, first_ref=first_ref, second_ref=second_ref, base=base):
            j, at = base + i, PLANES * i
            to_even, to_odd = side_terms(k_refs[0], first_ref[at + odd], first_ref[at + even])
            more_odd, more_even = side_terms(k_refs[1], second_ref[at + even], second_ref[at + odd])
            sum_ref[j, even] = acc_ref[j, even] + (to_even + more_even)
            sum_ref[j, odd] = acc_ref[j, odd] + (to_odd + more_odd)
            pltpu.make_async_copy(sum_ref.at[j], out_ref.at[origin + j], sems.at[j]).start()

        base += size
    for j in range(base):
        pltpu.make_async_copy(sum_ref.at[j], out_ref.at[origin + j], sems.at[j]).wait()


VMEM = pl.BlockSpec(memory_space=pltpu.VMEM)
SMEM = pl.BlockSpec(memory_space=pltpu.SMEM)
ANY = pl.BlockSpec(memory_space=pl.ANY)
PARAMS = pltpu.CompilerParams(vmem_limit_bytes=16 * 1024 * 1024)


def finish(name, origin, weights, acc, chunks, out, shape):
    chained = out is not None
    return pl.pallas_call(
        functools.partial(finish_kernel, origin, chained),
        out_shape=jax.ShapeDtypeStruct(shape, jnp.float32),
        in_specs=[VMEM] * (3 + len(chunks)) + [ANY] * chained,
        out_specs=ANY,
        input_output_aliases={3 + len(chunks): 0} if chained else {},
        scratch_shapes=[pltpu.VMEM(acc.shape, jnp.float32), pltpu.SemaphoreType.DMA((acc.shape[0],))],
        compiler_params=PARAMS,
        cost_estimate=pl.CostEstimate(flops=1, bytes_accessed=1, transcendentals=0),
        name=name,
    )(*weights, acc, *chunks, *([out] if chained else []))


def hops(slabs):
    swap = [(i, i ^ 1) for i in range(slabs)]
    onward = [(i, i + 2 if i % 2 == 0 else i - 2) for i in range(slabs)]
    onward = [(a, b) for a, b in onward if 0 <= b < slabs]
    back = [(b, a) for a, b in onward]
    return swap, onward, back


def everywhere(field, groups):
    band, axis = lax.axis_index("band"), field.ndim - 4
    if groups == STEPS:
        own = lax.dynamic_slice_in_dim(field, band * BLOCK, BLOCK, axis)
        return [own] + [
            lax.ppermute(own, "band", [(i, (i - step) % STEPS) for i in range(STEPS)]) for step in range(1, STEPS)
        ]
    out = []
    for step in range(STEPS):
        mine = lax.slice_in_dim(field, step * BLOCK, (step + 1) * BLOCK, axis=axis)
        mine = jnp.where(band == step * (groups // STEPS), mine, jnp.zeros_like(mine))
        out.append(lax.psum(mine, "band"))
    return out


def after(value, *others):
    return lax.optimization_barrier((value, *others))[0]


def per_device(orbitals, occupations):
    orb_count, planes, rows, columns = orbitals.shape
    groups, slabs = lax.axis_size("band"), lax.axis_size("dom")
    assert planes == PLANES and slabs % 2 == 0 and slabs > 2 and sum(CHUNKS) == orb_count * planes
    swap, onward, back = hops(slabs)
    n = len(CHUNKS)
    starts = [sum(CHUNKS[:i]) for i in range(n)]
    assert all(n % planes == 0 for n in CHUNKS)
    cuts = [0] + [sum(CHUNKS[:upto]) // planes for upto in GROUPS]
    f32 = lambda *shape: jax.ShapeDtypeStruct(shape, jnp.float32)

    sent = pl.pallas_call(
        functools.partial(cut_kernel, starts),
        out_shape=[f32(size, rows, columns) for size in CHUNKS],
        in_specs=[ANY],
        out_specs=[VMEM] * n,
        scratch_shapes=[pltpu.SemaphoreType.DMA((n,))],
        compiler_params=PARAMS,
        name="cut",
    )(orbitals)
    around = lax.ppermute(sent[-1], "dom", back)
    first = [lax.ppermute(part, "dom", swap) for part in sent]
    local = everywhere(orbitals[: STEPS * BLOCK], groups)
    k_local = pl.pallas_call(
        functools.partial(local_weight_kernel, orb_count),
        out_shape=f32(planes, len(OWN) + len(BESIDE), rows, columns),
        in_specs=[SMEM] + [VMEM] * STEPS,
        out_specs=VMEM,
        compiler_params=PARAMS,
        cost_estimate=pl.CostEstimate(flops=1, bytes_accessed=1, transcendentals=0),
        name="local_weights",
    )(occupations, *local)
    acc = pl.pallas_call(
        local_kernel,
        out_shape=[f32(b - a, planes, rows, columns) for a, b in zip(cuts, cuts[1:])],
        in_specs=[VMEM] * 2,
        out_specs=[VMEM] * len(GROUPS),
        compiler_params=PARAMS,
        cost_estimate=pl.CostEstimate(flops=1, bytes_accessed=1, transcendentals=0),
        name="local",
    )(k_local, orbitals)

    count = 0
    while sum(CHUNKS[:count]) < STEPS * BLOCK * planes:
        count += 1

    def halo_weights(name, parts):
        blocks = jnp.concatenate(parts[:count])[: STEPS * BLOCK * planes]
        blocks = everywhere(blocks.reshape(-1, planes, rows, columns), groups)
        return pl.pallas_call(
            functools.partial(halo_weight_kernel, name == "second", orb_count),
            out_shape=f32(ACROSS + 1, rows, columns),
            in_specs=[SMEM] + [VMEM] * (2 * STEPS),
            out_specs=VMEM,
            compiler_params=PARAMS,
            cost_estimate=pl.CostEstimate(flops=1, bytes_accessed=1, transcendentals=0),
            name=name + "_hop_weights",
        )(occupations, *local, *blocks)

    k_first = halo_weights("first", first)
    before = {0: around, 1: k_local, 2: k_first}
    second = [
        lax.ppermute(after(part, before[i]) if i in before else part, "dom", onward) for i, part in enumerate(first[:-1])
    ]
    second.append(lax.ppermute(around, "dom", swap))
    k_halo = [k_first, halo_weights("second", second)]
    acc = [after(acc[0], first[-1]), *acc[1:]]

    out, begin = None, 0
    for g, upto in enumerate(GROUPS):
        chunks = first[begin:upto] + second[begin:upto]
        out = finish(f"finish_{g}", cuts[g], k_halo, acc[g], chunks, out, orbitals.shape)
        begin = upto
    return out


def solution(mesh):
    in_specs = (P("band", "dom", None, None), P())
    out_specs = P("band", "dom", None, None)
    return jax.shard_map(
        per_device, mesh=mesh, in_specs=in_specs, out_specs=out_specs, check_vma=False
    )
```

time: 50.1 us -> 46.6 us (0.930)
  waiting for transfers between devices: 18.8 us -> 7.85 us
  starting transfers between devices: 18.2 us -> 26.8 us
  Pallas kernels: 11.4 us -> 9.53 us
    ppermute x10 -> x11, waiting for transfers between devices: 17.5 us -> 7.85 us  [the longest x5 6.6 us: per_device(): first = [lax.ppermute(part, 'dom', swap) for part in sent]]
    ppermute x10 -> x11, starting transfers between devices: 17 us -> 26.6 us  [the longest x4 15.9 us: per_device(): lax.ppermute(after(part, before[i]) if i in before else part, 'dom', onward)]
    pallas_call x4 -> x5, Pallas kernels: 6.53 us -> 4.73 us  [the longest x2 2.66 us: finish(): pl.pallas_call(functools.partial(finish_kernel, origin, chained), out_sha...]
    unnamed x4 -> x6, local copies, waits for them, and re-layouts: 0.01 us -> 1.42 us
    ppermute x3, waiting for transfers between devices: 1.32 us -> 0.01 us  [everywhere(): lax.ppermute(own, 'band', [(i, (i - step) % STEPS) for i in range(STEPS)])]
    slice x1 -> x2, local copies, waits for them, and re-layouts: 1.2 us -> 0.01 us  [per_device(): local = everywhere(orbitals[:STEPS * BLOCK], groups)]
    ppermute x3, starting transfers between devices: 1.14 us -> 0.21 us  [everywhere(): lax.ppermute(own, 'band', [(i, (i - step) % STEPS) for i in range(STEPS)])]
  transfers between devices with their start and end apart: 13 -> 14, of which waited for: 8 -> 6; matrix products, arithmetic and copies ran while one was open for 0% -> 0% of each run, Pallas kernels for 20% -> 17%
where the time goes in v3:
time: 46.6 us; the launch traced here: 46 us
  starting transfers between devices  26.8 us (58%)
  Pallas kernels  9.53 us (20%)
  waiting for transfers between devices  7.85 us (17%)
  local copies, waits for them, and re-layouts  1.49 us (3%)
    ppermute x4, starting transfers between devices, per_device(): lax.ppermute(after(part, before[i]) if i in before else part, 'dom', onward)  15.9 us
    ppermute x5, starting transfers between devices, per_device(): first = [lax.ppermute(part, 'dom', swap) for part in sent]  9.38 us
    ppermute x5, waiting for transfers between devices, per_device(): first = [lax.ppermute(part, 'dom', swap) for part in sent]  6.6 us
    pallas_call x1, Pallas kernels, per_device(): pl.pallas_call(local_kernel, out_shape=[f32(b - a, planes, rows, columns)...  3.07 us
    pallas_call x2, Pallas kernels, finish(): pl.pallas_call(functools.partial(finish_kernel, origin, chained), out_sha...  2.66 us
    pallas_call x1, Pallas kernels, per_device(): pl.pallas_call(functools.partial(local_weight_kernel, orb_count), out_sha...  1.72 us
    pallas_call x2, Pallas kernels, halo_weights(): pl.pallas_call(functools.partial(halo_weight_kernel, name == 'second', or...  1.6 us
    unnamed x6, local copies, waits for them, and re-layouts  1.42 us
  transfers between devices with their start and end apart: 14, of which 6 were waited for; matrix products, arithmetic and copies ran while one was open for 0% of the time, Pallas kernels for 17%

profile of v3, /device:TPU:0, one launch (start us, length us, event | category | flops | bytes accessed | tf_op | source)
XLA Modules:
  0.0 46.0 jit_solution(14279686878234219835)
XLA Ops:
  0.0 0.0 copy-start
  0.0 1.4 %copy-done = f32[12,2,128,128]{3,2,1,0:T(8,128)S(1)} copy-done((f32[12,2,128,128]{3,2,1,0:T(8,128)S(1)}, f32[12,2,128,128]{3,2,1,0:T(8,128)}, u32[]{:S(2)}) %copy-start) | copy-done | bytes 1572888
  1.4 0.0 slice-start
  1.4 0.0 copy-start.2
  1.4 0.5 %cut.1 = (f32[4,128,128]{2,1,0:T(8,128)S(1)}, f32[6,128,128]{2,1,0:T(8,128)S(1)}, f32[6,128,128]{2,1,0:T(8,128)S(1)}, f32[4,128,128]{2,1,0:T(8,128)S(1)}, f32[4,128,128]{2,1,0:T(8,128)S(1)}) custom-call(f32[12,2,128,128]{3,2,1,0:T(8,128)S(1)} %copy-done), custom_call_target="tpu_custom_call" | custom-call | tf_op jit(solution)/shard_map/cut/pallas_call | solution.py:242
  1.9 3.0 %collective-permute-start.2 = (f32[6,128,128]{2,1,0:T(8,128)S(1)}, f32[6,128,128]{2,1,0:T(8,128)S(1)}, u32[]{:S(2)}, u32[]{:S(2)}) collective-permute-start(f32[6,128,128]{2,1,0:T(8,128)S(1)} %get-tuple-element.17), channel_id=1, source_target_pairs={{0,1},{1,0},{2,3},{3,2},{4,5},{5,4},{6,7},{7,6},{8,9},{9,8},{10,11... | collective-permute-start | bytes 1179656 | tf_op jit(solution)/shard_map/ppermute | solution.py:252
  4.9 0.0 slice-done
  4.9 0.1 collective-permute-start
  5.0 0.6 %collective-permute-start.1 = (f32[4,128,128]{2,1,0:T(8,128)S(1)}, f32[4,128,128]{2,1,0:T(8,128)S(1)}, u32[]{:S(2)}, u32[]{:S(2)}) collective-permute-start(f32[4,128,128]{2,1,0:T(8,128)S(1)} %get-tuple-element.16), channel_id=1, source_target_pairs={{0,1},{1,0},{2,3},{3,2},{4,5},{5,4},{6,7},{7,6},{8,9},{9,8},{10,11... | collective-permute-start | bytes 786440 | tf_op jit(solution)/shard_map/ppermute | solution.py:252
  5.6 1.3 %collective-permute-start.4 = (f32[4,128,128]{2,1,0:T(8,128)S(1)}, f32[4,128,128]{2,1,0:T(8,128)S(1)}, u32[]{:S(2)}, u32[]{:S(2)}) collective-permute-start(f32[4,128,128]{2,1,0:T(8,128)S(1)} %get-tuple-element.18), channel_id=1, source_target_pairs={{2,0},{4,2},{1,3},{6,4},{3,5},{8,6},{5,7},{10,8},{7,9},{12,10},{9,... | collective-permute-start | bytes 786440 | tf_op jit(solution)/shard_map/ppermute | solution.py:251
  6.8 3.8 %collective-permute-start.12 = (f32[6,128,128]{2,1,0:T(8,128)S(1)}, f32[6,128,128]{2,1,0:T(8,128)S(1)}, u32[]{:S(2)}, u32[]{:S(2)}) collective-permute-start(f32[6,128,128]{2,1,0:T(8,128)S(1)} %get-tuple-element.25), channel_id=1, source_target_pairs={{0,1},{1,0},{2,3},{3,2},{4,5},{5,4},{6,7},{7,6},{8,9},{9,8},{10,11... | collective-permute-start | bytes 1179656 | tf_op jit(solution)/shard_map/ppermute | solution.py:252
  10.6 0.0 collective-permute-done.refs_1_
  10.6 0.0 copy-done.2
  10.6 1.7 %local_weights.1.k_ref = f32[2,18,128,128]{3,2,1,0:T(8,128)S(1)} custom-call(f32[24]{0:T(128)S(1)} %copy-done.2, f32[2,2,128,128]{3,2,1,0:T(8,128)S(1)} %constant_dynamic-slice_fusion.2.refs_0_, f32[2,2,128,128]{3,2,1,0:T(8,128)S(1)} %collective-permute-done.refs_1_), custom_call_target="tpu_custom_call" | custom-call | flops 1 | bytes 1 | tf_op jit(solution)/shard_map/local_weights/pallas_call | solution.py:254
  12.3 2.5 %collective-permute-done.2.refs_4_ = f32[6,128,128]{2,1,0:T(8,128)S(1)} collective-permute-done((f32[6,128,128]{2,1,0:T(8,128)S(1)}, f32[6,128,128]{2,1,0:T(8,128)S(1)}, u32[]{:S(2)}, u32[]{:S(2)}) %collective-permute-start.2) | collective-permute-done | bytes 393248 | tf_op jit(solution)/shard_map/ppermute | solution.py:252
  14.8 4.0 %collective-permute-start.6 = (f32[6,128,128]{2,1,0:T(8,128)S(1)}, f32[6,128,128]{2,1,0:T(8,128)S(1)}, u32[]{:S(2)}, u32[]{:S(2)}) collective-permute-start(f32[6,128,128]{2,1,0:T(8,128)S(1)} %collective-permute-done.2.refs_4_), channel_id=1, source_target_pairs={{0,2},{2,4},{3,1},{4,6},{5,3},{6,8},{7,5},{8,10},{9,7},{10,12},{11... | collective-permute-start | bytes 1179656 | tf_op jit(solution)/shard_map/ppermute | solution.py:293
  18.9 1.6 %collective-permute-done.1.refs_3_ = f32[4,128,128]{2,1,0:T(8,128)S(1)} collective-permute-done((f32[4,128,128]{2,1,0:T(8,128)S(1)}, f32[4,128,128]{2,1,0:T(8,128)S(1)}, u32[]{:S(2)}, u32[]{:S(2)}) %collective-permute-start.1) | collective-permute-done | bytes 262176 | tf_op jit(solution)/shard_map/ppermute | solution.py:252
  20.5 0.1 collective-permute-start.3
  20.6 0.0 collective-permute-done.4
  20.6 4.0 %collective-permute-start.5 = (f32[4,128,128]{2,1,0:T(8,128)S(1)}, f32[4,128,128]{2,1,0:T(8,128)S(1)}, u32[]{:S(2)}, u32[]{:S(2)}) collective-permute-start(f32[4,128,128]{2,1,0:T(8,128)S(1)} %collective-permute-done.1.refs_3_), channel_id=1, source_target_pairs={{0,2},{2,4},{3,1},{4,6},{5,3},{6,8},{7,5},{8,10},{9,7},{10,12},{11... | collective-permute-start | bytes 786440 | tf_op jit(solution)/shard_map/ppermute | solution.py:293
  24.6 0.0 copy-start.1
  24.7 0.1 collective-permute-start.8
  24.7 0.0 collective-permute-done.3.refs_3_
  24.7 2.0 %collective-permute-start.9 = (f32[4,128,128]{2,1,0:T(8,128)S(1)}, f32[4,128,128]{2,1,0:T(8,128)S(1)}, u32[]{:S(2)}, u32[]{:S(2)}) collective-permute-start(f32[4,128,128]{2,1,0:T(8,128)S(1)} %get-tuple-element.18), channel_id=1, source_target_pairs={{0,1},{1,0},{2,3},{3,2},{4,5},{5,4},{6,7},{7,6},{8,9},{9,8},{10,11... | collective-permute-start | bytes 786440 | tf_op jit(solution)/shard_map/ppermute | solution.py:252
  26.7 0.8 %first_hop_weights.1.refs_0_ = f32[7,128,128]{2,1,0:T(8,128)S(1)} custom-call(f32[24]{0:T(128)S(1)} %copy-done.2, f32[2,2,128,128]{3,2,1,0:T(8,128)S(1)} %constant_dynamic-slice_fusion.2.refs_0_, f32[2,2,128,128]{3,2,1,0:T(8,128)S(1)} %collective-permute-done.refs_1_, f32[2,2,128,128]{3,2,1,0:T(8,128)S(1)} %constant_dynamic-slice_fusion.1.refs_2_, ...), custom_call_target="tpu_custom_call" | custom-call | flops 1 | bytes 1 | tf_op jit(solution)/shard_map/first_hop_weights/pallas_call | solution.py:280
  27.5 1.0 %collective-permute-done.12.refs_5_ = f32[6,128,128]{2,1,0:T(8,128)S(1)} collective-permute-done((f32[6,128,128]{2,1,0:T(8,128)S(1)}, f32[6,128,128]{2,1,0:T(8,128)S(1)}, u32[]{:S(2)}, u32[]{:S(2)}) %collective-permute-start.12) | collective-permute-done | bytes 393248 | tf_op jit(solution)/shard_map/ppermute | solution.py:252
  28.5 3.9 %collective-permute-start.13 = (f32[6,128,128]{2,1,0:T(8,128)S(1)}, f32[6,128,128]{2,1,0:T(8,128)S(1)}, u32[]{:S(2)}, u32[]{:S(2)}) collective-permute-start(f32[6,128,128]{2,1,0:T(8,128)S(1)} %collective-permute-done.12.refs_5_), channel_id=1, source_target_pairs={{0,2},{2,4},{3,1},{4,6},{5,3},{6,8},{7,5},{8,10},{9,7},{10,12},{11... | collective-permute-start | bytes 1179656 | tf_op jit(solution)/shard_map/ppermute | solution.py:293
  32.5 0.0 collective-permute-done.5.refs_6_
  32.5 0.0 collective-permute-done.6.refs_7_
  32.6 0.1 collective-permute-start.7
  32.7 1.5 %collective-permute-done.8.refs_3_ = f32[4,128,128]{2,1,0:T(8,128)S(1)} collective-permute-done((f32[4,128,128]{2,1,0:T(8,128)S(1)}, f32[4,128,128]{2,1,0:T(8,128)S(1)}, u32[]{:S(2)}, u32[]{:S(2)}) %collective-permute-start.8) | collective-permute-done | bytes 262176 | tf_op jit(solution)/shard_map/ppermute | solution.py:252
  34.2 3.9 %collective-permute-start.10 = (f32[4,128,128]{2,1,0:T(8,128)S(1)}, f32[4,128,128]{2,1,0:T(8,128)S(1)}, u32[]{:S(2)}, u32[]{:S(2)}) collective-permute-start(f32[4,128,128]{2,1,0:T(8,128)S(1)} %collective-permute-done.8.refs_3_), channel_id=1, source_target_pairs={{0,2},{2,4},{3,1},{4,6},{5,3},{6,8},{7,5},{8,10},{9,7},{10,12},{11... | collective-permute-start | bytes 786440 | tf_op jit(solution)/shard_map/ppermute | solution.py:293
  38.1 0.1 collective-permute-start.11
  38.2 0.0 copy-done.1
  38.2 3.1 %local.1 = (f32[8,2,128,128]{3,2,1,0:T(8,128)S(1)}, f32[4,2,128,128]{3,2,1,0:T(8,128)S(1)}) custom-call(f32[2,18,128,128]{3,2,1,0:T(8,128)S(1)} %local_weights.1.k_ref, f32[12,2,128,128]{3,2,1,0:T(8,128)S(1)} %copy-done.1), custom_call_target="tpu_custom_call" | custom-call | flops 1 | bytes 1 | tf_op jit(solution)/shard_map/local/pallas_call | solution.py:263
  41.3 0.0 collective-permute-done.9.refs_4_
  41.3 0.0 collective-permute-done.7.refs_3_
  41.3 0.8 %second_hop_weights.1.refs_1_ = f32[7,128,128]{2,1,0:T(8,128)S(1)} custom-call(f32[24]{0:T(128)S(1)} %copy-done.2, f32[2,2,128,128]{3,2,1,0:T(8,128)S(1)} %constant_dynamic-slice_fusion.2.refs_0_, f32[2,2,128,128]{3,2,1,0:T(8,128)S(1)} %collective-permute-done.refs_1_, f32[2,2,128,128]{3,2,1,0:T(8,128)S(1)} %constant_dynamic-slice_fusion.refs_2_, ...), custom_call_target="tpu_custom_call" | custom-call | flops 1 | bytes 1 | tf_op jit(solution)/shard_map/second_hop_weights/pallas_call | solution.py:280
  42.1 0.0 collective-permute-done.13.refs_8_
  42.1 1.5 %finish_0.1.refs_7_ = f32[12,2,128,128]{3,2,1,0:T(8,128)} custom-call(f32[7,128,128]{2,1,0:T(8,128)S(1)} %first_hop_weights.1.refs_0_, f32[7,128,128]{2,1,0:T(8,128)S(1)} %second_hop_weights.1.refs_1_, f32[8,2,128,128]{3,2,1,0:T(8,128)S(1)} %get-tuple-element.24.refs_2_, f32[4,128,128]{2,1,0:T(8,128)S(1)} %collective-permute-done.1.refs_3_, ...), custom_call_target="tpu_custom_call" | custom-call | flops 1 | bytes 1 | tf_op jit(solution)/shard_map/finish_0/pallas_call | solution.py:191
  43.7 1.2 %collective-permute-done.10.refs_5_ = f32[4,128,128]{2,1,0:T(8,128)S(1)} collective-permute-done((f32[4,128,128]{2,1,0:T(8,128)S(1)}, f32[4,128,128]{2,1,0:T(8,128)S(1)}, u32[]{:S(2)}, u32[]{:S(2)}) %collective-permute-start.10) | collective-permute-done | bytes 262176 | tf_op jit(solution)/shard_map/ppermute | solution.py:293
  44.9 0.1 collective-permute-done.11.refs_6_
  44.9 1.1 %finish_1.1 = f32[12,2,128,128]{3,2,1,0:T(8,128)} custom-call(f32[7,128,128]{2,1,0:T(8,128)S(1)} %first_hop_weights.1.refs_0_, f32[7,128,128]{2,1,0:T(8,128)S(1)} %second_hop_weights.1.refs_1_, f32[4,2,128,128]{3,2,1,0:T(8,128)S(1)} %get-tuple-element.21.refs_2_, f32[4,128,128]{2,1,0:T(8,128)S(1)} %collective-permute-done.8.refs_3_, ...), custom_call_target="tpu_custom_call", output_to_operand_aliasing={{}: (7, {})} | custom-call | flops 1 | bytes 1 | tf_op jit(solution)/shard_map/finish_1/pallas_call | solution.py:191
  (5 shorter events, 0.1 us)
Async XLA Ops:
  0.0 1.4 %copy-start = (f32[12,2,128,128]{3,2,1,0:T(8,128)S(1)}, f32[12,2,128,128]{3,2,1,0:T(8,128)}, u32[]{:S(2)}) copy-start(f32[12,2,128,128]{3,2,1,0:T(8,128)} %orb_ref.3) | copy-start | bytes 4718596
  1.4 3.5 %slice-start = ((f32[12,2,128,128]{3,2,1,0:T(8,128)}), f32[4,2,128,128]{3,2,1,0:T(8,128)S(1)}, s32[]{:S(2)}) async-start(f32[12,2,128,128]{3,2,1,0:T(8,128)} %orb_ref.3), calls=%async_computation | async-start | bytes 1048576 | tf_op jit(solution)/shard_map/slice | solution.py:253
  1.4 9.2 %copy-start.2 = (f32[24]{0:T(128)S(1)}, f32[24]{0:T(128)}, u32[]{:S(2)}) copy-start(f32[24]{0:T(128)} %occ_ref.5) | copy-start | bytes 292
  1.9 12.9 %collective-permute-start.2 = (f32[6,128,128]{2,1,0:T(8,128)S(1)}, f32[6,128,128]{2,1,0:T(8,128)S(1)}, u32[]{:S(2)}, u32[]{:S(2)}) collective-permute-start(f32[6,128,128]{2,1,0:T(8,128)S(1)} %get-tuple-element.17), channel_id=1, source_target_pairs={{0,1},{1,0},{2,3},{3,2},{4,5},{5,4},{6,7},{7,6},{8,9},{9,8},{10,11... | collective-permute-start | bytes 1179656 | tf_op jit(solution)/shard_map/ppermute | solution.py:252
  4.9 5.7 %collective-permute-start = (f32[2,2,128,128]{3,2,1,0:T(8,128)S(1)}, f32[2,2,128,128]{3,2,1,0:T(8,128)S(1)}, u32[]{:S(2)}, u32[]{:S(2)}) collective-permute-start(f32[2,2,128,128]{3,2,1,0:T(8,128)S(1)} %constant_dynamic-slice_fusion.2.refs_0_), channel_id=1, source_target_pairs={{0,16},{16,0},{1,17},{17,1},{2,18},{18,2},{3,19},{19,3},{4,20},{20... | collective-permute-start | bytes 786440 | tf_op jit(solution)/shard_map/ppermute | solution.py:217
  5.0 15.5 %collective-permute-start.1 = (f32[4,128,128]{2,1,0:T(8,128)S(1)}, f32[4,128,128]{2,1,0:T(8,128)S(1)}, u32[]{:S(2)}, u32[]{:S(2)}) collective-permute-start(f32[4,128,128]{2,1,0:T(8,128)S(1)} %get-tuple-element.16), channel_id=1, source_target_pairs={{0,1},{1,0},{2,3},{3,2},{4,5},{5,4},{6,7},{7,6},{8,9},{9,8},{10,11... | collective-permute-start | bytes 786440 | tf_op jit(solution)/shard_map/ppermute | solution.py:252
  5.6 15.1 %collective-permute-start.4 = (f32[4,128,128]{2,1,0:T(8,128)S(1)}, f32[4,128,128]{2,1,0:T(8,128)S(1)}, u32[]{:S(2)}, u32[]{:S(2)}) collective-permute-start(f32[4,128,128]{2,1,0:T(8,128)S(1)} %get-tuple-element.18), channel_id=1, source_target_pairs={{2,0},{4,2},{1,3},{6,4},{3,5},{8,6},{5,7},{10,8},{7,9},{12,10},{9,... | collective-permute-start | bytes 786440 | tf_op jit(solution)/shard_map/ppermute | solution.py:251
  6.8 21.7 %collective-permute-start.12 = (f32[6,128,128]{2,1,0:T(8,128)S(1)}, f32[6,128,128]{2,1,0:T(8,128)S(1)}, u32[]{:S(2)}, u32[]{:S(2)}) collective-permute-start(f32[6,128,128]{2,1,0:T(8,128)S(1)} %get-tuple-element.25), channel_id=1, source_target_pairs={{0,1},{1,0},{2,3},{3,2},{4,5},{5,4},{6,7},{7,6},{8,9},{9,8},{10,11... | collective-permute-start | bytes 1179656 | tf_op jit(solution)/shard_map/ppermute | solution.py:252
  14.8 17.7 %collective-permute-start.6 = (f32[6,128,128]{2,1,0:T(8,128)S(1)}, f32[6,128,128]{2,1,0:T(8,128)S(1)}, u32[]{:S(2)}, u32[]{:S(2)}) collective-permute-start(f32[6,128,128]{2,1,0:T(8,128)S(1)} %collective-permute-done.2.refs_4_), channel_id=1, source_target_pairs={{0,2},{2,4},{3,1},{4,6},{5,3},{6,8},{7,5},{8,10},{9,7},{10,12},{11... | collective-permute-start | bytes 1179656 | tf_op jit(solution)/shard_map/ppermute | solution.py:293
  20.5 4.2 %collective-permute-start.3 = (f32[2,2,128,128]{3,2,1,0:T(8,128)S(1)}, f32[2,2,128,128]{3,2,1,0:T(8,128)S(1)}, u32[]{:S(2)}, u32[]{:S(2)}) collective-permute-start(f32[2,2,128,128]{3,2,1,0:T(8,128)S(1)} %constant_dynamic-slice_fusion.1.refs_2_), channel_id=1, source_target_pairs={{0,16},{16,0},{1,17},{17,1},{2,18},{18,2},{3,19},{19,3},{4,20},{20... | collective-permute-start | bytes 786440 | tf_op jit(solution)/shard_map/ppermute | solution.py:217
  20.6 11.9 %collective-permute-start.5 = (f32[4,128,128]{2,1,0:T(8,128)S(1)}, f32[4,128,128]{2,1,0:T(8,128)S(1)}, u32[]{:S(2)}, u32[]{:S(2)}) collective-permute-start(f32[4,128,128]{2,1,0:T(8,128)S(1)} %collective-permute-done.1.refs_3_), channel_id=1, source_target_pairs={{0,2},{2,4},{3,1},{4,6},{5,3},{6,8},{7,5},{8,10},{9,7},{10,12},{11... | collective-permute-start | bytes 786440 | tf_op jit(solution)/shard_map/ppermute | solution.py:293
  24.6 13.6 %copy-start.1 = (f32[12,2,128,128]{3,2,1,0:T(8,128)S(1)}, f32[12,2,128,128]{3,2,1,0:T(8,128)}, u32[]{:S(2)}) copy-start(f32[12,2,128,128]{3,2,1,0:T(8,128)} %orb_ref.3) | copy-start | bytes 4718596
  24.7 9.5 %collective-permute-start.8 = (f32[4,128,128]{2,1,0:T(8,128)S(1)}, f32[4,128,128]{2,1,0:T(8,128)S(1)}, u32[]{:S(2)}, u32[]{:S(2)}) collective-permute-start(f32[4,128,128]{2,1,0:T(8,128)S(1)} %get-tuple-element.22), channel_id=1, source_target_pairs={{0,1},{1,0},{2,3},{3,2},{4,5},{5,4},{6,7},{7,6},{8,9},{9,8},{10,11... | collective-permute-start | bytes 786440 | tf_op jit(solution)/shard_map/ppermute | solution.py:252
  24.7 16.5 %collective-permute-start.9 = (f32[4,128,128]{2,1,0:T(8,128)S(1)}, f32[4,128,128]{2,1,0:T(8,128)S(1)}, u32[]{:S(2)}, u32[]{:S(2)}) collective-permute-start(f32[4,128,128]{2,1,0:T(8,128)S(1)} %get-tuple-element.18), channel_id=1, source_target_pairs={{0,1},{1,0},{2,3},{3,2},{4,5},{5,4},{6,7},{7,6},{8,9},{9,8},{10,11... | collective-permute-start | bytes 786440 | tf_op jit(solution)/shard_map/ppermute | solution.py:252
  28.5 13.6 %collective-permute-start.13 = (f32[6,128,128]{2,1,0:T(8,128)S(1)}, f32[6,128,128]{2,1,0:T(8,128)S(1)}, u32[]{:S(2)}, u32[]{:S(2)}) collective-permute-start(f32[6,128,128]{2,1,0:T(8,128)S(1)} %collective-permute-done.12.refs_5_), channel_id=1, source_target_pairs={{0,2},{2,4},{3,1},{4,6},{5,3},{6,8},{7,5},{8,10},{9,7},{10,12},{11... | collective-permute-start | bytes 1179656 | tf_op jit(solution)/shard_map/ppermute | solution.py:293
  32.6 8.7 %collective-permute-start.7 = (f32[2,2,128,128]{3,2,1,0:T(8,128)S(1)}, f32[2,2,128,128]{3,2,1,0:T(8,128)S(1)}, u32[]{:S(2)}, u32[]{:S(2)}) collective-permute-start(f32[2,2,128,128]{3,2,1,0:T(8,128)S(1)} %constant_dynamic-slice_fusion.refs_2_), channel_id=1, source_target_pairs={{0,16},{16,0},{1,17},{17,1},{2,18},{18,2},{3,19},{19,3},{4,20},{20... | collective-permute-start | bytes 786440 | tf_op jit(solution)/shard_map/ppermute | solution.py:217
  34.2 10.7 %collective-permute-start.10 = (f32[4,128,128]{2,1,0:T(8,128)S(1)}, f32[4,128,128]{2,1,0:T(8,128)S(1)}, u32[]{:S(2)}, u32[]{:S(2)}) collective-permute-start(f32[4,128,128]{2,1,0:T(8,128)S(1)} %collective-permute-done.8.refs_3_), channel_id=1, source_target_pairs={{0,2},{2,4},{3,1},{4,6},{5,3},{6,8},{7,5},{8,10},{9,7},{10,12},{11... | collective-permute-start | bytes 786440 | tf_op jit(solution)/shard_map/ppermute | solution.py:293
  38.1 6.8 %collective-permute-start.11 = (f32[4,128,128]{2,1,0:T(8,128)S(1)}, f32[4,128,128]{2,1,0:T(8,128)S(1)}, u32[]{:S(2)}, u32[]{:S(2)}) collective-permute-start(f32[4,128,128]{2,1,0:T(8,128)S(1)} %collective-permute-done.4), channel_id=1, source_target_pairs={{0,1},{1,0},{2,3},{3,2},{4,5},{5,4},{6,7},{7,6},{8,9},{9,8},{10,11... | collective-permute-start | bytes 786440 | tf_op jit(solution)/shard_map/ppermute | solution.py:295

commit v4 on v3

--- a/solution.py
+++ b/solution.py
@@ -102,25 +102,20 @@
             k_ref[p, len(OWN) + k] = pair_weight(weighted, there, dy, dz, scale_of(dy, dz, 1))
 
 
-def local_kernel(k_ref, orb_ref, *acc_refs):
-    base = 0
-    for acc_ref in acc_refs:
-
-        @pl.loop(0, acc_ref.shape[0])
-        def _(j, acc_ref=acc_ref, base=base):
-            for p in range(PLANES):
-                groups = {}
-                for plane, terms, first in ((p, OWN, 0), (1 - p, BESIDE, len(OWN))):
-                    field = orb_ref[base + j, plane]
-                    for k, (dy, dz) in enumerate(terms):
-                        term = k_ref[p, first + k] * shifted(field, dy, 0)
-                        groups[dz] = groups[dz] + term if dz in groups else term
-                out = groups[0]
-                for dz in (1, -1, 2, -2):
-                    out = out + shifted(groups[dz], 0, dz)
-                acc_ref[j, p] = out
-
-        base += acc_ref.shape[0]
+def local_kernel(first, k_ref, orb_ref, acc_ref):
+    @pl.loop(0, acc_ref.shape[0])
+    def _(j):
+        for p in range(PLANES):
+            groups = {}
+            for plane, terms, base in ((p, OWN, 0), (1 - p, BESIDE, len(OWN))):
+                field = orb_ref[first + j, plane]
+                for k, (dy, dz) in enumerate(terms):
+                    term = k_ref[p, base + k] * shifted(field, dy, 0)
+                    groups[dz] = groups[dz] + term if dz in groups else term
+            out = groups[0]
+            for dz in (1, -1, 2, -2):
+                out = out + shifted(groups[dz], 0, dz)
+            acc_ref[j, p] = out
 
 
 def nearest():
@@ -132,6 +127,8 @@
     n = STEPS
     local, slabs, k_ref = refs[:n], refs[n : 2 * n], refs[2 * n]
     weights = block_weights(occ_ref, orb_count)
+    dom, count = lax.axis_index("dom"), lax.axis_size("dom")
+    real = jnp.where((dom == 0) | (dom == count - 1), 0.0, 1.0) if hop else 1.0
     near = nearest()[hop]
     far = 1 - near
     pairs = [(r, i) for r in local for i in range(BLOCK)]
@@ -140,9 +137,9 @@
     there = [r[i, near] for r in slabs for i in range(BLOCK)]
     beyond = [r[i, far] for r in slabs for i in range(BLOCK)]
     for k, (dy, dz) in enumerate(BESIDE):
-        k_ref[k] = pair_weight(here, there, dy, dz, scale_of(dy, dz, 1))
-    k_ref[BEYOND] = pair_weight(here, beyond, 0, 0, TWO)
-    k_ref[ACROSS] = pair_weight(behind, there, 0, 0, TWO)
+        k_ref[k] = pair_weight(here, there, dy, dz, scale_of(dy, dz, 1) * real)
+    k_ref[BEYOND] = pair_weight(here, beyond, 0, 0, TWO * real)
+    k_ref[ACROSS] = pair_weight(behind, there, 0, 0, TWO * real)
 
 
 def side_terms(k_ref, near_plane, far_plane):
@@ -204,9 +201,10 @@
 def hops(slabs):
     swap = [(i, i ^ 1) for i in range(slabs)]
     onward = [(i, i + 2 if i % 2 == 0 else i - 2) for i in range(slabs)]
+    ring = [(a, b % slabs) for a, b in onward]
     onward = [(a, b) for a, b in onward if 0 <= b < slabs]
     back = [(b, a) for a, b in onward]
-    return swap, onward, back
+    return swap, onward, ring, back
 
 
 def everywhere(field, groups):
@@ -232,22 +230,25 @@
     orb_count, planes, rows, columns = orbitals.shape
     groups, slabs = lax.axis_size("band"), lax.axis_size("dom")
     assert planes == PLANES and slabs % 2 == 0 and slabs > 2 and sum(CHUNKS) == orb_count * planes
-    swap, onward, back = hops(slabs)
+    swap, onward, ring, back = hops(slabs)
     n = len(CHUNKS)
     starts = [sum(CHUNKS[:i]) for i in range(n)]
     assert all(n % planes == 0 for n in CHUNKS)
     cuts = [0] + [sum(CHUNKS[:upto]) // planes for upto in GROUPS]
     f32 = lambda *shape: jax.ShapeDtypeStruct(shape, jnp.float32)
 
-    sent = pl.pallas_call(
-        functools.partial(cut_kernel, starts),
-        out_shape=[f32(size, rows, columns) for size in CHUNKS],
-        in_specs=[ANY],
-        out_specs=[VMEM] * n,
-        scratch_shapes=[pltpu.SemaphoreType.DMA((n,))],
-        compiler_params=PARAMS,
-        name="cut",
-    )(orbitals)
+    def cut(name, ids):
+        return pl.pallas_call(
+            functools.partial(cut_kernel, [starts[i] for i in ids]),
+            out_shape=[f32(CHUNKS[i], rows, columns) for i in ids],
+            in_specs=[ANY],
+            out_specs=[VMEM] * len(ids),
+            scratch_shapes=[pltpu.SemaphoreType.DMA((len(ids),))],
+            compiler_params=PARAMS,
+            name=name,
+        )(orbitals)
+
+    sent = [*cut("cut_first", range(2)), *cut("cut_rest", range(2, n))]
     around = lax.ppermute(sent[-1], "dom", back)
     first = [lax.ppermute(part, "dom", swap) for part in sent]
     local = everywhere(orbitals[: STEPS * BLOCK], groups)
@@ -260,15 +261,18 @@
         cost_estimate=pl.CostEstimate(flops=1, bytes_accessed=1, transcendentals=0),
         name="local_weights",
     )(occupations, *local)
-    acc = pl.pallas_call(
-        local_kernel,
-        out_shape=[f32(b - a, planes, rows, columns) for a, b in zip(cuts, cuts[1:])],
-        in_specs=[VMEM] * 2,
-        out_specs=[VMEM] * len(GROUPS),
-        compiler_params=PARAMS,
-        cost_estimate=pl.CostEstimate(flops=1, bytes_accessed=1, transcendentals=0),
-        name="local",
-    )(k_local, orbitals)
+    def local_sums(g):
+        return pl.pallas_call(
+            functools.partial(local_kernel, cuts[g]),
+            out_shape=f32(cuts[g + 1] - cuts[g], planes, rows, columns),
+            in_specs=[VMEM] * 2,
+            out_specs=VMEM,
+            compiler_params=PARAMS,
+            cost_estimate=pl.CostEstimate(flops=1, bytes_accessed=1, transcendentals=0),
+            name=f"local_{g}",
+        )(k_local, orbitals)
+
+    acc = [local_sums(g) for g in range(len(GROUPS))]
 
     count = 0
     while sum(CHUNKS[:count]) < STEPS * BLOCK * planes:
@@ -290,7 +294,8 @@
     k_first = halo_weights("first", first)
     before = {0: around, 1: k_local, 2: k_first}
     second = [
-        lax.ppermute(after(part, before[i]) if i in before else part, "dom", onward) for i, part in enumerate(first[:-1])
+        lax.ppermute(after(part, before[i]) if i in before else part, "dom", ring if i < n - 2 else onward)
+        for i, part in enumerate(first[:-1])
     ]
     second.append(lax.ppermute(around, "dom", swap))
     k_halo = [k_first, halo_weights("second", second)]

time: 46.6 us -> 46.2 us (level)
  waiting for transfers between devices: 7.85 us -> 10.1 us
  starting transfers between devices: 26.8 us -> 24.6 us
    ppermute x4, starting transfers between devices: 15.9 us -> 11.2 us  [per_device(): lax.ppermute(after(part, before[i]) if i in before else part, 'dom', ring...]
    ppermute x5, starting transfers between devices: 9.38 us -> 11.9 us  [per_device(): first = [lax.ppermute(part, 'dom', swap) for part in sent]]
    ppermute x4, waiting for transfers between devices: 1.19 us -> 2.04 us  [per_device(): lax.ppermute(after(part, before[i]) if i in before else part, 'dom', ring...]
    ppermute x1, waiting for transfers between devices: 0.06 us -> 0.8 us  [per_device(): second.append(lax.ppermute(around, 'dom', swap))]
    ppermute x5, waiting for transfers between devices: 6.6 us -> 7.29 us  [per_device(): first = [lax.ppermute(part, 'dom', swap) for part in sent]]
    pallas_call x2 -> x4, Pallas kernels: 3.55 us -> 3.54 us  [the longest x2 3.07 us: local_sums(): pl.pallas_call(functools.partial(local_kernel, cuts[g]), out_shape=f32(cu...]
  transfers between devices with their start and end apart: 14 -> 14, of which waited for: 6 -> 6; matrix products, arithmetic and copies ran while one was open for 0% -> 0% of each run, Pallas kernels for 17% -> 18%
where the time goes in v4:
time: 46.2 us; the launch traced here: 46.1 us
  starting transfers between devices  24.6 us (53%)
  waiting for transfers between devices  10.1 us (22%)
  Pallas kernels  9.53 us (21%)
  local copies, waits for them, and re-layouts  1.49 us (3%)
    ppermute x5, starting transfers between devices, per_device(): first = [lax.ppermute(part, 'dom', swap) for part in sent]  11.9 us
    ppermute x4, starting transfers between devices, per_device(): lax.ppermute(after(part, before[i]) if i in before else part, 'dom', ring...  11.2 us
    ppermute x5, waiting for transfers between devices, per_device(): first = [lax.ppermute(part, 'dom', swap) for part in sent]  7.29 us
    pallas_call x2, Pallas kernels, local_sums(): pl.pallas_call(functools.partial(local_kernel, cuts[g]), out_shape=f32(cu...  3.07 us
    pallas_call x2, Pallas kernels, finish(): pl.pallas_call(functools.partial(finish_kernel, origin, chained), out_sha...  2.69 us
    ppermute x4, waiting for transfers between devices, per_device(): lax.ppermute(after(part, before[i]) if i in before else part, 'dom', ring...  2.04 us
    pallas_call x1, Pallas kernels, per_device(): pl.pallas_call(functools.partial(local_weight_kernel, orb_count), out_sha...  1.72 us
    pallas_call x2, Pallas kernels, halo_weights(): pl.pallas_call(functools.partial(halo_weight_kernel, name == 'second', or...  1.57 us
  transfers between devices with their start and end apart: 14, of which 6 were waited for; matrix products, arithmetic and copies ran while one was open for 0% of the time, Pallas kernels for 18%

profile of v4, /device:TPU:0, one launch (start us, length us, event | category | flops | bytes accessed | tf_op | source)
XLA Modules:
  0.0 46.1 jit_solution(14179557403034204332)
XLA Ops:
  0.0 0.0 copy-start
  0.0 1.4 %copy-done = f32[12,2,128,128]{3,2,1,0:T(8,128)S(1)} copy-done((f32[12,2,128,128]{3,2,1,0:T(8,128)S(1)}, f32[12,2,128,128]{3,2,1,0:T(8,128)}, u32[]{:S(2)}) %copy-start) | copy-done | bytes 1572888
  1.4 0.0 slice-start
  1.4 0.0 copy-start.1
  1.4 0.2 cut_first.1
  1.6 0.0 copy-start.2
  1.7 3.0 %collective-permute-start.2 = (f32[6,128,128]{2,1,0:T(8,128)S(1)}, f32[6,128,128]{2,1,0:T(8,128)S(1)}, u32[]{:S(2)}, u32[]{:S(2)}) collective-permute-start(f32[6,128,128]{2,1,0:T(8,128)S(1)} %get-tuple-element.15), channel_id=1, source_target_pairs={{0,1},{1,0},{2,3},{3,2},{4,5},{5,4},{6,7},{7,6},{8,9},{9,8},{10,11... | collective-permute-start | bytes 1179656 | tf_op jit(solution)/shard_map/ppermute | solution.py:253
  4.7 0.0 slice-done
  4.7 0.1 collective-permute-start
  4.8 0.8 %collective-permute-start.1 = (f32[4,128,128]{2,1,0:T(8,128)S(1)}, f32[4,128,128]{2,1,0:T(8,128)S(1)}, u32[]{:S(2)}, u32[]{:S(2)}) collective-permute-start(f32[4,128,128]{2,1,0:T(8,128)S(1)} %get-tuple-element.14), channel_id=1, source_target_pairs={{0,1},{1,0},{2,3},{3,2},{4,5},{5,4},{6,7},{7,6},{8,9},{9,8},{10,11... | collective-permute-start | bytes 786440 | tf_op jit(solution)/shard_map/ppermute | solution.py:253
  5.6 0.0 copy-done.1
  5.6 0.2 cut_rest.1
  5.8 1.3 %collective-permute-start.4 = (f32[4,128,128]{2,1,0:T(8,128)S(1)}, f32[4,128,128]{2,1,0:T(8,128)S(1)}, u32[]{:S(2)}, u32[]{:S(2)}) collective-permute-start(f32[4,128,128]{2,1,0:T(8,128)S(1)} %get-tuple-element.16), channel_id=1, source_target_pairs={{2,0},{4,2},{1,3},{6,4},{3,5},{8,6},{5,7},{10,8},{7,9},{12,10},{9,... | collective-permute-start | bytes 786440 | tf_op jit(solution)/shard_map/ppermute | solution.py:252
  7.1 3.5 %collective-permute-start.12 = (f32[6,128,128]{2,1,0:T(8,128)S(1)}, f32[6,128,128]{2,1,0:T(8,128)S(1)}, u32[]{:S(2)}, u32[]{:S(2)}) collective-permute-start(f32[6,128,128]{2,1,0:T(8,128)S(1)} %get-tuple-element.21), channel_id=1, source_target_pairs={{0,1},{1,0},{2,3},{3,2},{4,5},{5,4},{6,7},{7,6},{8,9},{9,8},{10,11... | collective-permute-start | bytes 1179656 | tf_op jit(solution)/shard_map/ppermute | solution.py:253
  10.6 0.0 collective-permute-done.refs_1_
  10.6 0.0 copy-done.2
  10.6 1.7 %local_weights.1.k_ref = f32[2,18,128,128]{3,2,1,0:T(8,128)S(1)} custom-call(f32[24]{0:T(128)S(1)} %copy-done.2, f32[2,2,128,128]{3,2,1,0:T(8,128)S(1)} %constant_dynamic-slice_fusion.2.refs_0_, f32[2,2,128,128]{3,2,1,0:T(8,128)S(1)} %collective-permute-done.refs_1_), custom_call_target="tpu_custom_call" | custom-call | flops 1 | bytes 1 | tf_op jit(solution)/shard_map/local_weights/pallas_call | solution.py:255
  12.4 2.2 %collective-permute-done.2.refs_4_ = f32[6,128,128]{2,1,0:T(8,128)S(1)} collective-permute-done((f32[6,128,128]{2,1,0:T(8,128)S(1)}, f32[6,128,128]{2,1,0:T(8,128)S(1)}, u32[]{:S(2)}, u32[]{:S(2)}) %collective-permute-start.2) | collective-permute-done | bytes 393248 | tf_op jit(solution)/shard_map/ppermute | solution.py:253
  14.6 2.1 %collective-permute-start.6 = (f32[6,128,128]{2,1,0:T(8,128)S(1)}, f32[6,128,128]{2,1,0:T(8,128)S(1)}, u32[]{:S(2)}, u32[]{:S(2)}) collective-permute-start(f32[6,128,128]{2,1,0:T(8,128)S(1)} %collective-permute-done.2.refs_4_), channel_id=1, source_target_pairs={{0,2},{1,15},{2,4},{3,1},{4,6},{5,3},{6,8},{7,5},{8,10},{9,7},{10,... | collective-permute-start | bytes 1179656 | tf_op jit(solution)/shard_map/ppermute | solution.py:297
  16.7 3.5 %collective-permute-done.1.refs_3_ = f32[4,128,128]{2,1,0:T(8,128)S(1)} collective-permute-done((f32[4,128,128]{2,1,0:T(8,128)S(1)}, f32[4,128,128]{2,1,0:T(8,128)S(1)}, u32[]{:S(2)}, u32[]{:S(2)}) %collective-permute-start.1) | collective-permute-done | bytes 262176 | tf_op jit(solution)/shard_map/ppermute | solution.py:253
  20.3 0.1 collective-permute-start.3
  20.4 0.0 collective-permute-done.4
  20.4 2.1 %collective-permute-start.5 = (f32[4,128,128]{2,1,0:T(8,128)S(1)}, f32[4,128,128]{2,1,0:T(8,128)S(1)}, u32[]{:S(2)}, u32[]{:S(2)}) collective-permute-start(f32[4,128,128]{2,1,0:T(8,128)S(1)} %collective-permute-done.1.refs_3_), channel_id=1, source_target_pairs={{0,2},{1,15},{2,4},{3,1},{4,6},{5,3},{6,8},{7,5},{8,10},{9,7},{10,... | collective-permute-start | bytes 786440 | tf_op jit(solution)/shard_map/ppermute | solution.py:297
  22.5 4.5 %collective-permute-start.8 = (f32[4,128,128]{2,1,0:T(8,128)S(1)}, f32[4,128,128]{2,1,0:T(8,128)S(1)}, u32[]{:S(2)}, u32[]{:S(2)}) collective-permute-start(f32[4,128,128]{2,1,0:T(8,128)S(1)} %get-tuple-element.19), channel_id=1, source_target_pairs={{0,1},{1,0},{2,3},{3,2},{4,5},{5,4},{6,7},{7,6},{8,9},{9,8},{10,11... | collective-permute-start | bytes 786440 | tf_op jit(solution)/shard_map/ppermute | solution.py:253
  27.1 0.0 collective-permute-done.3.refs_3_
  27.1 0.0 collective-permute-start.9
  27.1 0.8 %first_hop_weights.1.refs_0_ = f32[7,128,128]{2,1,0:T(8,128)S(1)} custom-call(f32[24]{0:T(128)S(1)} %copy-done.2, f32[2,2,128,128]{3,2,1,0:T(8,128)S(1)} %constant_dynamic-slice_fusion.2.refs_0_, f32[2,2,128,128]{3,2,1,0:T(8,128)S(1)} %collective-permute-done.refs_1_, f32[2,2,128,128]{3,2,1,0:T(8,128)S(1)} %constant_dynamic-slice_fusion.1.refs_2_, ...), custom_call_target="tpu_custom_call" | custom-call | flops 1 | bytes 1 | tf_op jit(solution)/shard_map/first_hop_weights/pallas_call | solution.py:284
  27.9 0.0 collective-permute-done.12.refs_5_
  27.9 2.8 %collective-permute-start.13 = (f32[6,128,128]{2,1,0:T(8,128)S(1)}, f32[6,128,128]{2,1,0:T(8,128)S(1)}, u32[]{:S(2)}, u32[]{:S(2)}) collective-permute-start(f32[6,128,128]{2,1,0:T(8,128)S(1)} %collective-permute-done.12.refs_5_), channel_id=1, source_target_pairs={{0,2},{1,15},{2,4},{3,1},{4,6},{5,3},{6,8},{7,5},{8,10},{9,7},{10,... | collective-permute-start | bytes 1179656 | tf_op jit(solution)/shard_map/ppermute | solution.py:297
  30.7 1.7 %collective-permute-done.5.refs_6_ = f32[4,128,128]{2,1,0:T(8,128)S(1)} collective-permute-done((f32[4,128,128]{2,1,0:T(8,128)S(1)}, f32[4,128,128]{2,1,0:T(8,128)S(1)}, u32[]{:S(2)}, u32[]{:S(2)}) %collective-permute-start.5) | collective-permute-done | bytes 262176 | tf_op jit(solution)/shard_map/ppermute | solution.py:297
  32.5 0.0 collective-permute-done.6.refs_7_
  32.5 0.1 collective-permute-start.7
  32.6 1.5 %collective-permute-done.8.refs_3_ = f32[4,128,128]{2,1,0:T(8,128)S(1)} collective-permute-done((f32[4,128,128]{2,1,0:T(8,128)S(1)}, f32[4,128,128]{2,1,0:T(8,128)S(1)}, u32[]{:S(2)}, u32[]{:S(2)}) %collective-permute-start.8) | collective-permute-done | bytes 262176 | tf_op jit(solution)/shard_map/ppermute | solution.py:253
  34.1 4.1 %collective-permute-start.10 = (f32[4,128,128]{2,1,0:T(8,128)S(1)}, f32[4,128,128]{2,1,0:T(8,128)S(1)}, u32[]{:S(2)}, u32[]{:S(2)}) collective-permute-start(f32[4,128,128]{2,1,0:T(8,128)S(1)} %collective-permute-done.8.refs_3_), channel_id=1, source_target_pairs={{0,2},{2,4},{3,1},{4,6},{5,3},{6,8},{7,5},{8,10},{9,7},{10,12},{11... | collective-permute-start | bytes 786440 | tf_op jit(solution)/shard_map/ppermute | solution.py:297
  38.3 0.1 collective-permute-start.11
  38.3 1.0 %local_1.1.refs_2_ = f32[4,2,128,128]{3,2,1,0:T(8,128)S(1)} custom-call(f32[2,18,128,128]{3,2,1,0:T(8,128)S(1)} %local_weights.1.k_ref, f32[12,2,128,128]{3,2,1,0:T(8,128)S(1)} %copy-done.1), custom_call_target="tpu_custom_call" | custom-call | flops 1 | bytes 1 | tf_op jit(solution)/shard_map/local_1/pallas_call | solution.py:265
  39.4 2.0 %local_0.1.refs_2_ = f32[8,2,128,128]{3,2,1,0:T(8,128)S(1)} custom-call(f32[2,18,128,128]{3,2,1,0:T(8,128)S(1)} %local_weights.1.k_ref, f32[12,2,128,128]{3,2,1,0:T(8,128)S(1)} %copy-done.1), custom_call_target="tpu_custom_call" | custom-call | flops 1 | bytes 1 | tf_op jit(solution)/shard_map/local_0/pallas_call | solution.py:265
  41.4 0.0 collective-permute-done.9.refs_4_
  41.4 0.0 collective-permute-done.7.refs_3_
  41.5 0.8 %second_hop_weights.1.refs_1_ = f32[7,128,128]{2,1,0:T(8,128)S(1)} custom-call(f32[24]{0:T(128)S(1)} %copy-done.2, f32[2,2,128,128]{3,2,1,0:T(8,128)S(1)} %constant_dynamic-slice_fusion.2.refs_0_, f32[2,2,128,128]{3,2,1,0:T(8,128)S(1)} %collective-permute-done.refs_1_, f32[2,2,128,128]{3,2,1,0:T(8,128)S(1)} %constant_dynamic-slice_fusion.refs_2_, ...), custom_call_target="tpu_custom_call" | custom-call | flops 1 | bytes 1 | tf_op jit(solution)/shard_map/second_hop_weights/pallas_call | solution.py:284
  42.3 0.0 collective-permute-done.13.refs_8_
  42.3 1.5 %finish_0.1.refs_7_ = f32[12,2,128,128]{3,2,1,0:T(8,128)} custom-call(f32[7,128,128]{2,1,0:T(8,128)S(1)} %first_hop_weights.1.refs_0_, f32[7,128,128]{2,1,0:T(8,128)S(1)} %second_hop_weights.1.refs_1_, f32[8,2,128,128]{3,2,1,0:T(8,128)S(1)} %local_0.1.refs_2_, f32[4,128,128]{2,1,0:T(8,128)S(1)} %collective-permute-done.1.refs_3_, ...), custom_call_target="tpu_custom_call" | custom-call | flops 1 | bytes 1 | tf_op jit(solution)/shard_map/finish_0/pallas_call | solution.py:188
  43.8 0.3 collective-permute-done.10.refs_5_
  44.1 0.8 %collective-permute-done.11.refs_6_ = f32[4,128,128]{2,1,0:T(8,128)S(1)} collective-permute-done((f32[4,128,128]{2,1,0:T(8,128)S(1)}, f32[4,128,128]{2,1,0:T(8,128)S(1)}, u32[]{:S(2)}, u32[]{:S(2)}) %collective-permute-start.11) | collective-permute-done | bytes 262176 | tf_op jit(solution)/shard_map/ppermute | solution.py:300
  44.9 1.1 %finish_1.1 = f32[12,2,128,128]{3,2,1,0:T(8,128)} custom-call(f32[7,128,128]{2,1,0:T(8,128)S(1)} %first_hop_weights.1.refs_0_, f32[7,128,128]{2,1,0:T(8,128)S(1)} %second_hop_weights.1.refs_1_, f32[4,2,128,128]{3,2,1,0:T(8,128)S(1)} %local_1.1.refs_2_, f32[4,128,128]{2,1,0:T(8,128)S(1)} %collective-permute-done.8.refs_3_, ...), custom_call_target="tpu_custom_call", output_to_operand_aliasing={{}: (7, {})} | custom-call | flops 1 | bytes 1 | tf_op jit(solution)/shard_map/finish_1/pallas_call | solution.py:188
  (5 shorter events, 0.1 us)
Async XLA Ops:
  0.0 1.4 %copy-start = (f32[12,2,128,128]{3,2,1,0:T(8,128)S(1)}, f32[12,2,128,128]{3,2,1,0:T(8,128)}, u32[]{:S(2)}) copy-start(f32[12,2,128,128]{3,2,1,0:T(8,128)} %orb_ref.7) | copy-start | bytes 4718596
  1.4 3.3 %slice-start = ((f32[12,2,128,128]{3,2,1,0:T(8,128)}), f32[4,2,128,128]{3,2,1,0:T(8,128)S(1)}, s32[]{:S(2)}) async-start(f32[12,2,128,128]{3,2,1,0:T(8,128)} %orb_ref.7), calls=%async_computation | async-start | bytes 1048576 | tf_op jit(solution)/shard_map/slice | solution.py:254
  1.4 4.1 %copy-start.1 = (f32[12,2,128,128]{3,2,1,0:T(8,128)S(1)}, f32[12,2,128,128]{3,2,1,0:T(8,128)}, u32[]{:S(2)}) copy-start(f32[12,2,128,128]{3,2,1,0:T(8,128)} %orb_ref.7) | copy-start | bytes 4718596
  1.6 9.0 %copy-start.2 = (f32[24]{0:T(128)S(1)}, f32[24]{0:T(128)}, u32[]{:S(2)}) copy-start(f32[24]{0:T(128)} %occ_ref.5) | copy-start | bytes 292
  1.7 12.9 %collective-permute-start.2 = (f32[6,128,128]{2,1,0:T(8,128)S(1)}, f32[6,128,128]{2,1,0:T(8,128)S(1)}, u32[]{:S(2)}, u32[]{:S(2)}) collective-permute-start(f32[6,128,128]{2,1,0:T(8,128)S(1)} %get-tuple-element.15), channel_id=1, source_target_pairs={{0,1},{1,0},{2,3},{3,2},{4,5},{5,4},{6,7},{7,6},{8,9},{9,8},{10,11... | collective-permute-start | bytes 1179656 | tf_op jit(solution)/shard_map/ppermute | solution.py:253
  4.7 5.9 %collective-permute-start = (f32[2,2,128,128]{3,2,1,0:T(8,128)S(1)}, f32[2,2,128,128]{3,2,1,0:T(8,128)S(1)}, u32[]{:S(2)}, u32[]{:S(2)}) collective-permute-start(f32[2,2,128,128]{3,2,1,0:T(8,128)S(1)} %constant_dynamic-slice_fusion.2.refs_0_), channel_id=1, source_target_pairs={{0,16},{16,0},{1,17},{17,1},{2,18},{18,2},{3,19},{19,3},{4,20},{20... | collective-permute-start | bytes 786440 | tf_op jit(solution)/shard_map/ppermute | solution.py:215
  4.8 15.5 %collective-permute-start.1 = (f32[4,128,128]{2,1,0:T(8,128)S(1)}, f32[4,128,128]{2,1,0:T(8,128)S(1)}, u32[]{:S(2)}, u32[]{:S(2)}) collective-permute-start(f32[4,128,128]{2,1,0:T(8,128)S(1)} %get-tuple-element.14), channel_id=1, source_target_pairs={{0,1},{1,0},{2,3},{3,2},{4,5},{5,4},{6,7},{7,6},{8,9},{9,8},{10,11... | collective-permute-start | bytes 786440 | tf_op jit(solution)/shard_map/ppermute | solution.py:253
  5.8 14.6 %collective-permute-start.4 = (f32[4,128,128]{2,1,0:T(8,128)S(1)}, f32[4,128,128]{2,1,0:T(8,128)S(1)}, u32[]{:S(2)}, u32[]{:S(2)}) collective-permute-start(f32[4,128,128]{2,1,0:T(8,128)S(1)} %get-tuple-element.16), channel_id=1, source_target_pairs={{2,0},{4,2},{1,3},{6,4},{3,5},{8,6},{5,7},{10,8},{7,9},{12,10},{9,... | collective-permute-start | bytes 786440 | tf_op jit(solution)/shard_map/ppermute | solution.py:252
  7.1 20.8 %collective-permute-start.12 = (f32[6,128,128]{2,1,0:T(8,128)S(1)}, f32[6,128,128]{2,1,0:T(8,128)S(1)}, u32[]{:S(2)}, u32[]{:S(2)}) collective-permute-start(f32[6,128,128]{2,1,0:T(8,128)S(1)} %get-tuple-element.21), channel_id=1, source_target_pairs={{0,1},{1,0},{2,3},{3,2},{4,5},{5,4},{6,7},{7,6},{8,9},{9,8},{10,11... | collective-permute-start | bytes 1179656 | tf_op jit(solution)/shard_map/ppermute | solution.py:253
  14.6 17.9 %collective-permute-start.6 = (f32[6,128,128]{2,1,0:T(8,128)S(1)}, f32[6,128,128]{2,1,0:T(8,128)S(1)}, u32[]{:S(2)}, u32[]{:S(2)}) collective-permute-start(f32[6,128,128]{2,1,0:T(8,128)S(1)} %collective-permute-done.2.refs_4_), channel_id=1, source_target_pairs={{0,2},{1,15},{2,4},{3,1},{4,6},{5,3},{6,8},{7,5},{8,10},{9,7},{10,... | collective-permute-start | bytes 1179656 | tf_op jit(solution)/shard_map/ppermute | solution.py:297
  20.3 6.8 %collective-permute-start.3 = (f32[2,2,128,128]{3,2,1,0:T(8,128)S(1)}, f32[2,2,128,128]{3,2,1,0:T(8,128)S(1)}, u32[]{:S(2)}, u32[]{:S(2)}) collective-permute-start(f32[2,2,128,128]{3,2,1,0:T(8,128)S(1)} %constant_dynamic-slice_fusion.1.refs_2_), channel_id=1, source_target_pairs={{0,16},{16,0},{1,17},{17,1},{2,18},{18,2},{3,19},{19,3},{4,20},{20... | collective-permute-start | bytes 786440 | tf_op jit(solution)/shard_map/ppermute | solution.py:215
  20.4 12.1 %collective-permute-start.5 = (f32[4,128,128]{2,1,0:T(8,128)S(1)}, f32[4,128,128]{2,1,0:T(8,128)S(1)}, u32[]{:S(2)}, u32[]{:S(2)}) collective-permute-start(f32[4,128,128]{2,1,0:T(8,128)S(1)} %collective-permute-done.1.refs_3_), channel_id=1, source_target_pairs={{0,2},{1,15},{2,4},{3,1},{4,6},{5,3},{6,8},{7,5},{8,10},{9,7},{10,... | collective-permute-start | bytes 786440 | tf_op jit(solution)/shard_map/ppermute | solution.py:297
  22.5 11.6 %collective-permute-start.8 = (f32[4,128,128]{2,1,0:T(8,128)S(1)}, f32[4,128,128]{2,1,0:T(8,128)S(1)}, u32[]{:S(2)}, u32[]{:S(2)}) collective-permute-start(f32[4,128,128]{2,1,0:T(8,128)S(1)} %get-tuple-element.19), channel_id=1, source_target_pairs={{0,1},{1,0},{2,3},{3,2},{4,5},{5,4},{6,7},{7,6},{8,9},{9,8},{10,11... | collective-permute-start | bytes 786440 | tf_op jit(solution)/shard_map/ppermute | solution.py:253
  27.1 14.4 %collective-permute-start.9 = (f32[4,128,128]{2,1,0:T(8,128)S(1)}, f32[4,128,128]{2,1,0:T(8,128)S(1)}, u32[]{:S(2)}, u32[]{:S(2)}) collective-permute-start(f32[4,128,128]{2,1,0:T(8,128)S(1)} %get-tuple-element.16), channel_id=1, source_target_pairs={{0,1},{1,0},{2,3},{3,2},{4,5},{5,4},{6,7},{7,6},{8,9},{9,8},{10,11... | collective-permute-start | bytes 786440 | tf_op jit(solution)/shard_map/ppermute | solution.py:253
  27.9 14.4 %collective-permute-start.13 = (f32[6,128,128]{2,1,0:T(8,128)S(1)}, f32[6,128,128]{2,1,0:T(8,128)S(1)}, u32[]{:S(2)}, u32[]{:S(2)}) collective-permute-start(f32[6,128,128]{2,1,0:T(8,128)S(1)} %collective-permute-done.12.refs_5_), channel_id=1, source_target_pairs={{0,2},{1,15},{2,4},{3,1},{4,6},{5,3},{6,8},{7,5},{8,10},{9,7},{10,... | collective-permute-start | bytes 1179656 | tf_op jit(solution)/shard_map/ppermute | solution.py:297
  32.5 8.9 %collective-permute-start.7 = (f32[2,2,128,128]{3,2,1,0:T(8,128)S(1)}, f32[2,2,128,128]{3,2,1,0:T(8,128)S(1)}, u32[]{:S(2)}, u32[]{:S(2)}) collective-permute-start(f32[2,2,128,128]{3,2,1,0:T(8,128)S(1)} %constant_dynamic-slice_fusion.refs_2_), channel_id=1, source_target_pairs={{0,16},{16,0},{1,17},{17,1},{2,18},{18,2},{3,19},{19,3},{4,20},{20... | collective-permute-start | bytes 786440 | tf_op jit(solution)/shard_map/ppermute | solution.py:215
  34.1 10.0 %collective-permute-start.10 = (f32[4,128,128]{2,1,0:T(8,128)S(1)}, f32[4,128,128]{2,1,0:T(8,128)S(1)}, u32[]{:S(2)}, u32[]{:S(2)}) collective-permute-start(f32[4,128,128]{2,1,0:T(8,128)S(1)} %collective-permute-done.8.refs_3_), channel_id=1, source_target_pairs={{0,2},{2,4},{3,1},{4,6},{5,3},{6,8},{7,5},{8,10},{9,7},{10,12},{11... | collective-permute-start | bytes 786440 | tf_op jit(solution)/shard_map/ppermute | solution.py:297
  38.3 6.6 %collective-permute-start.11 = (f32[4,128,128]{2,1,0:T(8,128)S(1)}, f32[4,128,128]{2,1,0:T(8,128)S(1)}, u32[]{:S(2)}, u32[]{:S(2)}) collective-permute-start(f32[4,128,128]{2,1,0:T(8,128)S(1)} %collective-permute-done.4), channel_id=1, source_target_pairs={{0,1},{1,0},{2,3},{3,2},{4,5},{5,4},{6,7},{7,6},{8,9},{9,8},{10,11... | collective-permute-start | bytes 786440 | tf_op jit(solution)/shard_map/ppermute | solution.py:300

commit v5 on v4

--- a/solution.py
+++ b/solution.py
@@ -151,25 +151,47 @@
     return beside + k_ref[BEYOND] * far_plane, k_ref[ACROSS] * near_plane
 
 
-def finish_kernel(origin, chained, *refs):
+def add_first_kernel(k_ref, acc_ref, *refs):
+    out_ref = refs[-1]
+    odd = nearest()[0]
+    even = 1 - odd
+    base = 0
+    for first_ref in refs[:-1]:
+        size = first_ref.shape[0] // PLANES
+
+        @pl.loop(0, size, unroll=size)
+        def _(i, first_ref=first_ref, base=base):
+            j, at = base + i, PLANES * i
+            to_even, to_odd = side_terms(k_ref, first_ref[at + odd], first_ref[at + even])
+            out_ref[j, even] = acc_ref[j, even] + to_even
+            out_ref[j, odd] = acc_ref[j, odd] + to_odd
+
+        base += size
+
+
+def finish_kernel(origin, hops_left, chained, *refs):
     k_refs, acc_ref, refs = refs[:2], refs[2], refs[3:]
     sum_ref, sems = refs[-2:]
     out_ref = refs[-3]
     chunk_refs = refs[: -3 - chained]
-    half = len(chunk_refs) // 2
+    count = len(chunk_refs) // hops_left
     odd = nearest()[0]
     even = 1 - odd
     base = 0
-    for first_ref, second_ref in zip(chunk_refs[:half], chunk_refs[half:]):
-        size = first_ref.shape[0] // PLANES
+    for at_chunk in range(count):
+        second_ref = chunk_refs[-count:][at_chunk]
+        first_ref = chunk_refs[at_chunk]
+        size = second_ref.shape[0] // PLANES
 
         @pl.loop(0, size, unroll=size)
         def _(i, first_ref=first_ref, second_ref=second_ref, base=base):
             j, at = base + i, PLANES * i
-            to_even, to_odd = side_terms(k_refs[0], first_ref[at + odd], first_ref[at + even])
-            more_odd, more_even = side_terms(k_refs[1], second_ref[at + even], second_ref[at + odd])
-            sum_ref[j, even] = acc_ref[j, even] + (to_even + more_even)
-            sum_ref[j, odd] = acc_ref[j, odd] + (to_odd + more_odd)
+            to_odd, to_even = side_terms(k_refs[1], second_ref[at + even], second_ref[at + odd])
+            if hops_left == 2:
+                more_even, more_odd = side_terms(k_refs[0], first_ref[at + odd], first_ref[at + even])
+                to_even, to_odd = to_even + more_even, to_odd + more_odd
+            sum_ref[j, even] = acc_ref[j, even] + to_even
+            sum_ref[j, odd] = acc_ref[j, odd] + to_odd
             pltpu.make_async_copy(sum_ref.at[j], out_ref.at[origin + j], sems.at[j]).start()
 
         base += size
@@ -183,10 +205,10 @@
 PARAMS = pltpu.CompilerParams(vmem_limit_bytes=16 * 1024 * 1024)
 
 
-def finish(name, origin, weights, acc, chunks, out, shape):
+def finish(name, origin, hops_left, weights, acc, chunks, out, shape):
     chained = out is not None
     return pl.pallas_call(
-        functools.partial(finish_kernel, origin, chained),
+        functools.partial(finish_kernel, origin, hops_left, chained),
         out_shape=jax.ShapeDtypeStruct(shape, jnp.float32),
         in_specs=[VMEM] * (3 + len(chunks)) + [ANY] * chained,
         out_specs=ANY,
@@ -303,8 +325,19 @@
 
     out, begin = None, 0
     for g, upto in enumerate(GROUPS):
-        chunks = first[begin:upto] + second[begin:upto]
-        out = finish(f"finish_{g}", cuts[g], k_halo, acc[g], chunks, out, orbitals.shape)
+        last = g == len(GROUPS) - 1
+        chunks = ([] if last else first[begin:upto]) + second[begin:upto]
+        if last:
+            acc[g] = pl.pallas_call(
+                add_first_kernel,
+                out_shape=f32(*acc[g].shape),
+                in_specs=[VMEM] * (2 + upto - begin),
+                out_specs=VMEM,
+                compiler_params=PARAMS,
+                cost_estimate=pl.CostEstimate(flops=1, bytes_accessed=1, transcendentals=0),
+                name="add_first",
+            )(k_first, acc[g], *first[begin:upto])
+        out = finish(f"finish_{g}", cuts[g], 1 if last else 2, k_halo, acc[g], chunks, out, orbitals.shape)
         begin = upto
     return out
 

time: 46.2 us -> 46 us (level)
    pallas_call x2 -> x3, Pallas kernels: 2.69 us -> 2.74 us  [the longest x2 2.47 us: finish(): pl.pallas_call(functools.partial(finish_kernel, origin, hops_left, chaine...]
  transfers between devices with their start and end apart: 14 -> 14, of which waited for: 6 -> 5; matrix products, arithmetic and copies ran while one was open for 0% -> 0% of each run, Pallas kernels for 18% -> 18%
where the time goes in v5:
time: 46 us; the launch traced here: 45.9 us
  starting transfers between devices  24.6 us (53%)
  waiting for transfers between devices  9.87 us (21%)
  Pallas kernels  9.59 us (21%)
  local copies, waits for them, and re-layouts  1.49 us (3%)
    ppermute x5, starting transfers between devices, per_device(): first = [lax.ppermute(part, 'dom', swap) for part in sent]  11.9 us
    ppermute x4, starting transfers between devices, per_device(): lax.ppermute(after(part, before[i]) if i in before else part, 'dom', ring...  11.2 us
    ppermute x5, waiting for transfers between devices, per_device(): first = [lax.ppermute(part, 'dom', swap) for part in sent]  7.29 us
    pallas_call x2, Pallas kernels, local_sums(): pl.pallas_call(functools.partial(local_kernel, cuts[g]), out_shape=f32(cu...  3.07 us
    pallas_call x2, Pallas kernels, finish(): pl.pallas_call(functools.partial(finish_kernel, origin, hops_left, chaine...  2.47 us
    ppermute x4, waiting for transfers between devices, per_device(): lax.ppermute(after(part, before[i]) if i in before else part, 'dom', ring...  1.77 us
    pallas_call x1, Pallas kernels, per_device(): pl.pallas_call(functools.partial(local_weight_kernel, orb_count), out_sha...  1.72 us
    pallas_call x2, Pallas kernels, halo_weights(): pl.pallas_call(functools.partial(halo_weight_kernel, name == 'second', or...  1.58 us
  transfers between devices with their start and end apart: 14, of which 5 were waited for; matrix products, arithmetic and copies ran while one was open for 0% of the time, Pallas kernels for 18%

profile of v5, /device:TPU:0, one launch (start us, length us, event | category | flops | bytes accessed | tf_op | source)
XLA Modules:
  0.0 45.9 jit_solution(12679274112910420801)
XLA Ops:
  0.0 0.0 copy-start
  0.0 1.4 %copy-done = f32[12,2,128,128]{3,2,1,0:T(8,128)S(1)} copy-done((f32[12,2,128,128]{3,2,1,0:T(8,128)S(1)}, f32[12,2,128,128]{3,2,1,0:T(8,128)}, u32[]{:S(2)}) %copy-start) | copy-done | bytes 1572888
  1.4 0.0 slice-start
  1.4 0.0 copy-start.1
  1.4 0.2 cut_first.1
  1.6 0.0 copy-start.2
  1.7 3.0 %collective-permute-start.2 = (f32[6,128,128]{2,1,0:T(8,128)S(1)}, f32[6,128,128]{2,1,0:T(8,128)S(1)}, u32[]{:S(2)}, u32[]{:S(2)}) collective-permute-start(f32[6,128,128]{2,1,0:T(8,128)S(1)} %get-tuple-element.15), channel_id=1, source_target_pairs={{0,1},{1,0},{2,3},{3,2},{4,5},{5,4},{6,7},{7,6},{8,9},{9,8},{10,11... | collective-permute-start | bytes 1179656 | tf_op jit(solution)/shard_map/ppermute | solution.py:275
  4.7 0.0 slice-done
  4.7 0.1 collective-permute-start
  4.8 0.8 %collective-permute-start.1 = (f32[4,128,128]{2,1,0:T(8,128)S(1)}, f32[4,128,128]{2,1,0:T(8,128)S(1)}, u32[]{:S(2)}, u32[]{:S(2)}) collective-permute-start(f32[4,128,128]{2,1,0:T(8,128)S(1)} %get-tuple-element.14), channel_id=1, source_target_pairs={{0,1},{1,0},{2,3},{3,2},{4,5},{5,4},{6,7},{7,6},{8,9},{9,8},{10,11... | collective-permute-start | bytes 786440 | tf_op jit(solution)/shard_map/ppermute | solution.py:275
  5.6 0.0 copy-done.1
  5.6 0.2 cut_rest.1
  5.8 1.3 %collective-permute-start.4 = (f32[4,128,128]{2,1,0:T(8,128)S(1)}, f32[4,128,128]{2,1,0:T(8,128)S(1)}, u32[]{:S(2)}, u32[]{:S(2)}) collective-permute-start(f32[4,128,128]{2,1,0:T(8,128)S(1)} %get-tuple-element.16), channel_id=1, source_target_pairs={{2,0},{4,2},{1,3},{6,4},{3,5},{8,6},{5,7},{10,8},{7,9},{12,10},{9,... | collective-permute-start | bytes 786440 | tf_op jit(solution)/shard_map/ppermute | solution.py:274
  7.1 3.5 %collective-permute-start.12 = (f32[6,128,128]{2,1,0:T(8,128)S(1)}, f32[6,128,128]{2,1,0:T(8,128)S(1)}, u32[]{:S(2)}, u32[]{:S(2)}) collective-permute-start(f32[6,128,128]{2,1,0:T(8,128)S(1)} %get-tuple-element.21), channel_id=1, source_target_pairs={{0,1},{1,0},{2,3},{3,2},{4,5},{5,4},{6,7},{7,6},{8,9},{9,8},{10,11... | collective-permute-start | bytes 1179656 | tf_op jit(solution)/shard_map/ppermute | solution.py:275
  10.6 0.0 collective-permute-done.refs_1_
  10.6 0.0 copy-done.2
  10.6 1.7 %local_weights.1.k_ref = f32[2,18,128,128]{3,2,1,0:T(8,128)S(1)} custom-call(f32[24]{0:T(128)S(1)} %copy-done.2, f32[2,2,128,128]{3,2,1,0:T(8,128)S(1)} %constant_dynamic-slice_fusion.2.refs_0_, f32[2,2,128,128]{3,2,1,0:T(8,128)S(1)} %collective-permute-done.refs_1_), custom_call_target="tpu_custom_call" | custom-call | flops 1 | bytes 1 | tf_op jit(solution)/shard_map/local_weights/pallas_call | solution.py:277
  12.4 2.2 %collective-permute-done.2.refs_4_ = f32[6,128,128]{2,1,0:T(8,128)S(1)} collective-permute-done((f32[6,128,128]{2,1,0:T(8,128)S(1)}, f32[6,128,128]{2,1,0:T(8,128)S(1)}, u32[]{:S(2)}, u32[]{:S(2)}) %collective-permute-start.2) | collective-permute-done | bytes 393248 | tf_op jit(solution)/shard_map/ppermute | solution.py:275
  14.6 2.1 %collective-permute-start.6 = (f32[6,128,128]{2,1,0:T(8,128)S(1)}, f32[6,128,128]{2,1,0:T(8,128)S(1)}, u32[]{:S(2)}, u32[]{:S(2)}) collective-permute-start(f32[6,128,128]{2,1,0:T(8,128)S(1)} %collective-permute-done.2.refs_4_), channel_id=1, source_target_pairs={{0,2},{1,15},{2,4},{3,1},{4,6},{5,3},{6,8},{7,5},{8,10},{9,7},{10,... | collective-permute-start | bytes 1179656 | tf_op jit(solution)/shard_map/ppermute | solution.py:319
  16.7 3.5 %collective-permute-done.1.refs_3_ = f32[4,128,128]{2,1,0:T(8,128)S(1)} collective-permute-done((f32[4,128,128]{2,1,0:T(8,128)S(1)}, f32[4,128,128]{2,1,0:T(8,128)S(1)}, u32[]{:S(2)}, u32[]{:S(2)}) %collective-permute-start.1) | collective-permute-done | bytes 262176 | tf_op jit(solution)/shard_map/ppermute | solution.py:275
  20.3 0.1 collective-permute-start.3
  20.4 0.0 collective-permute-done.4
  20.4 2.1 %collective-permute-start.5 = (f32[4,128,128]{2,1,0:T(8,128)S(1)}, f32[4,128,128]{2,1,0:T(8,128)S(1)}, u32[]{:S(2)}, u32[]{:S(2)}) collective-permute-start(f32[4,128,128]{2,1,0:T(8,128)S(1)} %collective-permute-done.1.refs_3_), channel_id=1, source_target_pairs={{0,2},{1,15},{2,4},{3,1},{4,6},{5,3},{6,8},{7,5},{8,10},{9,7},{10,... | collective-permute-start | bytes 786440 | tf_op jit(solution)/shard_map/ppermute | solution.py:319
  22.5 4.5 %collective-permute-start.8 = (f32[4,128,128]{2,1,0:T(8,128)S(1)}, f32[4,128,128]{2,1,0:T(8,128)S(1)}, u32[]{:S(2)}, u32[]{:S(2)}) collective-permute-start(f32[4,128,128]{2,1,0:T(8,128)S(1)} %get-tuple-element.19), channel_id=1, source_target_pairs={{0,1},{1,0},{2,3},{3,2},{4,5},{5,4},{6,7},{7,6},{8,9},{9,8},{10,11... | collective-permute-start | bytes 786440 | tf_op jit(solution)/shard_map/ppermute | solution.py:275
  27.1 0.0 collective-permute-done.3.refs_3_
  27.1 0.0 collective-permute-start.9
  27.1 0.8 %first_hop_weights.1.k_ref.refs_0_ = f32[7,128,128]{2,1,0:T(8,128)S(1)} custom-call(f32[24]{0:T(128)S(1)} %copy-done.2, f32[2,2,128,128]{3,2,1,0:T(8,128)S(1)} %constant_dynamic-slice_fusion.2.refs_0_, f32[2,2,128,128]{3,2,1,0:T(8,128)S(1)} %collective-permute-done.refs_1_, f32[2,2,128,128]{3,2,1,0:T(8,128)S(1)} %constant_dynamic-slice_fusion.1.refs_2_, ...), custom_call_target="tpu_custom_call" | custom-call | flops 1 | bytes 1 | tf_op jit(solution)/shard_map/first_hop_weights/pallas_call | solution.py:306
  27.9 0.0 collective-permute-done.12.refs_5_
  27.9 2.8 %collective-permute-start.13 = (f32[6,128,128]{2,1,0:T(8,128)S(1)}, f32[6,128,128]{2,1,0:T(8,128)S(1)}, u32[]{:S(2)}, u32[]{:S(2)}) collective-permute-start(f32[6,128,128]{2,1,0:T(8,128)S(1)} %collective-permute-done.12.refs_5_), channel_id=1, source_target_pairs={{0,2},{1,15},{2,4},{3,1},{4,6},{5,3},{6,8},{7,5},{8,10},{9,7},{10,... | collective-permute-start | bytes 1179656 | tf_op jit(solution)/shard_map/ppermute | solution.py:319
  30.7 1.7 %collective-permute-done.5.refs_6_ = f32[4,128,128]{2,1,0:T(8,128)S(1)} collective-permute-done((f32[4,128,128]{2,1,0:T(8,128)S(1)}, f32[4,128,128]{2,1,0:T(8,128)S(1)}, u32[]{:S(2)}, u32[]{:S(2)}) %collective-permute-start.5) | collective-permute-done | bytes 262176 | tf_op jit(solution)/shard_map/ppermute | solution.py:319
  32.5 0.0 collective-permute-done.6.refs_7_
  32.5 0.1 collective-permute-start.7
  32.6 1.5 %collective-permute-done.8.refs_0_ = f32[4,128,128]{2,1,0:T(8,128)S(1)} collective-permute-done((f32[4,128,128]{2,1,0:T(8,128)S(1)}, f32[4,128,128]{2,1,0:T(8,128)S(1)}, u32[]{:S(2)}, u32[]{:S(2)}) %collective-permute-start.8) | collective-permute-done | bytes 262176 | tf_op jit(solution)/shard_map/ppermute | solution.py:275
  34.1 4.1 %collective-permute-start.10 = (f32[4,128,128]{2,1,0:T(8,128)S(1)}, f32[4,128,128]{2,1,0:T(8,128)S(1)}, u32[]{:S(2)}, u32[]{:S(2)}) collective-permute-start(f32[4,128,128]{2,1,0:T(8,128)S(1)} %collective-permute-done.8.refs_0_), channel_id=1, source_target_pairs={{0,2},{2,4},{3,1},{4,6},{5,3},{6,8},{7,5},{8,10},{9,7},{10,12},{11... | collective-permute-start | bytes 786440 | tf_op jit(solution)/shard_map/ppermute | solution.py:319
  38.3 0.1 collective-permute-start.11
  38.3 1.0 %local_1.1.acc_ref = f32[4,2,128,128]{3,2,1,0:T(8,128)S(1)} custom-call(f32[2,18,128,128]{3,2,1,0:T(8,128)S(1)} %local_weights.1.k_ref, f32[12,2,128,128]{3,2,1,0:T(8,128)S(1)} %copy-done.1), custom_call_target="tpu_custom_call" | custom-call | flops 1 | bytes 1 | tf_op jit(solution)/shard_map/local_1/pallas_call | solution.py:287
  39.4 2.0 %local_0.1.refs_2_ = f32[8,2,128,128]{3,2,1,0:T(8,128)S(1)} custom-call(f32[2,18,128,128]{3,2,1,0:T(8,128)S(1)} %local_weights.1.k_ref, f32[12,2,128,128]{3,2,1,0:T(8,128)S(1)} %copy-done.1), custom_call_target="tpu_custom_call" | custom-call | flops 1 | bytes 1 | tf_op jit(solution)/shard_map/local_0/pallas_call | solution.py:287
  41.4 0.0 collective-permute-done.9.refs_1_
  41.4 0.3 add_first.1.refs_2_
  41.7 0.0 collective-permute-done.7.refs_3_
  41.7 0.8 %second_hop_weights.1.refs_1_ = f32[7,128,128]{2,1,0:T(8,128)S(1)} custom-call(f32[24]{0:T(128)S(1)} %copy-done.2, f32[2,2,128,128]{3,2,1,0:T(8,128)S(1)} %constant_dynamic-slice_fusion.2.refs_0_, f32[2,2,128,128]{3,2,1,0:T(8,128)S(1)} %collective-permute-done.refs_1_, f32[2,2,128,128]{3,2,1,0:T(8,128)S(1)} %constant_dynamic-slice_fusion.refs_2_, ...), custom_call_target="tpu_custom_call" | custom-call | flops 1 | bytes 1 | tf_op jit(solution)/shard_map/second_hop_weights/pallas_call | solution.py:306
  42.5 0.0 collective-permute-done.13.refs_8_
  42.5 1.5 %finish_0.1.refs_5_ = f32[12,2,128,128]{3,2,1,0:T(8,128)} custom-call(f32[7,128,128]{2,1,0:T(8,128)S(1)} %first_hop_weights.1.k_ref.refs_0_, f32[7,128,128]{2,1,0:T(8,128)S(1)} %second_hop_weights.1.refs_1_, f32[8,2,128,128]{3,2,1,0:T(8,128)S(1)} %local_0.1.refs_2_, f32[4,128,128]{2,1,0:T(8,128)S(1)} %collective-permute-done.1.refs_3_, ...), custom_call_target="tpu_custom_call" | custom-call | flops 1 | bytes 1 | tf_op jit(solution)/shard_map/finish_0/pallas_call | solution.py:210
  44.1 0.0 collective-permute-done.10.refs_3_
  44.1 0.8 %collective-permute-done.11.refs_4_ = f32[4,128,128]{2,1,0:T(8,128)S(1)} collective-permute-done((f32[4,128,128]{2,1,0:T(8,128)S(1)}, f32[4,128,128]{2,1,0:T(8,128)S(1)}, u32[]{:S(2)}, u32[]{:S(2)}) %collective-permute-start.11) | collective-permute-done | bytes 262176 | tf_op jit(solution)/shard_map/ppermute | solution.py:322
  44.9 0.9 %finish_1.1 = f32[12,2,128,128]{3,2,1,0:T(8,128)} custom-call(f32[7,128,128]{2,1,0:T(8,128)S(1)} %first_hop_weights.1.k_ref.refs_0_, f32[7,128,128]{2,1,0:T(8,128)S(1)} %second_hop_weights.1.refs_1_, f32[4,2,128,128]{3,2,1,0:T(8,128)S(1)} %add_first.1.refs_2_, f32[4,128,128]{2,1,0:T(8,128)S(1)} %collective-permute-done.10.refs_3_, ...), custom_call_target="tpu_custom_call", output_to_operand_aliasing={{}: (5, {})} | custom-call | flops 1 | bytes 1 | tf_op jit(solution)/shard_map/finish_1/pallas_call | solution.py:210
  (5 shorter events, 0.1 us)
Async XLA Ops:
  0.0 1.4 %copy-start = (f32[12,2,128,128]{3,2,1,0:T(8,128)S(1)}, f32[12,2,128,128]{3,2,1,0:T(8,128)}, u32[]{:S(2)}) copy-start(f32[12,2,128,128]{3,2,1,0:T(8,128)} %orb_ref.7) | copy-start | bytes 4718596
  1.4 3.3 %slice-start = ((f32[12,2,128,128]{3,2,1,0:T(8,128)}), f32[4,2,128,128]{3,2,1,0:T(8,128)S(1)}, s32[]{:S(2)}) async-start(f32[12,2,128,128]{3,2,1,0:T(8,128)} %orb_ref.7), calls=%async_computation | async-start | bytes 1048576 | tf_op jit(solution)/shard_map/slice | solution.py:276
  1.4 4.1 %copy-start.1 = (f32[12,2,128,128]{3,2,1,0:T(8,128)S(1)}, f32[12,2,128,128]{3,2,1,0:T(8,128)}, u32[]{:S(2)}) copy-start(f32[12,2,128,128]{3,2,1,0:T(8,128)} %orb_ref.7) | copy-start | bytes 4718596
  1.6 9.0 %copy-start.2 = (f32[24]{0:T(128)S(1)}, f32[24]{0:T(128)}, u32[]{:S(2)}) copy-start(f32[24]{0:T(128)} %occ_ref.5) | copy-start | bytes 292
  1.7 12.9 %collective-permute-start.2 = (f32[6,128,128]{2,1,0:T(8,128)S(1)}, f32[6,128,128]{2,1,0:T(8,128)S(1)}, u32[]{:S(2)}, u32[]{:S(2)}) collective-permute-start(f32[6,128,128]{2,1,0:T(8,128)S(1)} %get-tuple-element.15), channel_id=1, source_target_pairs={{0,1},{1,0},{2,3},{3,2},{4,5},{5,4},{6,7},{7,6},{8,9},{9,8},{10,11... | collective-permute-start | bytes 1179656 | tf_op jit(solution)/shard_map/ppermute | solution.py:275
  4.7 5.9 %collective-permute-start = (f32[2,2,128,128]{3,2,1,0:T(8,128)S(1)}, f32[2,2,128,128]{3,2,1,0:T(8,128)S(1)}, u32[]{:S(2)}, u32[]{:S(2)}) collective-permute-start(f32[2,2,128,128]{3,2,1,0:T(8,128)S(1)} %constant_dynamic-slice_fusion.2.refs_0_), channel_id=1, source_target_pairs={{0,16},{16,0},{1,17},{17,1},{2,18},{18,2},{3,19},{19,3},{4,20},{20... | collective-permute-start | bytes 786440 | tf_op jit(solution)/shard_map/ppermute | solution.py:237
  4.8 15.5 %collective-permute-start.1 = (f32[4,128,128]{2,1,0:T(8,128)S(1)}, f32[4,128,128]{2,1,0:T(8,128)S(1)}, u32[]{:S(2)}, u32[]{:S(2)}) collective-permute-start(f32[4,128,128]{2,1,0:T(8,128)S(1)} %get-tuple-element.14), channel_id=1, source_target_pairs={{0,1},{1,0},{2,3},{3,2},{4,5},{5,4},{6,7},{7,6},{8,9},{9,8},{10,11... | collective-permute-start | bytes 786440 | tf_op jit(solution)/shard_map/ppermute | solution.py:275
  5.8 14.6 %collective-permute-start.4 = (f32[4,128,128]{2,1,0:T(8,128)S(1)}, f32[4,128,128]{2,1,0:T(8,128)S(1)}, u32[]{:S(2)}, u32[]{:S(2)}) collective-permute-start(f32[4,128,128]{2,1,0:T(8,128)S(1)} %get-tuple-element.16), channel_id=1, source_target_pairs={{2,0},{4,2},{1,3},{6,4},{3,5},{8,6},{5,7},{10,8},{7,9},{12,10},{9,... | collective-permute-start | bytes 786440 | tf_op jit(solution)/shard_map/ppermute | solution.py:274
  7.1 20.8 %collective-permute-start.12 = (f32[6,128,128]{2,1,0:T(8,128)S(1)}, f32[6,128,128]{2,1,0:T(8,128)S(1)}, u32[]{:S(2)}, u32[]{:S(2)}) collective-permute-start(f32[6,128,128]{2,1,0:T(8,128)S(1)} %get-tuple-element.21), channel_id=1, source_target_pairs={{0,1},{1,0},{2,3},{3,2},{4,5},{5,4},{6,7},{7,6},{8,9},{9,8},{10,11... | collective-permute-start | bytes 1179656 | tf_op jit(solution)/shard_map/ppermute | solution.py:275
  14.6 17.9 %collective-permute-start.6 = (f32[6,128,128]{2,1,0:T(8,128)S(1)}, f32[6,128,128]{2,1,0:T(8,128)S(1)}, u32[]{:S(2)}, u32[]{:S(2)}) collective-permute-start(f32[6,128,128]{2,1,0:T(8,128)S(1)} %collective-permute-done.2.refs_4_), channel_id=1, source_target_pairs={{0,2},{1,15},{2,4},{3,1},{4,6},{5,3},{6,8},{7,5},{8,10},{9,7},{10,... | collective-permute-start | bytes 1179656 | tf_op jit(solution)/shard_map/ppermute | solution.py:319
  20.3 6.8 %collective-permute-start.3 = (f32[2,2,128,128]{3,2,1,0:T(8,128)S(1)}, f32[2,2,128,128]{3,2,1,0:T(8,128)S(1)}, u32[]{:S(2)}, u32[]{:S(2)}) collective-permute-start(f32[2,2,128,128]{3,2,1,0:T(8,128)S(1)} %constant_dynamic-slice_fusion.1.refs_2_), channel_id=1, source_target_pairs={{0,16},{16,0},{1,17},{17,1},{2,18},{18,2},{3,19},{19,3},{4,20},{20... | collective-permute-start | bytes 786440 | tf_op jit(solution)/shard_map/ppermute | solution.py:237
  20.4 12.1 %collective-permute-start.5 = (f32[4,128,128]{2,1,0:T(8,128)S(1)}, f32[4,128,128]{2,1,0:T(8,128)S(1)}, u32[]{:S(2)}, u32[]{:S(2)}) collective-permute-start(f32[4,128,128]{2,1,0:T(8,128)S(1)} %collective-permute-done.1.refs_3_), channel_id=1, source_target_pairs={{0,2},{1,15},{2,4},{3,1},{4,6},{5,3},{6,8},{7,5},{8,10},{9,7},{10,... | collective-permute-start | bytes 786440 | tf_op jit(solution)/shard_map/ppermute | solution.py:319
  22.5 11.6 %collective-permute-start.8 = (f32[4,128,128]{2,1,0:T(8,128)S(1)}, f32[4,128,128]{2,1,0:T(8,128)S(1)}, u32[]{:S(2)}, u32[]{:S(2)}) collective-permute-start(f32[4,128,128]{2,1,0:T(8,128)S(1)} %get-tuple-element.19), channel_id=1, source_target_pairs={{0,1},{1,0},{2,3},{3,2},{4,5},{5,4},{6,7},{7,6},{8,9},{9,8},{10,11... | collective-permute-start | bytes 786440 | tf_op jit(solution)/shard_map/ppermute | solution.py:275
  27.1 14.4 %collective-permute-start.9 = (f32[4,128,128]{2,1,0:T(8,128)S(1)}, f32[4,128,128]{2,1,0:T(8,128)S(1)}, u32[]{:S(2)}, u32[]{:S(2)}) collective-permute-start(f32[4,128,128]{2,1,0:T(8,128)S(1)} %get-tuple-element.16), channel_id=1, source_target_pairs={{0,1},{1,0},{2,3},{3,2},{4,5},{5,4},{6,7},{7,6},{8,9},{9,8},{10,11... | collective-permute-start | bytes 786440 | tf_op jit(solution)/shard_map/ppermute | solution.py:275
  27.9 14.6 %collective-permute-start.13 = (f32[6,128,128]{2,1,0:T(8,128)S(1)}, f32[6,128,128]{2,1,0:T(8,128)S(1)}, u32[]{:S(2)}, u32[]{:S(2)}) collective-permute-start(f32[6,128,128]{2,1,0:T(8,128)S(1)} %collective-permute-done.12.refs_5_), channel_id=1, source_target_pairs={{0,2},{1,15},{2,4},{3,1},{4,6},{5,3},{6,8},{7,5},{8,10},{9,7},{10,... | collective-permute-start | bytes 1179656 | tf_op jit(solution)/shard_map/ppermute | solution.py:319
  32.5 9.2 %collective-permute-start.7 = (f32[2,2,128,128]{3,2,1,0:T(8,128)S(1)}, f32[2,2,128,128]{3,2,1,0:T(8,128)S(1)}, u32[]{:S(2)}, u32[]{:S(2)}) collective-permute-start(f32[2,2,128,128]{3,2,1,0:T(8,128)S(1)} %constant_dynamic-slice_fusion.refs_2_), channel_id=1, source_target_pairs={{0,16},{16,0},{1,17},{17,1},{2,18},{18,2},{3,19},{19,3},{4,20},{20... | collective-permute-start | bytes 786440 | tf_op jit(solution)/shard_map/ppermute | solution.py:237
  34.1 10.0 %collective-permute-start.10 = (f32[4,128,128]{2,1,0:T(8,128)S(1)}, f32[4,128,128]{2,1,0:T(8,128)S(1)}, u32[]{:S(2)}, u32[]{:S(2)}) collective-permute-start(f32[4,128,128]{2,1,0:T(8,128)S(1)} %collective-permute-done.8.refs_0_), channel_id=1, source_target_pairs={{0,2},{2,4},{3,1},{4,6},{5,3},{6,8},{7,5},{8,10},{9,7},{10,12},{11... | collective-permute-start | bytes 786440 | tf_op jit(solution)/shard_map/ppermute | solution.py:319
  38.3 6.6 %collective-permute-start.11 = (f32[4,128,128]{2,1,0:T(8,128)S(1)}, f32[4,128,128]{2,1,0:T(8,128)S(1)}, u32[]{:S(2)}, u32[]{:S(2)}) collective-permute-start(f32[4,128,128]{2,1,0:T(8,128)S(1)} %collective-permute-done.4), channel_id=1, source_target_pairs={{0,1},{1,0},{2,3},{3,2},{4,5},{5,4},{6,7},{7,6},{8,9},{9,8},{10,11... | collective-permute-start | bytes 786440 | tf_op jit(solution)/shard_map/ppermute | solution.py:322

commit v6 on v5

--- a/solution.py
+++ b/solution.py
@@ -103,7 +103,7 @@
 
 
 def local_kernel(first, k_ref, orb_ref, acc_ref):
-    @pl.loop(0, acc_ref.shape[0])
+    @pl.loop(0, acc_ref.shape[0], unroll=2)
     def _(j):
         for p in range(PLANES):
             groups = {}

time: 46 us -> 46 us (level)
  transfers between devices with their start and end apart: 14 -> 14, of which waited for: 5 -> 6; matrix products, arithmetic and copies ran while one was open for 0% -> 0% of each run, Pallas kernels for 18% -> 18%
where the time goes in v6:
time: 46 us; the launch traced here: 45.9 us
  starting transfers between devices  24.6 us (53%)
  waiting for transfers between devices  10.1 us (22%)
  Pallas kernels  9.4 us (20%)
  local copies, waits for them, and re-layouts  1.49 us (3%)
    ppermute x5, starting transfers between devices, per_device(): first = [lax.ppermute(part, 'dom', swap) for part in sent]  11.9 us
    ppermute x4, starting transfers between devices, per_device(): lax.ppermute(after(part, before[i]) if i in before else part, 'dom', ring...  11.2 us
    ppermute x5, waiting for transfers between devices, per_device(): first = [lax.ppermute(part, 'dom', swap) for part in sent]  7.29 us
    pallas_call x2, Pallas kernels, local_sums(): pl.pallas_call(functools.partial(local_kernel, cuts[g]), out_shape=f32(cu...  2.89 us
    pallas_call x2, Pallas kernels, finish(): pl.pallas_call(functools.partial(finish_kernel, origin, hops_left, chaine...  2.47 us
    ppermute x4, waiting for transfers between devices, per_device(): lax.ppermute(after(part, before[i]) if i in before else part, 'dom', ring...  1.96 us
    pallas_call x1, Pallas kernels, per_device(): pl.pallas_call(functools.partial(local_weight_kernel, orb_count), out_sha...  1.72 us
    pallas_call x2, Pallas kernels, halo_weights(): pl.pallas_call(functools.partial(halo_weight_kernel, name == 'second', or...  1.58 us
  transfers between devices with their start and end apart: 14, of which 6 were waited for; matrix products, arithmetic and copies ran while one was open for 0% of the time, Pallas kernels for 18%

profile of v6, /device:TPU:0, one launch (start us, length us, event | category | flops | bytes accessed | tf_op | source)
XLA Modules:
  0.0 45.9 jit_solution(14957249442918759741)
XLA Ops:
  0.0 0.0 copy-start
  0.0 1.4 %copy-done = f32[12,2,128,128]{3,2,1,0:T(8,128)S(1)} copy-done((f32[12,2,128,128]{3,2,1,0:T(8,128)S(1)}, f32[12,2,128,128]{3,2,1,0:T(8,128)}, u32[]{:S(2)}) %copy-start) | copy-done | bytes 1572888
  1.4 0.0 slice-start
  1.4 0.0 copy-start.1
  1.4 0.2 cut_first.1
  1.6 0.0 copy-start.2
  1.7 3.0 %collective-permute-start.2 = (f32[6,128,128]{2,1,0:T(8,128)S(1)}, f32[6,128,128]{2,1,0:T(8,128)S(1)}, u32[]{:S(2)}, u32[]{:S(2)}) collective-permute-start(f32[6,128,128]{2,1,0:T(8,128)S(1)} %get-tuple-element.15), channel_id=1, source_target_pairs={{0,1},{1,0},{2,3},{3,2},{4,5},{5,4},{6,7},{7,6},{8,9},{9,8},{10,11... | collective-permute-start | bytes 1179656 | tf_op jit(solution)/shard_map/ppermute | solution.py:275
  4.7 0.0 slice-done
  4.7 0.1 collective-permute-start
  4.8 0.8 %collective-permute-start.1 = (f32[4,128,128]{2,1,0:T(8,128)S(1)}, f32[4,128,128]{2,1,0:T(8,128)S(1)}, u32[]{:S(2)}, u32[]{:S(2)}) collective-permute-start(f32[4,128,128]{2,1,0:T(8,128)S(1)} %get-tuple-element.14), channel_id=1, source_target_pairs={{0,1},{1,0},{2,3},{3,2},{4,5},{5,4},{6,7},{7,6},{8,9},{9,8},{10,11... | collective-permute-start | bytes 786440 | tf_op jit(solution)/shard_map/ppermute | solution.py:275
  5.6 0.0 copy-done.1
  5.6 0.2 cut_rest.1
  5.8 1.3 %collective-permute-start.4 = (f32[4,128,128]{2,1,0:T(8,128)S(1)}, f32[4,128,128]{2,1,0:T(8,128)S(1)}, u32[]{:S(2)}, u32[]{:S(2)}) collective-permute-start(f32[4,128,128]{2,1,0:T(8,128)S(1)} %get-tuple-element.16), channel_id=1, source_target_pairs={{2,0},{4,2},{1,3},{6,4},{3,5},{8,6},{5,7},{10,8},{7,9},{12,10},{9,... | collective-permute-start | bytes 786440 | tf_op jit(solution)/shard_map/ppermute | solution.py:274
  7.1 3.5 %collective-permute-start.12 = (f32[6,128,128]{2,1,0:T(8,128)S(1)}, f32[6,128,128]{2,1,0:T(8,128)S(1)}, u32[]{:S(2)}, u32[]{:S(2)}) collective-permute-start(f32[6,128,128]{2,1,0:T(8,128)S(1)} %get-tuple-element.21), channel_id=1, source_target_pairs={{0,1},{1,0},{2,3},{3,2},{4,5},{5,4},{6,7},{7,6},{8,9},{9,8},{10,11... | collective-permute-start | bytes 1179656 | tf_op jit(solution)/shard_map/ppermute | solution.py:275
  10.6 0.0 collective-permute-done.refs_1_
  10.6 0.0 copy-done.2
  10.6 1.7 %local_weights.1.k_ref = f32[2,18,128,128]{3,2,1,0:T(8,128)S(1)} custom-call(f32[24]{0:T(128)S(1)} %copy-done.2, f32[2,2,128,128]{3,2,1,0:T(8,128)S(1)} %constant_dynamic-slice_fusion.2.refs_0_, f32[2,2,128,128]{3,2,1,0:T(8,128)S(1)} %collective-permute-done.refs_1_), custom_call_target="tpu_custom_call" | custom-call | flops 1 | bytes 1 | tf_op jit(solution)/shard_map/local_weights/pallas_call | solution.py:277
  12.4 2.2 %collective-permute-done.2.refs_4_ = f32[6,128,128]{2,1,0:T(8,128)S(1)} collective-permute-done((f32[6,128,128]{2,1,0:T(8,128)S(1)}, f32[6,128,128]{2,1,0:T(8,128)S(1)}, u32[]{:S(2)}, u32[]{:S(2)}) %collective-permute-start.2) | collective-permute-done | bytes 393248 | tf_op jit(solution)/shard_map/ppermute | solution.py:275
  14.6 2.1 %collective-permute-start.6 = (f32[6,128,128]{2,1,0:T(8,128)S(1)}, f32[6,128,128]{2,1,0:T(8,128)S(1)}, u32[]{:S(2)}, u32[]{:S(2)}) collective-permute-start(f32[6,128,128]{2,1,0:T(8,128)S(1)} %collective-permute-done.2.refs_4_), channel_id=1, source_target_pairs={{0,2},{1,15},{2,4},{3,1},{4,6},{5,3},{6,8},{7,5},{8,10},{9,7},{10,... | collective-permute-start | bytes 1179656 | tf_op jit(solution)/shard_map/ppermute | solution.py:319
  16.7 3.5 %collective-permute-done.1.refs_3_ = f32[4,128,128]{2,1,0:T(8,128)S(1)} collective-permute-done((f32[4,128,128]{2,1,0:T(8,128)S(1)}, f32[4,128,128]{2,1,0:T(8,128)S(1)}, u32[]{:S(2)}, u32[]{:S(2)}) %collective-permute-start.1) | collective-permute-done | bytes 262176 | tf_op jit(solution)/shard_map/ppermute | solution.py:275
  20.3 0.1 collective-permute-start.3
  20.4 0.0 collective-permute-done.4
  20.4 2.1 %collective-permute-start.5 = (f32[4,128,128]{2,1,0:T(8,128)S(1)}, f32[4,128,128]{2,1,0:T(8,128)S(1)}, u32[]{:S(2)}, u32[]{:S(2)}) collective-permute-start(f32[4,128,128]{2,1,0:T(8,128)S(1)} %collective-permute-done.1.refs_3_), channel_id=1, source_target_pairs={{0,2},{1,15},{2,4},{3,1},{4,6},{5,3},{6,8},{7,5},{8,10},{9,7},{10,... | collective-permute-start | bytes 786440 | tf_op jit(solution)/shard_map/ppermute | solution.py:319
  22.5 4.5 %collective-permute-start.8 = (f32[4,128,128]{2,1,0:T(8,128)S(1)}, f32[4,128,128]{2,1,0:T(8,128)S(1)}, u32[]{:S(2)}, u32[]{:S(2)}) collective-permute-start(f32[4,128,128]{2,1,0:T(8,128)S(1)} %get-tuple-element.19), channel_id=1, source_target_pairs={{0,1},{1,0},{2,3},{3,2},{4,5},{5,4},{6,7},{7,6},{8,9},{9,8},{10,11... | collective-permute-start | bytes 786440 | tf_op jit(solution)/shard_map/ppermute | solution.py:275
  27.1 0.0 collective-permute-done.3.refs_3_
  27.1 0.0 collective-permute-start.9
  27.1 0.8 %first_hop_weights.1.k_ref.refs_0_ = f32[7,128,128]{2,1,0:T(8,128)S(1)} custom-call(f32[24]{0:T(128)S(1)} %copy-done.2, f32[2,2,128,128]{3,2,1,0:T(8,128)S(1)} %constant_dynamic-slice_fusion.2.refs_0_, f32[2,2,128,128]{3,2,1,0:T(8,128)S(1)} %collective-permute-done.refs_1_, f32[2,2,128,128]{3,2,1,0:T(8,128)S(1)} %constant_dynamic-slice_fusion.1.refs_2_, ...), custom_call_target="tpu_custom_call" | custom-call | flops 1 | bytes 1 | tf_op jit(solution)/shard_map/first_hop_weights/pallas_call | solution.py:306
  27.9 0.0 collective-permute-done.12.refs_5_
  27.9 2.8 %collective-permute-start.13 = (f32[6,128,128]{2,1,0:T(8,128)S(1)}, f32[6,128,128]{2,1,0:T(8,128)S(1)}, u32[]{:S(2)}, u32[]{:S(2)}) collective-permute-start(f32[6,128,128]{2,1,0:T(8,128)S(1)} %collective-permute-done.12.refs_5_), channel_id=1, source_target_pairs={{0,2},{1,15},{2,4},{3,1},{4,6},{5,3},{6,8},{7,5},{8,10},{9,7},{10,... | collective-permute-start | bytes 1179656 | tf_op jit(solution)/shard_map/ppermute | solution.py:319
  30.7 1.7 %collective-permute-done.5.refs_6_ = f32[4,128,128]{2,1,0:T(8,128)S(1)} collective-permute-done((f32[4,128,128]{2,1,0:T(8,128)S(1)}, f32[4,128,128]{2,1,0:T(8,128)S(1)}, u32[]{:S(2)}, u32[]{:S(2)}) %collective-permute-start.5) | collective-permute-done | bytes 262176 | tf_op jit(solution)/shard_map/ppermute | solution.py:319
  32.5 0.0 collective-permute-done.6.refs_7_
  32.5 0.1 collective-permute-start.7
  32.6 1.5 %collective-permute-done.8.refs_0_ = f32[4,128,128]{2,1,0:T(8,128)S(1)} collective-permute-done((f32[4,128,128]{2,1,0:T(8,128)S(1)}, f32[4,128,128]{2,1,0:T(8,128)S(1)}, u32[]{:S(2)}, u32[]{:S(2)}) %collective-permute-start.8) | collective-permute-done | bytes 262176 | tf_op jit(solution)/shard_map/ppermute | solution.py:275
  34.1 4.1 %collective-permute-start.10 = (f32[4,128,128]{2,1,0:T(8,128)S(1)}, f32[4,128,128]{2,1,0:T(8,128)S(1)}, u32[]{:S(2)}, u32[]{:S(2)}) collective-permute-start(f32[4,128,128]{2,1,0:T(8,128)S(1)} %collective-permute-done.8.refs_0_), channel_id=1, source_target_pairs={{0,2},{2,4},{3,1},{4,6},{5,3},{6,8},{7,5},{8,10},{9,7},{10,12},{11... | collective-permute-start | bytes 786440 | tf_op jit(solution)/shard_map/ppermute | solution.py:319
  38.3 0.1 collective-permute-start.11
  38.3 1.0 %local_1.1.acc_ref = f32[4,2,128,128]{3,2,1,0:T(8,128)S(1)} custom-call(f32[2,18,128,128]{3,2,1,0:T(8,128)S(1)} %local_weights.1.k_ref, f32[12,2,128,128]{3,2,1,0:T(8,128)S(1)} %copy-done.1), custom_call_target="tpu_custom_call" | custom-call | flops 1 | bytes 1 | tf_op jit(solution)/shard_map/local_1/pallas_call | solution.py:287
  39.3 1.9 %local_0.1.refs_2_ = f32[8,2,128,128]{3,2,1,0:T(8,128)S(1)} custom-call(f32[2,18,128,128]{3,2,1,0:T(8,128)S(1)} %local_weights.1.k_ref, f32[12,2,128,128]{3,2,1,0:T(8,128)S(1)} %copy-done.1), custom_call_target="tpu_custom_call" | custom-call | flops 1 | bytes 1 | tf_op jit(solution)/shard_map/local_0/pallas_call | solution.py:287
  41.3 0.0 collective-permute-done.9.refs_1_
  41.3 0.3 add_first.1.refs_2_
  41.5 0.0 collective-permute-done.7.refs_3_
  41.5 0.8 %second_hop_weights.1.refs_1_ = f32[7,128,128]{2,1,0:T(8,128)S(1)} custom-call(f32[24]{0:T(128)S(1)} %copy-done.2, f32[2,2,128,128]{3,2,1,0:T(8,128)S(1)} %constant_dynamic-slice_fusion.2.refs_0_, f32[2,2,128,128]{3,2,1,0:T(8,128)S(1)} %collective-permute-done.refs_1_, f32[2,2,128,128]{3,2,1,0:T(8,128)S(1)} %constant_dynamic-slice_fusion.refs_2_, ...), custom_call_target="tpu_custom_call" | custom-call | flops 1 | bytes 1 | tf_op jit(solution)/shard_map/second_hop_weights/pallas_call | solution.py:306
  42.3 0.0 collective-permute-done.13.refs_8_
  42.4 1.5 %finish_0.1.refs_5_ = f32[12,2,128,128]{3,2,1,0:T(8,128)} custom-call(f32[7,128,128]{2,1,0:T(8,128)S(1)} %first_hop_weights.1.k_ref.refs_0_, f32[7,128,128]{2,1,0:T(8,128)S(1)} %second_hop_weights.1.refs_1_, f32[8,2,128,128]{3,2,1,0:T(8,128)S(1)} %local_0.1.refs_2_, f32[4,128,128]{2,1,0:T(8,128)S(1)} %collective-permute-done.1.refs_3_, ...), custom_call_target="tpu_custom_call" | custom-call | flops 1 | bytes 1 | tf_op jit(solution)/shard_map/finish_0/pallas_call | solution.py:210
  43.9 0.2 collective-permute-done.10.refs_3_
  44.1 0.8 %collective-permute-done.11.refs_4_ = f32[4,128,128]{2,1,0:T(8,128)S(1)} collective-permute-done((f32[4,128,128]{2,1,0:T(8,128)S(1)}, f32[4,128,128]{2,1,0:T(8,128)S(1)}, u32[]{:S(2)}, u32[]{:S(2)}) %collective-permute-start.11) | collective-permute-done | bytes 262176 | tf_op jit(solution)/shard_map/ppermute | solution.py:322
  44.9 0.9 %finish_1.1 = f32[12,2,128,128]{3,2,1,0:T(8,128)} custom-call(f32[7,128,128]{2,1,0:T(8,128)S(1)} %first_hop_weights.1.k_ref.refs_0_, f32[7,128,128]{2,1,0:T(8,128)S(1)} %second_hop_weights.1.refs_1_, f32[4,2,128,128]{3,2,1,0:T(8,128)S(1)} %add_first.1.refs_2_, f32[4,128,128]{2,1,0:T(8,128)S(1)} %collective-permute-done.10.refs_3_, ...), custom_call_target="tpu_custom_call", output_to_operand_aliasing={{}: (5, {})} | custom-call | flops 1 | bytes 1 | tf_op jit(solution)/shard_map/finish_1/pallas_call | solution.py:210
  (5 shorter events, 0.1 us)
Async XLA Ops:
  0.0 1.4 %copy-start = (f32[12,2,128,128]{3,2,1,0:T(8,128)S(1)}, f32[12,2,128,128]{3,2,1,0:T(8,128)}, u32[]{:S(2)}) copy-start(f32[12,2,128,128]{3,2,1,0:T(8,128)} %orb_ref.7) | copy-start | bytes 4718596
  1.4 3.3 %slice-start = ((f32[12,2,128,128]{3,2,1,0:T(8,128)}), f32[4,2,128,128]{3,2,1,0:T(8,128)S(1)}, s32[]{:S(2)}) async-start(f32[12,2,128,128]{3,2,1,0:T(8,128)} %orb_ref.7), calls=%async_computation | async-start | bytes 1048576 | tf_op jit(solution)/shard_map/slice | solution.py:276
  1.4 4.1 %copy-start.1 = (f32[12,2,128,128]{3,2,1,0:T(8,128)S(1)}, f32[12,2,128,128]{3,2,1,0:T(8,128)}, u32[]{:S(2)}) copy-start(f32[12,2,128,128]{3,2,1,0:T(8,128)} %orb_ref.7) | copy-start | bytes 4718596
  1.6 9.0 %copy-start.2 = (f32[24]{0:T(128)S(1)}, f32[24]{0:T(128)}, u32[]{:S(2)}) copy-start(f32[24]{0:T(128)} %occ_ref.5) | copy-start | bytes 292
  1.7 12.9 %collective-permute-start.2 = (f32[6,128,128]{2,1,0:T(8,128)S(1)}, f32[6,128,128]{2,1,0:T(8,128)S(1)}, u32[]{:S(2)}, u32[]{:S(2)}) collective-permute-start(f32[6,128,128]{2,1,0:T(8,128)S(1)} %get-tuple-element.15), channel_id=1, source_target_pairs={{0,1},{1,0},{2,3},{3,2},{4,5},{5,4},{6,7},{7,6},{8,9},{9,8},{10,11... | collective-permute-start | bytes 1179656 | tf_op jit(solution)/shard_map/ppermute | solution.py:275
  4.7 5.9 %collective-permute-start = (f32[2,2,128,128]{3,2,1,0:T(8,128)S(1)}, f32[2,2,128,128]{3,2,1,0:T(8,128)S(1)}, u32[]{:S(2)}, u32[]{:S(2)}) collective-permute-start(f32[2,2,128,128]{3,2,1,0:T(8,128)S(1)} %constant_dynamic-slice_fusion.2.refs_0_), channel_id=1, source_target_pairs={{0,16},{16,0},{1,17},{17,1},{2,18},{18,2},{3,19},{19,3},{4,20},{20... | collective-permute-start | bytes 786440 | tf_op jit(solution)/shard_map/ppermute | solution.py:237
  4.8 15.5 %collective-permute-start.1 = (f32[4,128,128]{2,1,0:T(8,128)S(1)}, f32[4,128,128]{2,1,0:T(8,128)S(1)}, u32[]{:S(2)}, u32[]{:S(2)}) collective-permute-start(f32[4,128,128]{2,1,0:T(8,128)S(1)} %get-tuple-element.14), channel_id=1, source_target_pairs={{0,1},{1,0},{2,3},{3,2},{4,5},{5,4},{6,7},{7,6},{8,9},{9,8},{10,11... | collective-permute-start | bytes 786440 | tf_op jit(solution)/shard_map/ppermute | solution.py:275
  5.8 14.6 %collective-permute-start.4 = (f32[4,128,128]{2,1,0:T(8,128)S(1)}, f32[4,128,128]{2,1,0:T(8,128)S(1)}, u32[]{:S(2)}, u32[]{:S(2)}) collective-permute-start(f32[4,128,128]{2,1,0:T(8,128)S(1)} %get-tuple-element.16), channel_id=1, source_target_pairs={{2,0},{4,2},{1,3},{6,4},{3,5},{8,6},{5,7},{10,8},{7,9},{12,10},{9,... | collective-permute-start | bytes 786440 | tf_op jit(solution)/shard_map/ppermute | solution.py:274
  7.1 20.8 %collective-permute-start.12 = (f32[6,128,128]{2,1,0:T(8,128)S(1)}, f32[6,128,128]{2,1,0:T(8,128)S(1)}, u32[]{:S(2)}, u32[]{:S(2)}) collective-permute-start(f32[6,128,128]{2,1,0:T(8,128)S(1)} %get-tuple-element.21), channel_id=1, source_target_pairs={{0,1},{1,0},{2,3},{3,2},{4,5},{5,4},{6,7},{7,6},{8,9},{9,8},{10,11... | collective-permute-start | bytes 1179656 | tf_op jit(solution)/shard_map/ppermute | solution.py:275
  14.6 17.9 %collective-permute-start.6 = (f32[6,128,128]{2,1,0:T(8,128)S(1)}, f32[6,128,128]{2,1,0:T(8,128)S(1)}, u32[]{:S(2)}, u32[]{:S(2)}) collective-permute-start(f32[6,128,128]{2,1,0:T(8,128)S(1)} %collective-permute-done.2.refs_4_), channel_id=1, source_target_pairs={{0,2},{1,15},{2,4},{3,1},{4,6},{5,3},{6,8},{7,5},{8,10},{9,7},{10,... | collective-permute-start | bytes 1179656 | tf_op jit(solution)/shard_map/ppermute | solution.py:319
  20.3 6.8 %collective-permute-start.3 = (f32[2,2,128,128]{3,2,1,0:T(8,128)S(1)}, f32[2,2,128,128]{3,2,1,0:T(8,128)S(1)}, u32[]{:S(2)}, u32[]{:S(2)}) collective-permute-start(f32[2,2,128,128]{3,2,1,0:T(8,128)S(1)} %constant_dynamic-slice_fusion.1.refs_2_), channel_id=1, source_target_pairs={{0,16},{16,0},{1,17},{17,1},{2,18},{18,2},{3,19},{19,3},{4,20},{20... | collective-permute-start | bytes 786440 | tf_op jit(solution)/shard_map/ppermute | solution.py:237
  20.4 12.1 %collective-permute-start.5 = (f32[4,128,128]{2,1,0:T(8,128)S(1)}, f32[4,128,128]{2,1,0:T(8,128)S(1)}, u32[]{:S(2)}, u32[]{:S(2)}) collective-permute-start(f32[4,128,128]{2,1,0:T(8,128)S(1)} %collective-permute-done.1.refs_3_), channel_id=1, source_target_pairs={{0,2},{1,15},{2,4},{3,1},{4,6},{5,3},{6,8},{7,5},{8,10},{9,7},{10,... | collective-permute-start | bytes 786440 | tf_op jit(solution)/shard_map/ppermute | solution.py:319
  22.5 11.6 %collective-permute-start.8 = (f32[4,128,128]{2,1,0:T(8,128)S(1)}, f32[4,128,128]{2,1,0:T(8,128)S(1)}, u32[]{:S(2)}, u32[]{:S(2)}) collective-permute-start(f32[4,128,128]{2,1,0:T(8,128)S(1)} %get-tuple-element.19), channel_id=1, source_target_pairs={{0,1},{1,0},{2,3},{3,2},{4,5},{5,4},{6,7},{7,6},{8,9},{9,8},{10,11... | collective-permute-start | bytes 786440 | tf_op jit(solution)/shard_map/ppermute | solution.py:275
  27.1 14.2 %collective-permute-start.9 = (f32[4,128,128]{2,1,0:T(8,128)S(1)}, f32[4,128,128]{2,1,0:T(8,128)S(1)}, u32[]{:S(2)}, u32[]{:S(2)}) collective-permute-start(f32[4,128,128]{2,1,0:T(8,128)S(1)} %get-tuple-element.16), channel_id=1, source_target_pairs={{0,1},{1,0},{2,3},{3,2},{4,5},{5,4},{6,7},{7,6},{8,9},{9,8},{10,11... | collective-permute-start | bytes 786440 | tf_op jit(solution)/shard_map/ppermute | solution.py:275
  27.9 14.5 %collective-permute-start.13 = (f32[6,128,128]{2,1,0:T(8,128)S(1)}, f32[6,128,128]{2,1,0:T(8,128)S(1)}, u32[]{:S(2)}, u32[]{:S(2)}) collective-permute-start(f32[6,128,128]{2,1,0:T(8,128)S(1)} %collective-permute-done.12.refs_5_), channel_id=1, source_target_pairs={{0,2},{1,15},{2,4},{3,1},{4,6},{5,3},{6,8},{7,5},{8,10},{9,7},{10,... | collective-permute-start | bytes 1179656 | tf_op jit(solution)/shard_map/ppermute | solution.py:319
  32.5 9.0 %collective-permute-start.7 = (f32[2,2,128,128]{3,2,1,0:T(8,128)S(1)}, f32[2,2,128,128]{3,2,1,0:T(8,128)S(1)}, u32[]{:S(2)}, u32[]{:S(2)}) collective-permute-start(f32[2,2,128,128]{3,2,1,0:T(8,128)S(1)} %constant_dynamic-slice_fusion.refs_2_), channel_id=1, source_target_pairs={{0,16},{16,0},{1,17},{17,1},{2,18},{18,2},{3,19},{19,3},{4,20},{20... | collective-permute-start | bytes 786440 | tf_op jit(solution)/shard_map/ppermute | solution.py:237
  34.1 10.0 %collective-permute-start.10 = (f32[4,128,128]{2,1,0:T(8,128)S(1)}, f32[4,128,128]{2,1,0:T(8,128)S(1)}, u32[]{:S(2)}, u32[]{:S(2)}) collective-permute-start(f32[4,128,128]{2,1,0:T(8,128)S(1)} %collective-permute-done.8.refs_0_), channel_id=1, source_target_pairs={{0,2},{2,4},{3,1},{4,6},{5,3},{6,8},{7,5},{8,10},{9,7},{10,12},{11... | collective-permute-start | bytes 786440 | tf_op jit(solution)/shard_map/ppermute | solution.py:319
  38.3 6.6 %collective-permute-start.11 = (f32[4,128,128]{2,1,0:T(8,128)S(1)}, f32[4,128,128]{2,1,0:T(8,128)S(1)}, u32[]{:S(2)}, u32[]{:S(2)}) collective-permute-start(f32[4,128,128]{2,1,0:T(8,128)S(1)} %collective-permute-done.4), channel_id=1, source_target_pairs={{0,1},{1,0},{2,3},{3,2},{4,5},{5,4},{6,7},{7,6},{8,9},{9,8},{10,11... | collective-permute-start | bytes 786440 | tf_op jit(solution)/shard_map/ppermute | solution.py:322
